TPU v7x, 128 devices: a whole 4x4x4 slice. The times are simulated.
128 devices in a mesh: sp: 4 (over z_lo, core), fsdp: 32 (over z_hi, x, y).
Axes of the slice: x: 4, y: 4, z: 4 (z_hi: 2, z_lo: 2; z = z_hi * 2 + z_lo), core: 2. Of those that a mesh axis runs over, the one named last changes fastest.
Arguments:
- hidden_in: bfloat16 [16384, 768], P(('fsdp', 'sp')), may hold values from -6 to 6
- qkv_weight: bfloat16 [768, 2304], P('fsdp'), may hold values from -0.3125 to 0.3125
- query_bias: bfloat16 [768], P('fsdp'), may hold values from -3 to 3
- value_bias: bfloat16 [768], P('fsdp'), may hold values from -3 to 3
- output_weight: bfloat16 [768, 768], P('fsdp'), may hold values from -1.75 to 1.75
- output_bias: bfloat16 [768], P('fsdp'), may hold values from -3 to 3
- first_gain: bfloat16 [768], P('fsdp'), may hold values from 0.25 to 1.75
- first_shift: bfloat16 [768], P('fsdp'), may hold values from -3 to 3
- up_weight: bfloat16 [768, 3072], P('fsdp'), may hold values from -0.21875 to 0.21875
- up_bias: bfloat16 [3072], P('fsdp'), may hold values from -3 to 3
- down_weight: bfloat16 [3072, 768], P('fsdp'), may hold values from -0.109375 to 0.109375
- down_bias: bfloat16 [768], P('fsdp'), may hold values from -3 to 3
- second_gain: bfloat16 [768], P('fsdp'), may hold values from 0.25 to 1.75
- second_shift: bfloat16 [768], P('fsdp'), may hold values from -3 to 3
- valid_length: int32 [1], replicated, may hold values from 16128 to 16384
- out_cotangent: bfloat16 [16384, 768], P(('fsdp', 'sp')), may hold values from -6 to 6
Outputs:
- output: bfloat16 [16384, 768], P(('fsdp', 'sp'))
- input_grad: float32 [16384, 768], P(('fsdp', 'sp'))
- qkv_weight_grad: float32 [768, 2304], P('fsdp')
- query_bias_grad: float32 [768], P('fsdp')
- value_bias_grad: float32 [768], P('fsdp')
- output_weight_grad: float32 [768, 768], P('fsdp')
- output_bias_grad: float32 [768], P('fsdp')
- first_gain_grad: float32 [768], P('fsdp')
- first_shift_grad: float32 [768], P('fsdp')
- up_weight_grad: float32 [768, 3072], P('fsdp')
- up_bias_grad: float32 [3072], P('fsdp')
- down_weight_grad: float32 [3072, 768], P('fsdp')
- down_bias_grad: float32 [768], P('fsdp')
- second_gain_grad: float32 [768], P('fsdp')
- second_shift_grad: float32 [768], P('fsdp')
All inputs are finite; a program needn't handle non-finite values.
Results may differ from a plain program's by a relative error of at most 0.028.
Values may be sent and summed in bfloat16 or wider, within the bound.
A program may use at most 128 MiB of HBM per device.

v0:
```python
import math

import jax
import jax.numpy as jnp
from jax import lax
from jax.sharding import PartitionSpec as P

HEADS = 12
HEAD_DIM = 64


epsilon = 1e-05
masked = -1e30


def outer_sum(left_side, right_side):
    return lax.dot_general(
        left_side, right_side, (((0,), (0,)), ((), ())), preferred_element_type=jnp.float32
    )


def times_transposed(left_side, right_side):
    return lax.dot_general(
        left_side, right_side, (((1,), (1,)), ((), ())), preferred_element_type=jnp.float32
    )


def norm_forward(incoming, norm_gain, norm_shift):
    row_mean = jnp.mean(incoming, axis=-1, keepdims=True)
    centered = incoming - row_mean
    inverse = lax.rsqrt(jnp.mean(centered * centered, axis=-1, keepdims=True) + epsilon)
    normed = centered * inverse
    return (normed * norm_gain + norm_shift, normed, inverse)


def norm_backward(incoming, normed, inverse, norm_gain):
    scaled = incoming * norm_gain
    adjusted = (
        scaled
        - jnp.mean(scaled, axis=-1, keepdims=True)
        - normed * jnp.mean(scaled * normed, axis=-1, keepdims=True)
    )
    return (adjusted * inverse, jnp.sum(incoming * normed, axis=0), jnp.sum(incoming, axis=0))


def block_scores(query_rows, key_block, offset, mask_info):
    valid_length, query_seq, seq_len = mask_info
    scores = (
        jnp.einsum("rhd,khd->hrk", query_rows, key_block, preferred_element_type=jnp.float32)
        * 0.125
    )
    places = offset + lax.iota(jnp.int32, key_block.shape[0])
    key_seq = places // seq_len
    matches = key_seq[:, None] == lax.iota(jnp.int32, valid_length.shape[0])[None, :]
    limits = jnp.sum(jnp.where(matches, valid_length[None, :], 0), axis=1)
    allowed = (key_seq == query_seq) & (places - key_seq * seq_len < limits)
    return jnp.where(allowed[None, None, :], scores, masked)


def split_blocks(key_part, value_part, first_row):
    key_count = key_part.shape[0]
    block_size = math.gcd(key_count, 1024)
    block_count = key_count // block_size
    key_blocks = key_part.reshape((block_count, block_size) + key_part.shape[1:])
    value_blocks = value_part.reshape((block_count, block_size) + value_part.shape[1:])
    offsets = first_row + block_size * lax.iota(jnp.int32, block_count)
    return (key_blocks, value_blocks, offsets)


def fold_keys(softmax_state, key_part, value_part, first_row, query_rows, mask_info):
    blocked = split_blocks(key_part, value_part, first_row)

    def fold_advance(carried, block_item):
        running_max, running_sum, weighted = carried
        key_block, value_block, offset = block_item
        scores = block_scores(query_rows, key_block, offset, mask_info)
        new_max = jnp.maximum(running_max, jnp.max(scores, axis=-1))
        decay = jnp.exp(running_max - new_max)
        prob_block = jnp.exp(scores - new_max[..., None])
        running_sum = running_sum * decay + jnp.sum(prob_block, axis=-1)
        weighted = weighted * decay[..., None] + jnp.einsum(
            "hrk,khd->hrd",
            prob_block.astype(jnp.bfloat16),
            value_block,
            preferred_element_type=jnp.float32,
        )
        return ((new_max, running_sum, weighted), None)

    softmax_state, unused = lax.scan(fold_advance, softmax_state, blocked)
    return softmax_state


def attention_grads(query_rows, key_all, value_all, grad_out, log_sum, deltas, mask_info):
    blocked = split_blocks(key_all, value_all, 0)

    def attention_advance(grad_query, block_item):
        key_block, value_block, offset = block_item
        scores = block_scores(query_rows, key_block, offset, mask_info)
        prob_block = jnp.exp(scores - log_sum[..., None])
        grad_values = jnp.einsum(
            "hrk,rhd->khd",
            prob_block.astype(jnp.bfloat16),
            grad_out,
            preferred_element_type=jnp.float32,
        )
        grad_probs = jnp.einsum(
            "rhd,khd->hrk", grad_out, value_block, preferred_element_type=jnp.float32
        )
        grad_scores = (prob_block * (grad_probs - deltas[..., None])).astype(jnp.bfloat16) * 0.125
        grad_query = grad_query + jnp.einsum(
            "hrk,khd->rhd", grad_scores, key_block, preferred_element_type=jnp.float32
        )
        grad_keys = jnp.einsum(
            "hrk,rhd->khd", grad_scores, query_rows, preferred_element_type=jnp.float32
        )
        block_size = key_block.shape[0]
        terms = jnp.concatenate(
            (grad_keys.reshape(block_size, -1), grad_values.reshape(block_size, -1)), axis=1
        )
        return (grad_query, terms)

    grad_query, terms = lax.scan(
        attention_advance, jnp.zeros(query_rows.shape, jnp.float32), blocked
    )
    return (grad_query, terms.reshape(key_all.shape[0], -1))


def on_device(
    hidden_in,
    qkv_weight,
    query_bias,
    value_bias,
    output_weight,
    output_bias,
    first_gain,
    first_shift,
    up_weight,
    up_bias,
    down_weight,
    down_bias,
    second_gain,
    second_shift,
    valid_length,
    out_cotangent,
):
    groups = lax.axis_size("sp")
    tokens = hidden_in.shape[0]
    model_width = hidden_in.shape[1]
    local_heads = HEADS // groups
    head_span = local_heads * HEAD_DIM
    row_count = groups * tokens
    seq_len = row_count * lax.axis_size("fsdp") // valid_length.shape[0]
    query_seq = lax.axis_index("fsdp") * row_count // seq_len
    mask_info = (valid_length, query_seq, seq_len)
    (
        whole_qkv,
        whole_qbias,
        whole_vbias,
        whole_out,
        whole_obias,
        whole_gone,
        whole_sone,
        whole_up,
        whole_ubias,
        whole_down,
        whole_dbias,
        whole_gtwo,
        whole_stwo,
    ) = (
        lax.all_gather(qkv_weight, "fsdp", axis=0, tiled=True),
        lax.all_gather(query_bias, "fsdp", axis=0, tiled=True),
        lax.all_gather(value_bias, "fsdp", axis=0, tiled=True),
        lax.all_gather(output_weight, "fsdp", axis=0, tiled=True),
        lax.all_gather(output_bias, "fsdp", axis=0, tiled=True),
        lax.all_gather(first_gain, "fsdp", axis=0, tiled=True),
        lax.all_gather(first_shift, "fsdp", axis=0, tiled=True),
        lax.all_gather(up_weight, "fsdp", axis=0, tiled=True),
        lax.all_gather(up_bias, "fsdp", axis=0, tiled=True),
        lax.all_gather(down_weight, "fsdp", axis=0, tiled=True),
        lax.all_gather(down_bias, "fsdp", axis=0, tiled=True),
        lax.all_gather(second_gain, "fsdp", axis=0, tiled=True),
        lax.all_gather(second_shift, "fsdp", axis=0, tiled=True),
    )
    residual_in = hidden_in.astype(jnp.float32)
    projected = jnp.dot(hidden_in, whole_qkv, preferred_element_type=jnp.float32)
    bias_row = jnp.concatenate((whole_qbias, jnp.zeros_like(whole_qbias), whole_vbias)).astype(
        jnp.float32
    )
    packed = (projected + bias_row).astype(jnp.bfloat16).reshape(tokens, 3, groups, head_span)
    regrouped = lax.all_to_all(packed, "sp", split_axis=2, concat_axis=0, tiled=True)
    query_rows = regrouped[:, 0, 0].reshape(row_count, local_heads, HEAD_DIM)
    key_rows = regrouped[:, 1, 0].reshape(row_count, local_heads, HEAD_DIM)
    value_rows = regrouped[:, 2, 0].reshape(row_count, local_heads, HEAD_DIM)
    initial = (
        jnp.full((local_heads, row_count), masked, jnp.float32),
        jnp.zeros((local_heads, row_count), jnp.float32),
        jnp.zeros((local_heads, row_count, HEAD_DIM), jnp.float32),
    )
    running_max, running_sum, weighted = fold_keys(
        initial,
        lax.all_gather(key_rows, "fsdp", axis=0, tiled=True),
        lax.all_gather(value_rows, "fsdp", axis=0, tiled=True),
        jnp.int32(0),
        query_rows,
        mask_info,
    )
    attended = (weighted / running_sum[..., None]).astype(jnp.bfloat16)
    log_sum = running_max + jnp.log(running_sum)
    head_rows = jnp.transpose(attended, (1, 0, 2)).reshape(row_count, 1, head_span)
    mixed = lax.all_to_all(head_rows, "sp", split_axis=0, concat_axis=1, tiled=True).reshape(
        tokens, model_width
    )
    branch_one = jnp.dot(mixed, whole_out, preferred_element_type=jnp.float32) + whole_obias.astype(
        jnp.float32
    )
    first, first_normed, first_inverse = norm_forward(
        residual_in + branch_one, whole_gone.astype(jnp.float32), whole_sone.astype(jnp.float32)
    )
    first_low = first.astype(jnp.bfloat16)
    pre_active = jnp.dot(
        first_low, whole_up, preferred_element_type=jnp.float32
    ) + whole_ubias.astype(jnp.float32)
    active = jax.nn.gelu(pre_active, approximate=False).astype(jnp.bfloat16)
    branch_two = jnp.dot(
        active, whole_down, preferred_element_type=jnp.float32
    ) + whole_dbias.astype(jnp.float32)
    result, second_normed, second_inverse = norm_forward(
        first + branch_two, whole_gtwo.astype(jnp.float32), whole_stwo.astype(jnp.float32)
    )
    cotangent = out_cotangent.astype(jnp.float32)
    grad_second, grad_gtwo, grad_stwo = norm_backward(
        cotangent, second_normed, second_inverse, whole_gtwo.astype(jnp.float32)
    )
    grad_down = grad_second.astype(jnp.bfloat16)
    grad_dweight = outer_sum(active, grad_down)
    grad_dbias = jnp.sum(grad_down.astype(jnp.float32), axis=0)
    grad_active = times_transposed(grad_down, whole_down)
    normal_cdf = 0.5 * (1.0 + jax.scipy.special.erf(pre_active * 0.7071067811865476))
    density = jnp.exp(-0.5 * pre_active * pre_active) * 0.3989422804014327
    grad_pre = (grad_active * (normal_cdf + pre_active * density)).astype(jnp.bfloat16)
    grad_uweight = outer_sum(first_low, grad_pre)
    grad_ubias = jnp.sum(grad_pre.astype(jnp.float32), axis=0)
    grad_first = grad_second + times_transposed(grad_pre, whole_up)
    grad_first_sum, grad_gone, grad_sone = norm_backward(
        grad_first, first_normed, first_inverse, whole_gone.astype(jnp.float32)
    )
    grad_branch = grad_first_sum.astype(jnp.bfloat16)
    grad_oweight = outer_sum(mixed, grad_branch)
    grad_obias = jnp.sum(grad_branch.astype(jnp.float32), axis=0)
    grad_mixed = times_transposed(grad_branch, whole_out).astype(jnp.bfloat16)
    grad_heads = lax.all_to_all(
        grad_mixed.reshape(tokens, groups, head_span), "sp", split_axis=1, concat_axis=0, tiled=True
    )
    grad_attended = grad_heads.reshape(row_count, local_heads, HEAD_DIM)
    deltas = jnp.einsum(
        "rhd,hrd->hr", grad_attended.astype(jnp.float32), attended.astype(jnp.float32)
    )
    key_again, value_again = (
        lax.all_gather(key_rows, "fsdp", axis=0, tiled=True),
        lax.all_gather(value_rows, "fsdp", axis=0, tiled=True),
    )
    grad_query, terms = attention_grads(
        query_rows, key_again, value_again, grad_attended, log_sum, deltas, mask_info
    )
    grad_pairs = lax.psum_scatter(
        terms.astype(jnp.bfloat16), "fsdp", scatter_dimension=0, tiled=True
    )
    stacked = jnp.concatenate(
        (grad_query.astype(jnp.bfloat16).reshape(row_count, head_span), grad_pairs), axis=1
    ).reshape(row_count, 3, 1, head_span)
    returned = lax.all_to_all(stacked, "sp", split_axis=0, concat_axis=2, tiled=True)
    grad_qkv = returned.reshape(tokens, 3 * model_width)
    grad_qweight = outer_sum(hidden_in, grad_qkv)
    column_sums = jnp.sum(grad_qkv.astype(jnp.float32), axis=0)
    grad_qbias = column_sums[:model_width]
    grad_vbias = column_sums[2 * model_width :]
    input_grad = grad_first_sum + times_transposed(grad_qkv, whole_qkv)
    (
        share_qkv,
        share_qbias,
        share_vbias,
        share_out,
        share_obias,
        share_gone,
        share_sone,
        share_up,
        share_ubias,
        share_down,
        share_dbias,
        share_gtwo,
        share_stwo,
    ) = (
        lax.psum_scatter(
            grad_qweight.astype(jnp.bfloat16), "fsdp", scatter_dimension=0, tiled=True
        ).astype(jnp.float32),
        lax.psum_scatter(
            grad_qbias.astype(jnp.bfloat16), "fsdp", scatter_dimension=0, tiled=True
        ).astype(jnp.float32),
        lax.psum_scatter(
            grad_vbias.astype(jnp.bfloat16), "fsdp", scatter_dimension=0, tiled=True
        ).astype(jnp.float32),
        lax.psum_scatter(
            grad_oweight.astype(jnp.bfloat16), "fsdp", scatter_dimension=0, tiled=True
        ).astype(jnp.float32),
        lax.psum_scatter(
            grad_obias.astype(jnp.bfloat16), "fsdp", scatter_dimension=0, tiled=True
        ).astype(jnp.float32),
        lax.psum_scatter(
            grad_gone.astype(jnp.bfloat16), "fsdp", scatter_dimension=0, tiled=True
        ).astype(jnp.float32),
        lax.psum_scatter(
            grad_sone.astype(jnp.bfloat16), "fsdp", scatter_dimension=0, tiled=True
        ).astype(jnp.float32),
        lax.psum_scatter(
            grad_uweight.astype(jnp.bfloat16), "fsdp", scatter_dimension=0, tiled=True
        ).astype(jnp.float32),
        lax.psum_scatter(
            grad_ubias.astype(jnp.bfloat16), "fsdp", scatter_dimension=0, tiled=True
        ).astype(jnp.float32),
        lax.psum_scatter(
            grad_dweight.astype(jnp.bfloat16), "fsdp", scatter_dimension=0, tiled=True
        ).astype(jnp.float32),
        lax.psum_scatter(
            grad_dbias.astype(jnp.bfloat16), "fsdp", scatter_dimension=0, tiled=True
        ).astype(jnp.float32),
        lax.psum_scatter(
            grad_gtwo.astype(jnp.bfloat16), "fsdp", scatter_dimension=0, tiled=True
        ).astype(jnp.float32),
        lax.psum_scatter(
            grad_stwo.astype(jnp.bfloat16), "fsdp", scatter_dimension=0, tiled=True
        ).astype(jnp.float32),
    )
    totals = (
        lax.psum(share_qkv.astype(jnp.bfloat16), "sp").astype(jnp.float32),
        lax.psum(share_qbias.astype(jnp.bfloat16), "sp").astype(jnp.float32),
        lax.psum(share_vbias.astype(jnp.bfloat16), "sp").astype(jnp.float32),
        lax.psum(share_out.astype(jnp.bfloat16), "sp").astype(jnp.float32),
        lax.psum(share_obias.astype(jnp.bfloat16), "sp").astype(jnp.float32),
        lax.psum(share_gone.astype(jnp.bfloat16), "sp").astype(jnp.float32),
        lax.psum(share_sone.astype(jnp.bfloat16), "sp").astype(jnp.float32),
        lax.psum(share_up.astype(jnp.bfloat16), "sp").astype(jnp.float32),
        lax.psum(share_ubias.astype(jnp.bfloat16), "sp").astype(jnp.float32),
        lax.psum(share_down.astype(jnp.bfloat16), "sp").astype(jnp.float32),
        lax.psum(share_dbias.astype(jnp.bfloat16), "sp").astype(jnp.float32),
        lax.psum(share_gtwo.astype(jnp.bfloat16), "sp").astype(jnp.float32),
        lax.psum(share_stwo.astype(jnp.bfloat16), "sp").astype(jnp.float32),
    )
    return (result.astype(jnp.bfloat16), input_grad) + tuple(totals)


def solution(mesh):
    placed = (
        P(("fsdp", "sp"), None),
        P("fsdp", None),
        P("fsdp"),
        P("fsdp"),
        P("fsdp", None),
        P("fsdp"),
        P("fsdp"),
        P("fsdp"),
        P("fsdp", None),
        P("fsdp"),
        P("fsdp", None),
        P("fsdp"),
        P("fsdp"),
        P("fsdp"),
        P(),
        P(("fsdp", "sp"), None),
    )
    return jax.shard_map(
        on_device,
        mesh=mesh,
        in_specs=placed,
        out_specs=(
            P(("fsdp", "sp"), None),
            P(("fsdp", "sp"), None),
            P("fsdp", None),
            P("fsdp"),
            P("fsdp"),
            P("fsdp", None),
            P("fsdp"),
            P("fsdp"),
            P("fsdp"),
            P("fsdp", None),
            P("fsdp"),
            P("fsdp", None),
            P("fsdp"),
            P("fsdp"),
            P("fsdp"),
        ),
        check_vma=False,
    )
```

profile of v0, /device:TPU:1, one launch (start us, length us, event | category | flops | bytes accessed | tf_op | source)
XLA Modules:
  0.0 2180.5 jit_solution(5839901821439205524)
XLA Ops:
  17.3 158.3 %all-reduce.19 = (bf16[768]{0:T(1024)(128)(2,1)S(1)}, bf16[768]{0:T(1024)(128)(2,1)S(1)}, bf16[3072]{0:T(1024)(128)(2,1)S(1)}, bf16[768]{0:T(1024)(128)(2,1)S(1)...) all-reduce(bf16[768]{0:T(1024)(128)(2,1)S(1)} %dynamic-update-slice, ...), channel_id=1, replica_groups=mesh['sp'=4,'fsdp'=32] {'fsdp'}, use_global_device_ids=true, to_apply=%add.1 | all-reduce | flops 8448 | bytes 33792
  178.8 39.5 %all_to_all.63 = bf16[128,3,4,192]{0,3,1,2:T(8,128)(2,1)S(1)} all-to-all(bf16[128,3,4,192]{0,3,1,2:T(8,128)(2,1)S(1)} %copy.123), channel_id=1, replica_groups=mesh['sp'=4,'fsdp'=32] {'sp'}, dimensions={2} | all-to-all | bytes 1179648 | tf_op jit(solution)/shard_map/all_to_all | solution.py:190
  222.2 94.6 %all-gather.11.cloned.1.call-done = bf16[16384,3,64]{0,2,1:T(8,128)(2,1)} async-done(((bf16[512,3,64]{0,2,1:T(8,128)(2,1)}), bf16[16384,3,64]{0,2,1:T(8,128)(2,1)}) %all-gather.11.cloned.1.call-update) | async-done | bytes 6291472 | tf_op jit(solution)/shard_map/all_gather | solution.py:202
  316.8 6.4 copy.172
  323.2 99.5 %all-gather.9.cloned.1.call-done = bf16[16384,3,64]{0,2,1:T(8,128)(2,1)} async-done(((bf16[512,3,64]{0,2,1:T(8,128)(2,1)}), bf16[16384,3,64]{0,2,1:T(8,128)(2,1)}) %all-gather.9.cloned.1.call-update) | async-done | bytes 6291472 | tf_op jit(solution)/shard_map/all_gather | solution.py:201
  422.7 6.4 copy.173
  429.1 150.7 %while.32 = (s32[]{:T(128)}, f32[3,512]{1,0:T(4,128)S(1)}, f32[3,512]{1,0:T(4,128)S(1)}, f32[3,512,64]{1,2,0:T(8,128)S(1)}, s32[16]{0:T(128)}, /*index=5*/s32[]{...) while((s32[]{:T(128)}, f32[3,512]{1,0:T(4,128)S(1)}, ...), condition=%wide.region_3.4_spmd.clone, body=%wide.region_0.3_spmd.clone.sunk | while | flops 420280832 | bytes 20746408 | solution.py:89
  582.3 5.0 all-to-all-start.1
  587.4 5.4 all-to-all-done.1
  595.7 7.6 fusion.50
  603.4 57.6 %all-gather.17.cloned.1.call-done = bf16[3072,768]{1,0:T(8,128)(2,1)} async-done(((bf16[96,768]{1,0:T(8,128)(2,1)}), bf16[3072,768]{1,0:T(8,128)(2,1)}) %all-gather.17.cloned.1.call-update) | async-done | bytes 4718608 | tf_op jit(solution)/shard_map/all_gather | solution.py:179
  676.4 5.5 all-to-all-start.2
  682.4 3.9 all-to-all-done.2
  688.2 245.8 %while.33 = (s32[]{:T(128)}, f32[512,3,64]{0,2,1:T(8,128)S(1)}, bf16[16,1024,384]{2,1,0:T(8,128)(2,1)}, bf16[16,1024,3,64]{1,3,2,0:T(8,128)(2,1)}, s32[16]{0:T(1...) while((s32[]{:T(128)}, f32[512,3,64]{0,2,1:T(8,128)S(1)}, ...), condition=%wide.region_13.14_spmd.clone, body=%wide.region_12.13_spmd.clone.sunk | while | flops 1025727488 | bytes 36592828 | solution.py:122
  757.3 3.5 fusion.155
  772.7 3.5 fusion.155
  788.0 3.5 fusion.155
  803.4 3.5 fusion.155
  818.8 3.5 fusion.155
  911.0 3.5 fusion.155
  934.3 246.8 %reduce-scatter.8.cloned.1.call-done = bf16[512,384]{1,0:T(8,128)(2,1)} async-done(((bf16[16384,384]{1,0:T(8,128)(2,1)}), bf16[512,384]{1,0:T(8,128)(2,1)}) %reduce-scatter.8.cloned.1.call-update) | async-done | bytes 393232 | tf_op jit(solution)/shard_map/reduce_scatter | solution.py:265
  1183.3 19.1 all_to_all.64
  1207.5 5.8 copy.151
  1214.5 3.6 convolution_convert_fusion.1
  1219.3 3.6 convolution_convert_fusion
  1236.9 151.0 %all-reduce.18 = (bf16[768]{0:T(1024)(128)(2,1)}, bf16[768]{0:T(1024)(128)(2,1)}, bf16[768]{0:T(1024)(128)(2,1)}, bf16[768]{0:T(1024)(128)(2,1)}, bf16[768]{0:T(...) all-reduce(bf16[768]{0:T(1024)(128)(2,1)} %dynamic-update-slice.8, ...), channel_id=1, replica_groups=mesh['sp'=4,'fsdp'=32] {'fsdp'}, use_global_device_ids=true, to_apply=%add.8 | all-reduce | flops 9984 | bytes 39936
  1388.6 47.8 %reduce-scatter.16.cloned.1.call-done = bf16[24,2304]{1,0:T(8,128)(2,1)} async-done(((bf16[768,2304]{1,0:T(8,128)(2,1)}), bf16[24,2304]{1,0:T(8,128)(2,1)}) %reduce-scatter.16.cloned.1.call-update) | async-done | bytes 110608
  1438.4 230.7 %reduce-scatter.12.cloned.1.call-done = bf16[24,3072]{1,0:T(8,128)(2,1)} async-done(((bf16[768,3072]{1,0:T(8,128)(2,1)}), bf16[24,3072]{1,0:T(8,128)(2,1)}) %reduce-scatter.12.cloned.1.call-update) | async-done | bytes 147472 | tf_op jit(solution)/shard_map/reduce_scatter | solution.py:314
  1669.1 232.4 %reduce-scatter.14.cloned.1.call-done = bf16[96,768]{1,0:T(8,128)(2,1)} async-done(((bf16[3072,768]{1,0:T(8,128)(2,1)}), bf16[96,768]{1,0:T(8,128)(2,1)}) %reduce-scatter.14.cloned.1.call-update) | async-done | bytes 147472 | tf_op jit(solution)/shard_map/reduce_scatter | solution.py:320
  1912.4 213.4 %reduce-scatter.10.cloned.1.call-done = bf16[24,768]{1,0:T(8,128)(2,1)} async-done(((bf16[768,768]{1,0:T(8,128)(2,1)}), bf16[24,768]{1,0:T(8,128)(2,1)}) %reduce-scatter.10.cloned.1.call-update) | async-done | bytes 36880 | tf_op jit(solution)/shard_map/reduce_scatter | solution.py:302
  2125.8 14.1 all-reduce.20
  2155.0 13.5 all-reduce.24.cloned.1.call-done
  (486 shorter events, 468.7 us)
Async XLA Ops:
  7.2 168.5 %all-gather.7.cloned.1.call-start = ((), (), s32[]{:S(2)}) async-start(), calls=%async_computation.9 | async-start | bytes 3649536 | tf_op jit(solution)/shard_map/all_gather | solution.py:170
  7.9 308.9 %all-gather.11.cloned.1.call-start = ((), (), s32[]{:S(2)}) async-start(), calls=%async_computation.11 | async-start | bytes 6488064 | tf_op jit(solution)/shard_map/all_gather | solution.py:202
  219.2 203.5 %all-gather.9.cloned.1.call-start = ((), (), s32[]{:S(2)}) async-start(), calls=%async_computation.10 | async-start | bytes 6488064 | tf_op jit(solution)/shard_map/all_gather | solution.py:201
  219.9 373.7 %all-gather.13.cloned.1.call-start = ((), (), s32[]{:S(2)}) async-start(), calls=%async_computation.12 | async-start | bytes 1216512 | tf_op jit(solution)/shard_map/all_gather | solution.py:173
  220.5 375.2 %all-gather.15.cloned.1.call-start = ((), (), s32[]{:S(2)}) async-start(), calls=%async_computation.13 | async-start | bytes 4866048 | tf_op jit(solution)/shard_map/all_gather | solution.py:177
  221.1 439.9 %all-gather.17.cloned.1.call-start = ((), (), s32[]{:S(2)}) async-start(), calls=%async_computation.14 | async-start | bytes 4866048 | tf_op jit(solution)/shard_map/all_gather | solution.py:179
  581.3 12.4 copy-start.11
  582.3 10.5 all-to-all-start.1
  587.3 81.3 %copy-start.15 = (f32[768]{0:T(1024)}, f32[768]{0:T(1024)S(1)}, u32[]{:S(2)}) copy-start(f32[768]{0:T(1024)S(1)} %convert_element_type.205) | copy-start | bytes 9220
  587.3 73.7 %copy-start.17 = (f32[768]{0:T(1024)}, f32[768]{0:T(1024)S(1)}, u32[]{:S(2)}) copy-start(f32[768]{0:T(1024)S(1)} %convert_element_type.206) | copy-start | bytes 9220
  587.3 78.1 %copy-start.19 = (f32[768]{0:T(1024)}, f32[768]{0:T(1024)S(1)}, u32[]{:S(2)}) copy-start(f32[768]{0:T(1024)S(1)} %convert_element_type.211) | copy-start | bytes 9220
  595.5 73.1 %copy-start.21 = (f32[128]{0:T(128)}, f32[128]{0:T(128)S(1)}, u32[]{:S(2)}) copy-start(f32[128]{0:T(128)S(1)} %broadcast_multiply_fusion.5) | copy-start | bytes 1540
  595.7 72.9 %copy-start.23 = (f32[128]{0:T(128)}, f32[128]{0:T(128)S(1)}, u32[]{:S(2)}) copy-start(f32[128]{0:T(128)S(1)} %add_rsqrt_fusion.1) | copy-start | bytes 1540
  603.4 61.0 %copy-start.3 = (bf16[128,3072]{1,0:T(8,128)(2,1)}, bf16[128,3072]{1,0:T(8,128)(2,1)S(1)}, u32[]{:S(2)}) copy-start(bf16[128,3072]{1,0:T(8,128)(2,1)S(1)} %get-tuple-element.708) | copy-start | bytes 2359300
  661.0 3.6 copy-start.14
  661.0 5.2 copy-start.7
  664.4 4.2 copy-start.25
  664.6 3.9 copy-start.29
  665.4 4.1 slice-start
  673.4 549.8 %copy-start.2 = (f32[128,768]{1,0:T(8,128)}, f32[128,768]{1,0:T(8,128)S(1)}, u32[]{:S(2)}) copy-start(f32[128,768]{1,0:T(8,128)S(1)} %get-tuple-element.695) | copy-start | bytes 1179652
  676.4 9.9 all-to-all-start.2
  681.8 499.3 %reduce-scatter.8.cloned.1.call-start = ((), (), s32[]{:S(2)}) async-start(), calls=%async_computation.15 | async-start | bytes 12976128 | tf_op jit(solution)/shard_map/reduce_scatter | solution.py:265
  934.1 502.3 %reduce-scatter.16.cloned.1.call-start = ((), (), s32[]{:S(2)}) async-start(), calls=%async_computation.19 | async-start | bytes 3649536
  1213.4 455.7 %reduce-scatter.12.cloned.1.call-start = ((), (), s32[]{:S(2)}) async-start(), calls=%async_computation.17 | async-start | bytes 4866048 | tf_op jit(solution)/shard_map/reduce_scatter | solution.py:314
  1218.2 683.3 %reduce-scatter.14.cloned.1.call-start = ((), (), s32[]{:S(2)}) async-start(), calls=%async_computation.18 | async-start | bytes 4866048 | tf_op jit(solution)/shard_map/reduce_scatter | solution.py:320
  1222.9 902.9 %reduce-scatter.10.cloned.1.call-start = ((), (), s32[]{:S(2)}) async-start(), calls=%async_computation.16 | async-start | bytes 1216512 | tf_op jit(solution)/shard_map/reduce_scatter | solution.py:302
  1225.3 11.6 copy-start.27
  1225.3 11.6 copy-start.28
  1225.3 926.5 %copy-start = (bf16[768,2304]{1,0:T(8,128)(2,1)S(1)}, bf16[768,2304]{1,0:T(8,128)(2,1)}, u32[]{:S(2)}) copy-start(bf16[768,2304]{1,0:T(8,128)(2,1)} %all-gather.7.cloned.1.call-done) | copy-start | bytes 10616836
  1225.3 676.1 %copy-start.20 = (f32[768]{0:T(1024)S(1)}, f32[768]{0:T(1024)}, u32[]{:S(2)}) copy-start(f32[768]{0:T(1024)} %copy-done.19) | copy-start | bytes 9220
  1225.3 676.1 %copy-start.26 = (f32[128]{0:T(128)S(1)}, f32[128]{0:T(128)}, u32[]{:S(2)}) copy-start(f32[128]{0:T(128)} %copy-done.25) | copy-start | bytes 1540
  1225.3 943.1 %all-reduce.24.cloned.1.call-start = ((), (), s32[]{:S(2)}) async-start(), calls=%async_computation.20 | async-start | bytes 1769472 | tf_op jit(solution)/shard_map/psum | solution.py:334
  (15 other events, 24.2 us)
Sparse Core Ops, SparseCore 0:
  11.1 81.2 all-gather.6
  219.3 97.4 all-gather.10
  320.1 102.5 all-gather.8
  425.6 65.8 all-gather.12
  494.5 81.6 all-gather.14
  579.1 81.8 all-gather.16
  934.2 246.8 reduce-scatter.7
  1213.5 222.8 reduce-scatter.15
  1441.5 227.5 reduce-scatter.11
  1674.0 227.3 reduce-scatter.13
  1906.3 219.4 reduce-scatter.9
  2128.4 40.0 all-reduce.23
where the time goes:
time: 2190 us; the launch traced here: 2180 us
  waiting for transfers between devices  1250 us (57%)
  blocking collectives  382 us (17%)
  matrix products  299 us (14%)
  local copies, waits for them, and re-layouts  122 us (6%)
  other arithmetic  98.5 us (4%)
    unnamed x2, blocking collectives  309 us
    reduce_scatter x1, waiting for transfers between devices, on_device(): lax.psum_scatter(terms.astype(jnp.bfloat16), 'fsdp', scatter_dimension=0,...  247 us
    reduce_scatter x1, waiting for transfers between devices, on_device(): lax.psum_scatter(grad_dweight.astype(jnp.bfloat16), 'fsdp', scatter_dimen...  232 us
    reduce_scatter x1, waiting for transfers between devices, on_device(): lax.psum_scatter(grad_uweight.astype(jnp.bfloat16), 'fsdp', scatter_dimen...  231 us
    reduce_scatter x1, waiting for transfers between devices, on_device(): lax.psum_scatter(grad_oweight.astype(jnp.bfloat16), 'fsdp', scatter_dimen...  213 us
    all_gather x1, waiting for transfers between devices, on_device(): lax.all_gather(key_rows, 'fsdp', axis=0, tiled=True)  99.5 us
    all_gather x1, waiting for transfers between devices, on_device(): lax.all_gather(value_rows, 'fsdp', axis=0, tiled=True)  94.6 us
    dot_general x32, matrix products, block_scores(): jnp.einsum('rhd,khd->hrk', query_rows, key_block, preferred_element_type=...  72.1 us
  transfers between devices with their start and end apart: 14, of which 11 were waited for; matrix products, arithmetic and copies ran while one was open for 11% of the time, Pallas kernels for 0%

commit v1 on v0

v1 whole, which is shorter than its diff:
```python
import functools

import jax
import jax.numpy as jnp
from jax import lax
from jax.experimental import pallas as pl
from jax.experimental.pallas import tpu as pltpu
from jax.sharding import PartitionSpec as P

HEADS = 12
HEAD_DIM = 64
SP = 4
FS = 32
YG = 4
XG = 8
LH = HEADS // SP

BF = jnp.bfloat16
F32 = jnp.float32
MESH = pl.DeviceIdType.MESH
epsilon = 1e-05
masked = -1e30
VMEM_LIMIT = 56 * 1024 * 1024


def dot_nn(a, b):
    return lax.dot_general(a, b, (((1,), (0,)), ((), ())), preferred_element_type=F32)


def dot_nt(a, b):
    return lax.dot_general(a, b, (((1,), (1,)), ((), ())), preferred_element_type=F32)


def dot_tn(a, b):
    return lax.dot_general(a, b, (((0,), (0,)), ((), ())), preferred_element_type=F32)


def norm_forward(incoming, norm_gain, norm_shift):
    row_mean = jnp.mean(incoming, axis=-1, keepdims=True)
    centered = incoming - row_mean
    inverse = lax.rsqrt(jnp.mean(centered * centered, axis=-1, keepdims=True) + epsilon)
    normed = centered * inverse
    return (normed * norm_gain + norm_shift, normed, inverse)


def norm_backward(incoming, normed, inverse, norm_gain):
    scaled = incoming * norm_gain
    adjusted = (
        scaled
        - jnp.mean(scaled, axis=-1, keepdims=True)
        - normed * jnp.mean(scaled * normed, axis=-1, keepdims=True)
    )
    return (
        adjusted * inverse,
        jnp.sum(incoming * normed, axis=0, keepdims=True),
        jnp.sum(incoming, axis=0, keepdims=True),
    )


def loop(low, high, body):
    def step(d, carried):
        body(d)
        return carried

    lax.fori_loop(low, high, step, 0)


def remote(src, dst, send, recv, **device):
    return pltpu.make_async_remote_copy(
        src_ref=src,
        dst_ref=dst,
        send_sem=send,
        recv_sem=recv,
        device_id=device,
        device_id_type=MESH,
    )


def greet(barrier, **device):
    pl.semaphore_signal(barrier, inc=1, device_id=device, device_id_type=MESH)


def greet_all(f, s):
    barrier = pltpu.get_barrier_semaphore()
    loop(1, FS, lambda d: greet(barrier, fsdp=lax.rem(f + d, FS)))
    loop(1, SP, lambda d: greet(barrier, sp=lax.rem(s + d, SP)))
    pl.semaphore_wait(barrier, FS - 1 + SP - 1)


def project_kernel(
    hid, wq, up, down, out, small,
    hid_all, wqkv, q_all, kv_all, up_g, down_g, out_g, vecs,
    wq_g, small_g, wf, q_st, kv_st, qvb,
    hid_s, hid_r, wq_s, wq_r, up_s, up_r, dn_s, dn_r, ou_s, ou_r, sm_s, sm_r,
    q_s, q_r, kv_s, kv_r, loc,
):
    s = lax.axis_index("sp")
    f = lax.axis_index("fsdp")
    i, j = f // YG, lax.rem(f, YG)
    owner = s == f // 8
    greet_all(f, s)
    rows = hid.shape[0]

    def hid_copy(d):
        dst = hid_all.at[pl.ds(s * rows, rows)]
        return remote(hid, dst, hid_s.at[d - 1], hid_r.at[d - 1], sp=lax.rem(s + d, SP))

    def fs_copy(src, buf, send, recv):
        return lambda d: remote(
            src, buf.at[f], send.at[d - 1], recv.at[d - 1], fsdp=lax.rem(f + d, FS)
        )

    wq_copy = fs_copy(wq, wq_g, wq_s, wq_r)
    small_copy = fs_copy(small, small_g, sm_s, sm_r)
    up_copy = fs_copy(up, up_g, up_s, up_r)

    def down_copy(d):
        k = lax.rem(f, 8)
        return remote(down, down_g.at[k], dn_s.at[d - 1], dn_r.at[k], fsdp=lax.rem(f + d, FS))

    def out_copy(d):
        k = lax.rem(f, 8)
        return remote(out, out_g.at[k], ou_s.at[d - 1], ou_r.at[k], fsdp=lax.rem(f + d, FS))

    loop(1, SP, lambda d: hid_copy(d).start())

    def first_sends(d):
        wq_copy(d).start()
        small_copy(d).start()

    loop(1, FS, first_sends)
    hid_all[pl.ds(pl.multiple_of(s * rows, rows), rows), :] = hid[...]
    wq_g[f] = wq[...]
    small_g[f] = small[...]
    up_own = pltpu.make_async_copy(up, up_g.at[f], loc.at[0])
    up_own.start()

    loop(1, SP, lambda d: hid_copy(d).wait())

    def first_waits(d):
        wq_copy(d).wait()
        small_copy(d).wait()

    loop(1, FS, first_waits)

    width = vecs.shape[1]
    total = jnp.zeros((8, width), F32)
    pad = jnp.zeros((8, width - 128), F32)
    for n in range(FS):
        piece = small_g[n][0:8].astype(F32)
        wide = jnp.concatenate((piece, pad), axis=1)
        total = total + (wide if n == 0 else pltpu.roll(wide, 24 * n, 1))
    vecs[0:8, :] = total
    ub = jnp.zeros((8, width), F32)
    qv = jnp.zeros((8, width), F32)
    for k in range(8):
        block = small_g[8 * s + k].astype(F32)
        ub_wide = jnp.concatenate((block[8:16], pad), axis=1)
        qv_wide = jnp.concatenate((block[0:8], pad), axis=1)
        ub = ub + (ub_wide if k == 0 else pltpu.roll(ub_wide, 96 * k, 1))
        qv = qv + (qv_wide if k == 0 else pltpu.roll(qv_wide, 24 * k, 1))
    vecs[8:16, :] = ub
    qvb[...] = qv
    lane = lax.broadcasted_iota(jnp.int32, (1, width), 1)
    qrow = qvb[0:1, :]
    vrow = qvb[1:2, :]
    bias = jnp.zeros((1, width), F32)
    wide_q = jnp.broadcast_to(qrow, (8, width))
    wide_v = jnp.broadcast_to(vrow, (8, width))
    bias = jnp.where((lane >= 384) & (lane < 576), pltpu.roll(wide_q, 384, 1)[0:1], 0.0)
    for h in range(LH):
        here = (lane >= 128 * h + 64) & (lane < 128 * h + 128)
        bias = bias + jnp.where(here, pltpu.roll(wide_v, 64 * h + 64, 1)[0:1], 0.0)

    def assemble(n):
        wf[pl.ds(pl.multiple_of(24 * n, 8), 24), :] = wq_g[n].astype(F32)

    loop(0, FS, assemble)
    wqkv[...] = wf[...].astype(BF)

    low_lane = lax.broadcasted_iota(jnp.int32, (rows, 128), 1) < HEAD_DIM

    def project(b):
        at = pl.ds(pl.multiple_of(b * rows, rows), rows)
        p = dot_nn(hid_all[at, :], wqkv[...]) + bias[:, :576]
        for h in range(LH):
            kv_st[h, at, :] = p[:, 128 * h : 128 * h + 128].astype(BF)
        q01 = p[:, 384:512] * 0.125
        q2 = jnp.concatenate((p[:, 512:576], jnp.zeros((rows, 64), F32)), axis=1) * 0.125
        q_st[0, at, :] = jnp.where(low_lane, q01, 0.0).astype(BF)
        q_st[1, at, :] = jnp.where(low_lane, pltpu.roll(q01, 64, 1), 0.0).astype(BF)
        q_st[2, at, :] = q2.astype(BF)

    loop(0, SP, project)

    def kv_copy(d):
        to = lax.rem(i + d, XG) * YG + j
        return remote(kv_st, kv_all.at[i], kv_s.at[d - 1], kv_r.at[d - 1], fsdp=to)

    def q_copy(d):
        to = i * YG + lax.rem(j + d, YG)
        return remote(q_st, q_all.at[j], q_s.at[d - 1], q_r.at[d - 1], fsdp=to)

    loop(1, XG, lambda d: kv_copy(d).start())
    loop(1, YG, lambda d: q_copy(d).start())
    kv_own = pltpu.make_async_copy(kv_st, kv_all.at[i], loc.at[1])
    q_own = pltpu.make_async_copy(q_st, q_all.at[j], loc.at[2])
    kv_own.start()
    q_own.start()
    loop(1, FS, lambda d: up_copy(d).start())

    @pl.when(owner)
    def _():
        def both(d):
            down_copy(d).start()
            out_copy(d).start()

        loop(1, FS, both)
        dn_own = pltpu.make_async_copy(down, down_g.at[lax.rem(f, 8)], loc.at[3])
        ou_own = pltpu.make_async_copy(out, out_g.at[lax.rem(f, 8)], loc.at[4])
        dn_own.start()
        ou_own.start()
        dn_own.wait()
        ou_own.wait()

    kv_own.wait()
    q_own.wait()
    up_own.wait()
    loop(1, XG, lambda d: kv_copy(d).wait())
    loop(1, YG, lambda d: q_copy(d).wait())
    loop(1, FS, lambda d: up_copy(d).wait())

    @pl.when(owner)
    def _():
        def both(d):
            down_copy(d).wait_send()
            out_copy(d).wait_send()

        loop(1, FS, both)

    def arrivals(k):
        @pl.when(8 * s + k != f)
        def _():
            other = lax.rem(f + 1, FS)
            remote(down, down_g.at[k], dn_s.at[0], dn_r.at[k], fsdp=other).wait_recv()
            remote(out, out_g.at[k], ou_s.at[0], ou_r.at[k], fsdp=other).wait_recv()

    loop(0, 8, arrivals)


def attend_kernel(valid, q, kv, o):
    rows = q.shape[2]
    keys = kv.shape[2]
    f = lax.axis_index("fsdp")
    first_key = ((XG - 1) * YG + lax.rem(f, YG)) * keys
    query = q[0, 0]
    m = l = acc = None
    for c in range(XG):
        block = kv[c, 0]
        scores = dot_nt(query, block)
        if c == XG - 1:
            place = first_key + lax.broadcasted_iota(jnp.int32, (1, keys), 1)
            scores = jnp.where(place < valid[0], scores, masked)
        top = jnp.max(scores, axis=1, keepdims=True)
        new = top if c == 0 else jnp.maximum(m, top)
        p = jnp.exp(scores - new)
        part = jnp.sum(p, axis=1, keepdims=True)
        weighted = dot_nn(p.astype(BF), block)
        if c == 0:
            l, acc = part, weighted
        else:
            decay = jnp.exp(m - new)
            l = l * decay + part
            acc = acc * decay + weighted
        m = new
    log_sum = m + jnp.log(l)
    high = log_sum.astype(BF).astype(F32)
    lane = lax.broadcasted_iota(jnp.int32, (rows, 128), 1)
    result = jnp.where(lane >= 64, acc / l, jnp.where(lane < 32, high, log_sum - high))
    o[0, 0] = result.astype(BF)


def middle_kernel(
    o_part, wo, wup, wdn, vecs, hid, cot,
    result, gfs, d_all, ld_all, dup, ddn, dwo, vp,
    o_rb, att, ld, st, own, first, n1, inv1, x_all, act, deriv, gd, gp, gb, gsec, rb, dbuf, ldrow, vg,
    o_s, o_r, ag_s, ag_r, rs_s, rs_r, d_s, d_r, l_s, l_r, loc,
):
    s = lax.axis_index("sp")
    f = lax.axis_index("fsdp")
    i, j = f // YG, lax.rem(f, YG)
    rows = hid.shape[0]
    tall = SP * rows
    barrier = pltpu.get_barrier_semaphore()
    loop(1, YG, lambda d: greet(barrier, fsdp=i * YG + lax.rem(j + d, YG)))
    loop(1, SP, lambda d: greet(barrier, sp=lax.rem(s + d, SP)))
    pl.semaphore_wait(barrier, YG - 1 + SP - 1)

    def y_peer(d):
        return i * YG + lax.rem(j + d, YG)

    def o_copy(d):
        src = o_part.at[lax.rem(j + d, YG)]
        return remote(src, o_rb.at[d - 1], o_s.at[d - 1], o_r.at[d - 1], fsdp=y_peer(d))

    loop(1, YG, lambda d: o_copy(d).start())
    loop(1, YG, lambda d: o_copy(d).wait())

    def span(b):
        return pl.ds(pl.multiple_of(b * rows, rows), rows)

    lane = lax.broadcasted_iota(jnp.int32, (rows, 128), 1)

    def merge(b):
        at = span(b)
        sums = jnp.zeros((rows, 128), F32)
        for h in range(LH):
            parts = [o_part[j, h, at, :].astype(F32)]
            parts += [o_rb[d, h, at, :].astype(F32) for d in range(YG - 1)]
            logs = [p[:, 0:1] + p[:, 32:33] for p in parts]
            top = functools.reduce(jnp.maximum, logs)
            weights = [jnp.exp(g - top) for g in logs]
            total = functools.reduce(jnp.add, weights)
            merged = functools.reduce(jnp.add, [p * w for p, w in zip(parts, weights)]) / total
            att[at, 128 * h : 128 * h + 128] = jnp.where(lane >= 64, merged, 0.0).astype(BF)
            sums = jnp.where(lane == 2 * h, top + jnp.log(total), sums)
        ld[at, :] = sums

    loop(0, SP, merge)

    def gather(e, buf):
        def copy(d):
            at = buf.at[pl.ds(s * rows, rows)]
            return remote(at, at, ag_s.at[e, d - 1], ag_r.at[e, d - 1], sp=lax.rem(s + d, SP))

        return copy

    def scatter(e):
        def copy(d):
            src = st.at[e, pl.ds(lax.rem(s + d, SP) * rows, rows)]
            sems = (rs_s.at[e, d - 1], rs_r.at[e, d - 1])
            return remote(src, rb.at[e, d - 1], *sems, sp=lax.rem(s + d, SP))

        return copy

    def collect(e):
        loop(1, SP, lambda d: scatter(e)(d).wait())
        total = own[...]
        for d in range(SP - 1):
            total = total + rb[e, d].astype(F32)
        return total

    def out_part(d):
        b = lax.rem(s + d, SP)
        value = dot_nn(att[span(b), :], wo[...])

        @pl.when(d < SP)
        def _():
            st[0, span(b), :] = value.astype(BF)
            scatter(0)(d).start()

        @pl.when(d == SP)
        def _():
            own[...] = value

    loop(1, SP + 1, out_part)
    summed = hid[...].astype(F32) + collect(0) + vecs[2:3, :]
    value, normed, inverse = norm_forward(summed, vecs[3:4, :], vecs[4:5, :])
    first[...] = value
    n1[...] = normed
    inv1[...] = jnp.broadcast_to(inverse, inv1.shape)
    x_all[span(s), :] = value.astype(BF)
    loop(1, SP, lambda d: gather(0, x_all)(d).start())

    def pipeline(e, buf, work):
        def step(d):
            b = lax.rem(s + SP - d, SP)

            @pl.when(d > 0)
            def _():
                gather(e, buf)(d).wait_recv()

            value = work(b)

            @pl.when(d > 0)
            def _():
                st[e + 1, span(b), :] = value.astype(BF)
                scatter(e + 1)(SP - d).start()

            @pl.when(d == 0)
            def _():
                own[...] = value

        loop(0, SP, step)
        loop(1, SP, lambda d: gather(e, buf)(d).wait_send())

    def feed(b):
        at = span(b)
        pre = dot_nn(x_all[at, :], wup[...]) + vecs[8:9, :]
        cdf = 0.5 * (1.0 + lax.erf(pre * 0.7071067811865476))
        density = jnp.exp(-0.5 * pre * pre) * 0.3989422804014327
        active = (pre * cdf).astype(BF)
        act[at, :] = active
        deriv[at, :] = cdf + pre * density
        return dot_nn(active, wdn[...])

    pipeline(0, x_all, feed)
    summed = first[...] + collect(1) + vecs[5:6, :]
    value, normed, inverse = norm_forward(summed, vecs[6:7, :], vecs[7:8, :])
    result[...] = value.astype(BF)
    grad, ggain, gshift = norm_backward(cot[...].astype(F32), normed, inverse, vecs[6:7, :])
    gsec[...] = grad
    low = grad.astype(BF)
    gd[span(s), :] = low
    loop(1, SP, lambda d: gather(1, gd)(d).start())
    vg[...] = jnp.zeros(vg.shape, F32)
    vg[3:4, :] = jnp.sum(low.astype(F32), axis=0, keepdims=True)
    vg[4:5, :] = ggain
    vg[5:6, :] = gshift

    def back(b):
        at = span(b)
        grad_pre = (dot_nt(gd[at, :], wdn[...]) * deriv[at, :]).astype(BF)
        gp[at, :] = grad_pre
        return dot_nt(grad_pre, wup[...])

    pipeline(1, gd, back)

    def weight_terms(c):
        at = pl.ds(pl.multiple_of(128 * c, 128), 128)
        ddn[at, :] = dot_tn(act[:, at], gd[...]).astype(BF)
        dup[at, :] = dot_tn(x_all[:, at], gp[...]).astype(BF)

    loop(0, act.shape[1] // 128, weight_terms)
    ub = jnp.sum(gp[...].astype(F32), axis=0, keepdims=True)
    grad_first = gsec[...] + collect(2)
    grad, ggain, gshift = norm_backward(grad_first, n1[...], inv1[:, 0:1], vecs[3:4, :])
    gfs[...] = grad
    low = grad.astype(BF)
    gb[span(s), :] = low
    loop(1, SP, lambda d: gather(2, gb)(d).start())
    vg[0:1, :] = jnp.sum(low.astype(F32), axis=0, keepdims=True)
    vg[1:2, :] = ggain
    vg[2:3, :] = gshift

    def branch(d):
        b = lax.rem(s + SP - d, SP)
        at = span(b)

        @pl.when(d > 0)
        def _():
            gather(2, gb)(d).wait_recv()

        value = dot_nt(gb[at, :], wo[...]).astype(BF)
        sums = ld[at, :]
        for h in range(LH):
            part = value[:, 128 * h : 128 * h + 128]
            dbuf[h, at, :] = part
            product = part.astype(F32) * att[at, 128 * h : 128 * h + 128].astype(F32)
            sums = jnp.where(lane == 2 * h + 1, jnp.sum(product, axis=1, keepdims=True), sums)
        ld[at, :] = sums

    loop(0, SP, branch)
    loop(1, SP, lambda d: gather(2, gb)(d).wait_send())
    ldrow[...] = jnp.transpose(ld[...], (1, 0))[0:8, :]

    def d_copy(d):
        return remote(dbuf, d_all.at[j], d_s.at[d - 1], d_r.at[d - 1], fsdp=y_peer(d))

    def l_copy(d):
        return remote(ldrow, ld_all.at[j], l_s.at[d - 1], l_r.at[d - 1], fsdp=y_peer(d))

    loop(1, YG, lambda d: d_copy(d).start())
    loop(1, YG, lambda d: l_copy(d).start())
    d_own = pltpu.make_async_copy(dbuf, d_all.at[j], loc.at[0])
    l_own = pltpu.make_async_copy(ldrow, ld_all.at[j], loc.at[1])
    d_own.start()
    l_own.start()
    for h in range(LH):
        value = dot_tn(att[:, 128 * h : 128 * h + 128], gb[...])
        dwo[64 * h : 64 * h + 64, :] = value[64:128].astype(BF)
    lane8 = lax.broadcasted_iota(jnp.int32, (8, 128), 1)
    wide = vg[...]
    width = wide.shape[1]
    ub_wide = jnp.broadcast_to(ub, (8, width))
    for n in range(FS):
        piece = wide if n == 0 else pltpu.roll(wide, width - 24 * n, 1)
        vp[n, 0:8, :] = jnp.where(lane8 < 24, piece[:, 0:128], 0.0)
        vp[n, 8:16, :] = jnp.zeros((8, 128), F32)
    for k in range(8):
        piece = ub_wide if k == 0 else pltpu.roll(ub_wide, width - 96 * k, 1)
        vp[8 * s + k, 8:16, :] = jnp.where(lane8 < 96, piece[:, 0:128], 0.0)
    d_own.wait()
    l_own.wait()
    loop(1, YG, lambda d: d_copy(d).wait())
    loop(1, YG, lambda d: l_copy(d).wait())


def attend_back_kernel(valid, q, dout, ld, kv, dkv, dq, acc):
    h = pl.program_id(0)
    step = pl.program_id(1)
    keys = kv.shape[2]
    f = lax.axis_index("fsdp")
    first_key = (step * YG + lax.rem(f, YG)) * keys

    @pl.when(step == 0)
    def _():
        acc[...] = jnp.zeros(acc.shape, F32)

    def work(last):
        block = kv[0, 0]
        flipped = jnp.transpose(block.astype(F32), (1, 0))[0:HEAD_DIM].astype(BF)
        total = None
        for n in range(YG):
            query = q[n, 0]
            grad = dout[n, 0]
            log_sum = ld[n, pl.ds(2 * h, 1), :]
            delta = ld[n, pl.ds(2 * h + 1, 1), :]
            scores = dot_nt(block, query)
            if last:
                place = first_key + lax.broadcasted_iota(jnp.int32, (keys, 1), 0)
                scores = jnp.where(place < valid[0], scores, masked)
            p = jnp.exp(scores - log_sum)
            grad_p = dot_nt(block, grad)
            grad_s = (p * (grad_p - delta)).astype(BF)
            terms = dot_nn(grad_s, query) + dot_nn(p.astype(BF), grad)
            total = terms if n == 0 else total + terms
            acc[n] = acc[n] + dot_nn(flipped, grad_s)
        dkv[0, 0] = total.astype(BF)

    @pl.when(step < XG - 1)
    def _():
        work(False)

    @pl.when(step == XG - 1)
    def _():
        work(True)
        dq[:, 0] = acc[...].astype(BF)


def finish_kernel(
    dkv, dq, hid_all, wqkv, gfs, dup, ddn, dwo, vp,
    input_grad, qkvg, upg, dng, outg, vecg, qvg,
    kv_rb, q_rb, g, wf, wp, bp, st, own, rb, wq_rb, up_rb, dn_rb, ou_rb, vp_rb, bp_rb,
    up_fin, dn_fin, ou_fin, v_fin, qv_fin,
    kv_s, kv_r, q_s, q_r, wq_s, wq_r, up_s, up_r, dn_s, dn_r, ou_s, ou_r, vp_s, vp_r, bp_s, bp_r,
    rs_s, rs_r, fin_s, fin_r, b_s, b_r,
):
    s = lax.axis_index("sp")
    f = lax.axis_index("fsdp")
    i, j = f // YG, lax.rem(f, YG)
    rows = gfs.shape[0]
    tall = SP * rows
    owner = s == f // 8
    greet_all(f, s)

    def kv_copy(d):
        to = lax.rem(i + d, XG)
        return remote(dkv.at[to], kv_rb.at[d - 1], kv_s.at[d - 1], kv_r.at[d - 1], fsdp=to * YG + j)

    def q_copy(d):
        to = lax.rem(j + d, YG)
        return remote(dq.at[to], q_rb.at[d - 1], q_s.at[d - 1], q_r.at[d - 1], fsdp=i * YG + to)

    def fs_copy(src, buf, send, recv):
        def copy(d):
            to = lax.rem(f + d, FS)
            return remote(src.at[to], buf.at[d - 1], send.at[d - 1], recv.at[d - 1], fsdp=to)

        return copy

    up_copy = fs_copy(dup, up_rb, up_s, up_r)
    vp_copy = fs_copy(vp, vp_rb, vp_s, vp_r)
    wq_copy = fs_copy(wp, wq_rb, wq_s, wq_r)
    bp_copy = fs_copy(bp, bp_rb, bp_s, bp_r)

    def owner_copies(k):
        to = 8 * s + k
        return (
            remote(ddn.at[k], dn_rb.at[f], dn_s.at[k], dn_r.at[f], fsdp=to),
            remote(dwo.at[k], ou_rb.at[f], ou_s.at[k], ou_r.at[f], fsdp=to),
        )

    loop(1, XG, lambda d: kv_copy(d).start())
    loop(1, YG, lambda d: q_copy(d).start())

    def early(d):
        up_copy(d).start()
        vp_copy(d).start()

    loop(1, FS, early)

    def to_owner(k):
        @pl.when(8 * s + k != f)
        def _():
            for copy in owner_copies(k):
                copy.start()

    loop(0, 8, to_owner)

    loop(1, XG, lambda d: kv_copy(d).wait())
    loop(1, YG, lambda d: q_copy(d).wait())

    def span(b):
        return pl.ds(pl.multiple_of(b * rows, rows), rows)

    def sum_keys(b):
        at = span(b)
        for h in range(LH):
            total = dkv[i, h, at, :].astype(F32)
            for d in range(XG - 1):
                total = total + kv_rb[d, h, at, :].astype(F32)
            g[at, 128 * h : 128 * h + 128] = total.astype(BF)

    loop(0, SP, sum_keys)
    total = dq[j].astype(F32)
    for d in range(YG - 1):
        total = total + q_rb[d].astype(F32)
    g[:, 384:576] = (jnp.transpose(total, (1, 0)) * 0.125).astype(BF)

    def weight_terms(c):
        at = pl.ds(pl.multiple_of(128 * c, 128), 128)
        wf[at, :] = dot_tn(hid_all[:, at], g[...])

    loop(0, wf.shape[0] // 128, weight_terms)

    def cut(n):
        wp[n] = wf[pl.ds(pl.multiple_of(24 * n, 8), 24), :].astype(BF)

    loop(0, FS, cut)
    loop(1, FS, lambda d: wq_copy(d).start())

    def input_part(d):
        b = lax.rem(s + d, SP)
        value = dot_nt(g[span(b), :], wqkv[...])

        @pl.when(d < SP)
        def _():
            st[span(b), :] = value.astype(BF)
            rs_copy(d).start()

        @pl.when(d == SP)
        def _():
            own[...] = value

    def rs_copy(d):
        to = lax.rem(s + d, SP)
        src = st.at[pl.ds(to * rows, rows)]
        return remote(src, rb.at[d - 1], rs_s.at[d - 1], rs_r.at[d - 1], sp=to)

    loop(1, SP + 1, input_part)

    sums = jnp.sum(g[...].astype(F32), axis=0, keepdims=True)
    lane = lax.broadcasted_iota(jnp.int32, (8, 128), 1)
    row = lax.broadcasted_iota(jnp.int32, (8, 256), 0)
    low = lax.broadcasted_iota(jnp.int32, (8, 128), 1) < 64
    wide = jnp.broadcast_to(jnp.concatenate((sums, jnp.zeros((1, 64), F32)), axis=1), (8, 640))
    heads = [pltpu.roll(wide[:, 128 * h : 128 * h + 128], 64, 1) for h in range(LH)]
    vrow = jnp.concatenate(
        (
            jnp.where(low, heads[0], wide[:, 128:256]),
            jnp.where(low, heads[2], 0.0),
        ),
        axis=1,
    )
    both = jnp.where(row == 0, wide[:, 384:640], jnp.where(row == 1, vrow, 0.0))
    bp[...] = jnp.zeros(bp.shape, F32)
    for k in range(8):
        piece = both if k == 0 else pltpu.roll(both, 256 - 24 * k, 1)
        bp[8 * s + k] = jnp.where(lane < 24, piece[:, 0:128], 0.0)
    loop(1, FS, lambda d: bp_copy(d).start())

    def late(d):
        up_copy(d).wait()
        vp_copy(d).wait()

    loop(1, FS, late)

    def add_up(src, buf, start):
        def step(d, total):
            return total + buf[d].astype(F32)

        return lax.fori_loop(0, FS - 1, step, start)

    up_fin[s] = add_up(dup, up_rb, dup[f].astype(F32)).astype(BF)
    v_fin[s] = add_up(vp, vp_rb, vp[f])

    def sp_copy(e, buf):
        def copy(d):
            at = buf.at[s]
            return remote(at, at, fin_s.at[e, d - 1], fin_r.at[e, d - 1], sp=lax.rem(s + d, SP))

        return copy

    loop(1, SP, lambda d: sp_copy(0, up_fin)(d).start())
    loop(1, SP, lambda d: sp_copy(1, v_fin)(d).start())

    def own_copies(d):
        to = lax.rem(s + d, SP)
        return (
            remote(dn_fin, dn_fin, b_s.at[0, d - 1], b_r.at[0], sp=to),
            remote(ou_fin, ou_fin, b_s.at[1, d - 1], b_r.at[1], sp=to),
        )

    @pl.when(owner)
    def _():
        def arrived(d):
            frm = lax.rem(f + d, FS)
            remote(ddn.at[0], dn_rb.at[frm], dn_s.at[0], dn_r.at[frm], fsdp=frm).wait_recv()
            remote(dwo.at[0], ou_rb.at[frm], ou_s.at[0], ou_r.at[frm], fsdp=frm).wait_recv()

        loop(1, FS, arrived)
        k = lax.rem(f, 8)
        dn_rb[f] = ddn[k]
        ou_rb[f] = dwo[k]

        def down_rows(c):
            at = pl.ds(pl.multiple_of(c * 32, 32), 32)

            def step(n, total):
                return total + dn_rb[n, at, :].astype(F32)

            start = jnp.zeros((32, dn_fin.shape[1]), F32)
            dn_fin[at, :] = lax.fori_loop(0, FS, step, start).astype(BF)

        loop(0, dn_fin.shape[0] // 32, down_rows)

        def step(n, total):
            return total + ou_rb[n].astype(F32)

        ou_fin[...] = lax.fori_loop(0, FS, step, jnp.zeros(ou_fin.shape, F32)).astype(BF)

        def send(d):
            for copy in own_copies(d):
                copy.start()

        loop(1, SP, send)

    def later(d):
        wq_copy(d).wait()
        bp_copy(d).wait()

    loop(1, FS, later)
    qkvg[s] = add_up(wp, wq_rb, wp[f].astype(F32)).astype(BF)
    qv_fin[s] = add_up(bp, bp_rb, bp[f])
    loop(1, SP, lambda d: sp_copy(2, qkvg)(d).start())
    loop(1, SP, lambda d: sp_copy(3, qv_fin)(d).start())

    loop(1, SP, lambda d: rs_copy(d).wait())
    total = gfs[...] + own[...]
    for d in range(SP - 1):
        total = total + rb[d].astype(F32)
    input_grad[...] = total

    loop(1, SP, lambda d: sp_copy(0, up_fin)(d).wait())
    loop(1, SP, lambda d: sp_copy(1, v_fin)(d).wait())
    for n in range(SP):
        upg[:, 768 * n : 768 * n + 768] = up_fin[n].astype(F32)
    vecg[...] = v_fin[0] + v_fin[1] + v_fin[2] + v_fin[3]

    @pl.when(owner)
    def _():
        def sent(d):
            for copy in own_copies(d):
                copy.wait_send()

        loop(1, SP, sent)

    @pl.when(jnp.logical_not(owner))
    def _():
        for copy in own_copies(1):
            copy.wait_recv()

    dng[...] = dn_fin[...].astype(F32)
    outg[...] = ou_fin[...].astype(F32)

    loop(1, SP, lambda d: sp_copy(2, qkvg)(d).wait())
    loop(1, SP, lambda d: sp_copy(3, qv_fin)(d).wait())
    qvg[...] = qv_fin[0] + qv_fin[1] + qv_fin[2] + qv_fin[3]

    def sent_all(k):
        @pl.when(8 * s + k != f)
        def _():
            for copy in owner_copies(k):
                copy.wait_send()

    loop(0, 8, sent_all)


def on_device(
    hidden_in,
    qkv_weight,
    query_bias,
    value_bias,
    output_weight,
    output_bias,
    first_gain,
    first_shift,
    up_weight,
    up_bias,
    down_weight,
    down_bias,
    second_gain,
    second_shift,
    valid_length,
    out_cotangent,
):
    s = lax.axis_index("sp")
    rows, width = hidden_in.shape
    tall = SP * rows
    slim = qkv_weight.shape[0]
    deep = down_weight.shape[0]
    share = up_weight.shape[1] // SP
    cols = LH * HEAD_DIM * 3
    vmem = pl.BlockSpec(memory_space=pltpu.VMEM)
    hbm = pl.BlockSpec(memory_space=pl.ANY)
    dma = pltpu.SemaphoreType.DMA
    shape = jax.ShapeDtypeStruct

    parts = qkv_weight.reshape(slim, 3, SP, LH, HEAD_DIM)
    parts = lax.dynamic_index_in_dim(parts, s, 2, keepdims=False)
    kv_cols = jnp.stack((parts[:, 1], parts[:, 2]), axis=2).reshape(slim, -1)
    wq = jnp.concatenate((kv_cols, parts[:, 0].reshape(slim, -1)), axis=1)
    up = lax.dynamic_slice_in_dim(up_weight, s * share, share, 1)
    small = jnp.stack(
        (
            query_bias, value_bias, output_bias, first_gain, first_shift, down_bias,
            second_gain, second_shift,
        )
    )
    small = jnp.pad(small, ((0, 8), (0, 128 - slim)))
    small = lax.dynamic_update_slice(small, up_bias[None, :], (8, 0))

    hid_all, wqkv, q_all, kv_all, up_g, down_g, out_g, vecs = pl.pallas_call(
        project_kernel,
        out_shape=(
            shape((tall, width), BF),
            shape((width, cols), BF),
            shape((YG, LH, tall, 128), BF),
            shape((XG, LH, tall, 128), BF),
            shape((FS, slim, share), BF),
            shape((8, deep, width), BF),
            shape((8, slim, width), BF),
            shape((16, width), F32),
        ),
        in_specs=[vmem] * 6,
        out_specs=(vmem, vmem, hbm, hbm, hbm, hbm, hbm, vmem),
        scratch_shapes=[
            pltpu.VMEM((FS, slim, cols), BF),
            pltpu.VMEM((FS, 16, 128), BF),
            pltpu.VMEM((width, cols), F32),
            pltpu.VMEM((LH, tall, 128), BF),
            pltpu.VMEM((LH, tall, 128), BF),
            pltpu.VMEM((8, width), F32),
        ]
        + [dma((n,)) for n in (3, 3, 31, 31, 31, 31, 31, 8, 31, 8, 31, 31, 3, 3, 7, 7, 5)],
        compiler_params=pltpu.CompilerParams(
            collective_id=0, has_side_effects=True, vmem_limit_bytes=VMEM_LIMIT
        ),
        name="project",
    )(hidden_in, wq, up, down_weight, output_weight, small)

    flops = 4 * LH * YG * XG * tall * tall * HEAD_DIM
    o_part = pl.pallas_call(
        attend_kernel,
        grid=(LH, YG),
        out_shape=shape((YG, LH, tall, 128), BF),
        in_specs=[
            pl.BlockSpec(memory_space=pltpu.SMEM),
            pl.BlockSpec((1, 1, tall, 128), lambda h, n: (n, h, 0, 0)),
            pl.BlockSpec((XG, 1, tall, 128), lambda h, n: (0, h, 0, 0)),
        ],
        out_specs=pl.BlockSpec((1, 1, tall, 128), lambda h, n: (n, h, 0, 0)),
        compiler_params=pltpu.CompilerParams(vmem_limit_bytes=VMEM_LIMIT),
        name="attend",
    )(valid_length, q_all, kv_all)

    wo = jnp.pad(out_g.reshape(LH, HEAD_DIM, width), ((0, 0), (HEAD_DIM, 0), (0, 0)))
    wo = wo.reshape(LH * 128, width)
    result, gfs, d_all, ld_all, dup, ddn, dwo, vp = pl.pallas_call(
        middle_kernel,
        out_shape=(
            shape((rows, width), BF),
            shape((rows, width), F32),
            shape((YG, LH, tall, 128), BF),
            shape((YG, 8, tall), F32),
            shape((width, share), BF),
            shape((share, width), BF),
            shape((LH * HEAD_DIM, width), BF),
            shape((FS, 16, 128), F32),
        ),
        in_specs=[vmem] * 7,
        out_specs=(vmem, vmem, hbm, hbm, vmem, vmem, vmem, vmem),
        scratch_shapes=[
            pltpu.VMEM((YG - 1, LH, tall, 128), BF),
            pltpu.VMEM((tall, LH * 128), BF),
            pltpu.VMEM((tall, 128), F32),
            pltpu.VMEM((3, tall, width), BF),
            pltpu.VMEM((rows, width), F32),
            pltpu.VMEM((rows, width), F32),
            pltpu.VMEM((rows, width), F32),
            pltpu.VMEM((rows, 128), F32),
            pltpu.VMEM((tall, width), BF),
            pltpu.VMEM((tall, share), BF),
            pltpu.VMEM((tall, share), F32),
            pltpu.VMEM((tall, width), BF),
            pltpu.VMEM((tall, share), BF),
            pltpu.VMEM((tall, width), BF),
            pltpu.VMEM((rows, width), F32),
            pltpu.VMEM((3, SP - 1, rows, width), BF),
            pltpu.VMEM((LH, tall, 128), BF),
            pltpu.VMEM((8, tall), F32),
            pltpu.VMEM((8, width), F32),
        ]
        + [dma((3,)), dma((3,))]
        + [dma((3, 3)) for _ in range(4)]
        + [dma((n,)) for n in (3, 3, 3, 3, 2)],
        compiler_params=pltpu.CompilerParams(
            collective_id=1, has_side_effects=True, vmem_limit_bytes=VMEM_LIMIT
        ),
        name="middle",
    )(
        o_part, wo, up_g.reshape(width, share), down_g.reshape(share, width), vecs,
        hidden_in, out_cotangent,
    )

    dkv, dq = pl.pallas_call(
        attend_back_kernel,
        grid=(LH, XG),
        out_shape=(shape((XG, LH, tall, 128), BF), shape((YG, LH, HEAD_DIM, tall), BF)),
        in_specs=[
            pl.BlockSpec(memory_space=pltpu.SMEM),
            pl.BlockSpec((YG, 1, tall, 128), lambda h, n: (0, h, 0, 0)),
            pl.BlockSpec((YG, 1, tall, 128), lambda h, n: (0, h, 0, 0)),
            pl.BlockSpec((YG, 8, tall), lambda h, n: (0, 0, 0)),
            pl.BlockSpec((1, 1, tall, 128), lambda h, n: (n, h, 0, 0)),
        ],
        out_specs=(
            pl.BlockSpec((1, 1, tall, 128), lambda h, n: (n, h, 0, 0)),
            pl.BlockSpec((YG, 1, HEAD_DIM, tall), lambda h, n: (0, h, 0, 0)),
        ),
        scratch_shapes=[pltpu.VMEM((YG, HEAD_DIM, tall), F32)],
        compiler_params=pltpu.CompilerParams(vmem_limit_bytes=VMEM_LIMIT),
        name="attend_back",
    )(valid_length, q_all, d_all, ld_all, kv_all)

    input_grad, qkvg, upg, dng, outg, vecg, qvg = pl.pallas_call(
        finish_kernel,
        out_shape=(
            shape((rows, width), F32),
            shape((SP, slim, cols), BF),
            shape((slim, SP * share), F32),
            shape((deep, width), F32),
            shape((slim, width), F32),
            shape((16, 128), F32),
            shape((8, 128), F32),
        ),
        in_specs=[vmem] * 9,
        out_specs=(vmem,) * 7,
        scratch_shapes=[
            pltpu.VMEM((XG - 1, LH, tall, 128), BF),
            pltpu.VMEM((YG - 1, LH * HEAD_DIM, tall), BF),
            pltpu.VMEM((tall, cols), BF),
            pltpu.VMEM((width, cols), F32),
            pltpu.VMEM((FS, slim, cols), BF),
            pltpu.VMEM((FS, 8, 128), F32),
            pltpu.VMEM((tall, width), BF),
            pltpu.VMEM((rows, width), F32),
            pltpu.VMEM((SP - 1, rows, width), BF),
            pltpu.VMEM((FS - 1, slim, cols), BF),
            pltpu.VMEM((FS - 1, slim, share), BF),
            pltpu.VMEM((FS, deep, width), BF),
            pltpu.VMEM((FS, slim, width), BF),
            pltpu.VMEM((FS - 1, 16, 128), F32),
            pltpu.VMEM((FS - 1, 8, 128), F32),
            pltpu.VMEM((SP, slim, share), BF),
            pltpu.VMEM((deep, width), BF),
            pltpu.VMEM((slim, width), BF),
            pltpu.VMEM((SP, 16, 128), F32),
            pltpu.VMEM((SP, 8, 128), F32),
        ]
        + [dma((n,)) for n in (7, 7, 3, 3, 31, 31, 31, 31, 8, 32, 8, 32, 31, 31, 31, 31, 3, 3)]
        + [dma((4, 3)), dma((4, 3)), dma((2, 3)), dma((2,))],
        compiler_params=pltpu.CompilerParams(
            collective_id=2, has_side_effects=True, vmem_limit_bytes=VMEM_LIMIT
        ),
        name="finish",
    )(
        dkv, dq.reshape(YG, LH * HEAD_DIM, tall), hid_all, wqkv, gfs,
        dup.reshape(FS, slim, share), ddn.reshape(8, deep, width), dwo.reshape(8, slim, width), vp,
    )

    kv_grad = qkvg[:, :, : LH * 128].reshape(SP, slim, LH, 2, HEAD_DIM)
    q_grad = qkvg[:, :, LH * 128 :].reshape(SP, slim, LH, 1, HEAD_DIM)
    qkv_grad = jnp.concatenate((q_grad, kv_grad), axis=3)
    qkv_grad = jnp.transpose(qkv_grad, (1, 3, 0, 2, 4)).reshape(slim, -1).astype(F32)
    return (
        result,
        input_grad,
        qkv_grad,
        qvg[0, :slim],
        qvg[1, :slim],
        outg,
        vecg[0, :slim],
        vecg[1, :slim],
        vecg[2, :slim],
        upg,
        vecg[8, :deep],
        dng,
        vecg[3, :slim],
        vecg[4, :slim],
        vecg[5, :slim],
    )


def solution(mesh):
    placed = (
        P(("fsdp", "sp"), None),
        P("fsdp", None),
        P("fsdp"),
        P("fsdp"),
        P("fsdp", None),
        P("fsdp"),
        P("fsdp"),
        P("fsdp"),
        P("fsdp", None),
        P("fsdp"),
        P("fsdp", None),
        P("fsdp"),
        P("fsdp"),
        P("fsdp"),
        P(),
        P(("fsdp", "sp"), None),
    )
    return jax.shard_map(
        on_device,
        mesh=mesh,
        in_specs=placed,
        out_specs=(
            P(("fsdp", "sp"), None),
            P(("fsdp", "sp"), None),
            P("fsdp", None),
            P("fsdp"),
            P("fsdp"),
            P("fsdp", None),
            P("fsdp"),
            P("fsdp"),
            P("fsdp"),
            P("fsdp", None),
            P("fsdp"),
            P("fsdp", None),
            P("fsdp"),
            P("fsdp"),
            P("fsdp"),
        ),
        check_vma=False,
    )
```

time: 2190 us -> 533 us (0.24)
  waiting for transfers between devices: 1250 us -> 0 us
  Pallas kernels: 0 us -> 511 us
  blocking collectives: 382 us -> 0 us
  matrix products: 299 us -> 0 us
  local copies, waits for them, and re-layouts: 122 us -> 14.7 us
  other arithmetic: 98.5 us -> 0.79 us
    reduce_scatter x4 -> x0, waiting for transfers between devices: 923 us -> none  [the longest x1 247 us: on_device(): lax.psum_scatter(terms.astype(jnp.bfloat16), 'fsdp', scatter_dimension=0,...]
    pallas_call x0 -> x5, Pallas kernels: none -> 511 us  [the longest x1 155 us: on_device(): pl.pallas_call(project_kernel, out_shape=(shape((tall, width), BF), shape...]
    unnamed x2 -> x0, blocking collectives: 309 us -> none
    dot_general x124 -> x0, matrix products: 299 us -> none  [the longest x32 72.1 us: block_scores(): jnp.einsum('rhd,khd->hrk', query_rows, key_block, preferred_element_type=...]
    all_gather x6 -> x0, waiting for transfers between devices: 252 us -> none  [the longest x1 99.5 us: on_device(): lax.all_gather(key_rows, 'fsdp', axis=0, tiled=True)]
    all_to_all x2 -> x0, blocking collectives: 58.6 us -> none  [the longest x1 39.5 us: on_device(): lax.all_to_all(packed, 'sp', split_axis=2, concat_axis=0, tiled=True)]
    unnamed x13 -> x0, waiting for transfers between devices: 50.8 us -> none
    and x32 -> x0, other arithmetic: 41.8 us -> none  [block_scores(): allowed = (key_seq == query_seq) & (places - key_seq * seq_len < limits)]
  transfers between devices with their start and end apart: 14 -> 0, of which waited for: 11 -> 0; matrix products, arithmetic and copies ran while one was open for 11% -> 0% of each run, Pallas kernels for 0% -> 0%
where the time goes in v1:
time: 533 us; the launch traced here: 528 us
  Pallas kernels  511 us (96%)
  local copies, waits for them, and re-layouts  14.7 us (3%)
    pallas_call x1, Pallas kernels, on_device(): pl.pallas_call(project_kernel, out_shape=(shape((tall, width), BF), shape...  155 us
    pallas_call x1, Pallas kernels, on_device(): pl.pallas_call(finish_kernel, out_shape=(shape((rows, width), F32), shape...  131 us
    pallas_call x1, Pallas kernels, on_device(): pl.pallas_call(middle_kernel, out_shape=(shape((rows, width), BF), shape(...  107 us
    pallas_call x1, Pallas kernels, on_device(): pl.pallas_call(attend_back_kernel, grid=(LH, XG), out_shape=(shape((XG, L...  74.2 us
    pallas_call x1, Pallas kernels, on_device(): pl.pallas_call(attend_kernel, grid=(LH, YG), out_shape=shape((YG, LH, tal...  42.8 us

profile of v1, /device:TPU:1, one launch (start us, length us, event | category | flops | bytes accessed | tf_op | source)
XLA Modules:
  0.0 527.6 jit_solution(16896238102118004137)
XLA Ops:
  0.6 0.0 copy-start
  1.4 0.8 stack.39
  2.2 0.8 dynamic_update_slice.3.small
  3.0 0.0 copy-done
  3.0 0.0 copy-start.6
  3.0 0.6 constant_dynamic-slice_fusion.up
  3.6 1.1 reshape.69
  4.9 0.1 reshape.70
  5.0 0.1 reshape_squeeze.3
  5.1 0.6 pad_maximum_fusion.1.wq
  5.7 155.0 %project.1 = (bf16[512,768]{1,0:T(8,128)(2,1)}, bf16[768,576]{1,0:T(8,128)(2,1)}, bf16[4,3,512,128]{3,2,1,0:T(8,128)(2,1)}, bf16[8,3,512,128]{3,2,1,0:T(8,128)(2...) custom-call(bf16[128,768]{1,0:T(8,128)(2,1)} %hid.3, ...), custom_call_target="tpu_custom_call" | custom-call | tf_op jit(solution)/shard_map/project/pallas_call | solution.py:834
  160.7 1.8 pad.9
  162.6 42.8 %attend.1.o_part = bf16[4,3,512,128]{3,2,1,0:T(8,128)(2,1)} custom-call(s32[1]{0:T(128)S(6)} %copy.53.valid, bf16[4,3,512,128]{3,2,1,0:T(8,128)(2,1)} %get-tuple-element.40.q, bf16[8,3,512,128]{3,2,1,0:T(8,128)(2,1)} %get-tuple-element.41.kv), custom_call_target="tpu_custom_call" | custom-call | tf_op jit(solution)/shard_map/attend/pallas_call | solution.py:864
  205.3 107.4 %middle.1 = (bf16[128,768]{1,0:T(8,128)(2,1)}, f32[128,768]{1,0:T(8,128)}, bf16[4,3,512,128]{3,2,1,0:T(8,128)(2,1)}, f32[4,8,512]{2,1,0:T(8,128)}, bf16[768,768]...) custom-call(bf16[4,3,512,128]{3,2,1,0:T(8,128)(2,1)} %attend.1.o_part, ...), custom_call_target="tpu_custom_call" | custom-call | tf_op jit(solution)/shard_map/middle/pallas_call | solution.py:880
  312.7 74.2 %attend_back.1 = (bf16[8,3,512,128]{3,2,1,0:T(8,128)(2,1)}, bf16[4,3,64,512]{3,2,1,0:T(8,128)(2,1)}) custom-call(s32[1]{0:T(128)S(6)} %copy.53.valid, bf16[4,3,512,128]{3,2,1,0:T(8,128)(2,1)} %get-tuple-element.40.q, bf16[4,3,512,128]{3,2,1,0:T(8,128)(2,1)} %get-tuple-element.47.dout, f32[4,8,512]{2,1,0:T(8,128)} %get-tuple-element.48.ld, ...), custom_call_target="tpu_custom_call" | custom-call | tf_op jit(solution)/shard_map/attend_back/pallas_call | solution.py:927
  386.9 131.3 %finish.1 = (f32[128,768]{1,0:T(8,128)}, bf16[4,24,576]{2,1,0:T(8,128)(2,1)}, f32[24,3072]{1,0:T(8,128)}, f32[96,768]{1,0:T(8,128)}, f32[24,768]{1,0:T(8,128)}, /*index=5*/f32[16,128]{1,0:T(8,128)}, f32[8,128]{1,0:T(8,128)}) custom-call(bf16[8,3,512,128]{3,2,1,0:T(8,128)(2,1)} %get-tuple-element.49.dkv, bf16[4,192,512]{2,1,0:T(8,128)(2,1)} %bitcast.51, ...), custom_call_target="tpu_custom_call" | custom-call | tf_op jit(solution)/shard_map/finish/pallas_call | solution.py:947
  518.2 1.3 slice_bitcast_fusion.5
  519.4 1.4 slice_bitcast_fusion.2
  520.9 0.8 slice.45
  521.7 0.9 slice.46
  522.6 0.1 reshape.79
  522.7 0.1 reshape.80
  522.8 0.0 copy-start.5
  522.8 0.1 copy.42
  522.9 0.2 convert_bitcast_fusion
  523.0 1.1 reshape.81
  524.1 0.7 copy.54
  524.8 0.7 copy.55
  525.5 0.6 copy.56
  526.2 0.0 copy-done.3
  526.2 0.7 copy.57
  526.9 0.7 copy.58
  (16 shorter events, 0.1 us)
Async XLA Ops:
  0.6 2.3 copy-start
  3.0 2.7 copy-start.6
  518.1 6.0 %copy-start.4 = (bf16[128,768]{1,0:T(8,128)(2,1)S(1)}, bf16[128,768]{1,0:T(8,128)(2,1)}, u32[]{:S(2)}) copy-start(bf16[128,768]{1,0:T(8,128)(2,1)} %get-tuple-element.93) | copy-start | bytes 589828
  518.2 6.6 %copy-start.1 = (f32[128,768]{1,0:T(8,128)S(1)}, f32[128,768]{1,0:T(8,128)}, u32[]{:S(2)}) copy-start(f32[128,768]{1,0:T(8,128)} %get-tuple-element.94) | copy-start | bytes 1179652
  522.8 2.7 copy-start.5
  522.9 3.3 copy-start.3
  523.0 3.8 copy-start.2

commit v2 on v1

--- a/solution.py
+++ b/solution.py
@@ -84,20 +84,24 @@
     barrier = pltpu.get_barrier_semaphore()
     loop(1, FS, lambda d: greet(barrier, fsdp=lax.rem(f + d, FS)))
     loop(1, SP, lambda d: greet(barrier, sp=lax.rem(s + d, SP)))
-    pl.semaphore_wait(barrier, FS - 1 + SP - 1)
-
-
-def project_kernel(
-    hid, wq, up, down, out, small,
-    hid_all, wqkv, q_all, kv_all, up_g, down_g, out_g, vecs,
-    wq_g, small_g, wf, q_st, kv_st, qvb,
+
+    @pl.when(s != f // 8)
+    def _():
+        loop(0, 8, lambda t: greet(barrier, fsdp=8 * s + t, sp=f // 8))
+
+    pl.semaphore_wait(barrier, FS - 1 + SP - 1 + jnp.where(s != f // 8, 8, 0))
+
+
+def forward_kernel(
+    valid, hid, wq, up, down, out, small,
+    hid_all, wqkv, q_all, kv_all, o_all, up_g, down_g, out_g, vecs,
+    wq_g, small_g, wf, q_st, kv_st, qvb, state, o_st,
     hid_s, hid_r, wq_s, wq_r, up_s, up_r, dn_s, dn_r, ou_s, ou_r, sm_s, sm_r,
-    q_s, q_r, kv_s, kv_r, loc,
+    q_s, q_r, kv_s, kv_r, o_s, o_r, loc,
 ):
     s = lax.axis_index("sp")
     f = lax.axis_index("fsdp")
     i, j = f // YG, lax.rem(f, YG)
-    owner = s == f // 8
     greet_all(f, s)
     rows = hid.shape[0]
 
@@ -114,13 +118,23 @@
     small_copy = fs_copy(small, small_g, sm_s, sm_r)
     up_copy = fs_copy(up, up_g, up_s, up_r)
 
-    def down_copy(d):
+    def owned_copies(t):
         k = lax.rem(f, 8)
-        return remote(down, down_g.at[k], dn_s.at[d - 1], dn_r.at[k], fsdp=lax.rem(f + d, FS))
-
-    def out_copy(d):
-        k = lax.rem(f, 8)
-        return remote(out, out_g.at[k], ou_s.at[d - 1], ou_r.at[k], fsdp=lax.rem(f + d, FS))
+        to = {"fsdp": 8 * s + t, "sp": f // 8}
+        return (
+            remote(down, down_g.at[k], dn_s.at[t], dn_r.at[k], **to),
+            remote(out, out_g.at[k], ou_s.at[t], ou_r.at[k], **to),
+        )
+
+    def owned_arrivals(k):
+        to = {"fsdp": 8 * s + k, "sp": f // 8}
+        return (
+            remote(down, down_g.at[k], dn_s.at[k], dn_r.at[k], **to),
+            remote(out, out_g.at[k], ou_s.at[k], ou_r.at[k], **to),
+        )
+
+    def is_self(t):
+        return (s == f // 8) & (8 * s + t == f)
 
     loop(1, SP, lambda d: hid_copy(d).start())
 
@@ -203,88 +217,134 @@
 
     loop(1, XG, lambda d: kv_copy(d).start())
     loop(1, YG, lambda d: q_copy(d).start())
-    kv_own = pltpu.make_async_copy(kv_st, kv_all.at[i], loc.at[1])
-    q_own = pltpu.make_async_copy(q_st, q_all.at[j], loc.at[2])
-    kv_own.start()
-    q_own.start()
+    kv_all[i] = kv_st[...]
+    q_all[j] = q_st[...]
+
+    tall = SP * rows
+    half = tall // 2
+    key_place = lax.broadcasted_iota(jnp.int32, (1, tall), 1)
+    lanes = lax.broadcasted_iota(jnp.int32, (half, 128), 1)
+
+    def o_copy(d, h):
+        to = lax.rem(j + YG - d, YG)
+        src = o_st.at[to, h]
+        return remote(src, o_all.at[j, h], o_s.at[d - 1, h], o_r.at[d - 1, h], fsdp=i * YG + to)
+
+    def attend(step, is_first, is_last):
+        places = [lax.rem(i + XG - 2 * step - c, XG) for c in range(2)]
+        limits = [
+            jnp.where((at * YG + j) * tall + key_place < valid[0], 0.0, masked) for at in places
+        ]
+
+        def tile(t):
+            d = t // LH
+            h = lax.rem(t, LH)
+            n = lax.rem(j + YG - d, YG)
+            if is_first:
+
+                @pl.when((d > 0) & (h == 0))
+                def _():
+                    q_copy(d).wait_recv()
+
+            for r in range(2):
+                at = pl.ds(r * half, half)
+                query = q_all[n, h, at, :]
+                blocks = [kv_all[p, h] for p in places]
+                scores = [dot_nt(query, block) + limit for block, limit in zip(blocks, limits)]
+                tops = [jnp.max(score, axis=1, keepdims=True) for score in scores]
+                top = jnp.maximum(tops[0], tops[1])
+                if not is_first:
+                    old = state[n, h, at, :]
+                    before = old[:, 0:1]
+                    top = jnp.maximum(top, before)
+                probs = [jnp.exp(score - top) for score in scores]
+                total = functools.reduce(
+                    jnp.add, [jnp.sum(p, axis=1, keepdims=True) for p in probs]
+                )
+                weighted = functools.reduce(
+                    jnp.add, [dot_nn(p.astype(BF), block) for p, block in zip(probs, blocks)]
+                )
+                if not is_first:
+                    decay = jnp.exp(before - top)
+                    total = total + decay * old[:, 32:33]
+                    weighted = weighted + decay * old
+                if is_last:
+                    log_sum = top + jnp.log(total)
+                    high = log_sum.astype(BF).astype(F32)
+                    logs = jnp.where(lanes < 32, high, log_sum - high)
+                    o_st[n, h, at, :] = jnp.where(lanes >= 64, weighted / total, logs).astype(BF)
+                else:
+                    logs = jnp.where(lanes < 32, top, total)
+                    state[n, h, at, :] = jnp.where(lanes >= 64, weighted, logs)
+            if is_last:
+
+                @pl.when(d > 0)
+                def _():
+                    o_copy(d, h).start()
+
+                @pl.when(d == 0)
+                def _():
+                    o_all[j, h] = o_st[j, h]
+
+        if is_last:
+            loop(LH, LH * YG, tile)
+            loop(0, LH, tile)
+        else:
+            loop(0, LH * YG, tile)
+
+    kv_copy(1).wait_recv()
+    attend(0, True, False)
     loop(1, FS, lambda d: up_copy(d).start())
 
-    @pl.when(owner)
+    def send_owned(t):
+        @pl.when(jnp.logical_not(is_self(t)))
+        def _():
+            for copy in owned_copies(t):
+                copy.start()
+
+    loop(0, 8, send_owned)
+
+    @pl.when(s == f // 8)
     def _():
-        def both(d):
-            down_copy(d).start()
-            out_copy(d).start()
-
-        loop(1, FS, both)
-        dn_own = pltpu.make_async_copy(down, down_g.at[lax.rem(f, 8)], loc.at[3])
-        ou_own = pltpu.make_async_copy(out, out_g.at[lax.rem(f, 8)], loc.at[4])
+        dn_own = pltpu.make_async_copy(down, down_g.at[lax.rem(f, 8)], loc.at[1])
+        ou_own = pltpu.make_async_copy(out, out_g.at[lax.rem(f, 8)], loc.at[2])
         dn_own.start()
         ou_own.start()
         dn_own.wait()
         ou_own.wait()
 
-    kv_own.wait()
-    q_own.wait()
+    def middle_pass(step):
+        kv_copy(2 * step).wait_recv()
+        kv_copy(2 * step + 1).wait_recv()
+        attend(step, False, False)
+
+    loop(1, XG // 2 - 1, middle_pass)
+    kv_copy(XG - 2).wait_recv()
+    kv_copy(XG - 1).wait_recv()
+    attend(XG // 2 - 1, False, True)
+
     up_own.wait()
-    loop(1, XG, lambda d: kv_copy(d).wait())
-    loop(1, YG, lambda d: q_copy(d).wait())
+    loop(1, XG, lambda d: kv_copy(d).wait_send())
+    loop(1, YG, lambda d: q_copy(d).wait_send())
     loop(1, FS, lambda d: up_copy(d).wait())
 
-    @pl.when(owner)
-    def _():
-        def both(d):
-            down_copy(d).wait_send()
-            out_copy(d).wait_send()
-
-        loop(1, FS, both)
-
-    def arrivals(k):
-        @pl.when(8 * s + k != f)
+    def owned_wait(t):
+        @pl.when(jnp.logical_not(is_self(t)))
         def _():
-            other = lax.rem(f + 1, FS)
-            remote(down, down_g.at[k], dn_s.at[0], dn_r.at[k], fsdp=other).wait_recv()
-            remote(out, out_g.at[k], ou_s.at[0], ou_r.at[k], fsdp=other).wait_recv()
-
-    loop(0, 8, arrivals)
-
-
-def attend_kernel(valid, q, kv, o):
-    rows = q.shape[2]
-    keys = kv.shape[2]
-    f = lax.axis_index("fsdp")
-    first_key = ((XG - 1) * YG + lax.rem(f, YG)) * keys
-    query = q[0, 0]
-    m = l = acc = None
-    for c in range(XG):
-        block = kv[c, 0]
-        scores = dot_nt(query, block)
-        if c == XG - 1:
-            place = first_key + lax.broadcasted_iota(jnp.int32, (1, keys), 1)
-            scores = jnp.where(place < valid[0], scores, masked)
-        top = jnp.max(scores, axis=1, keepdims=True)
-        new = top if c == 0 else jnp.maximum(m, top)
-        p = jnp.exp(scores - new)
-        part = jnp.sum(p, axis=1, keepdims=True)
-        weighted = dot_nn(p.astype(BF), block)
-        if c == 0:
-            l, acc = part, weighted
-        else:
-            decay = jnp.exp(m - new)
-            l = l * decay + part
-            acc = acc * decay + weighted
-        m = new
-    log_sum = m + jnp.log(l)
-    high = log_sum.astype(BF).astype(F32)
-    lane = lax.broadcasted_iota(jnp.int32, (rows, 128), 1)
-    result = jnp.where(lane >= 64, acc / l, jnp.where(lane < 32, high, log_sum - high))
-    o[0, 0] = result.astype(BF)
+            for copy in owned_copies(t):
+                copy.wait_send()
+            for copy in owned_arrivals(t):
+                copy.wait_recv()
+
+    loop(0, 8, owned_wait)
+    loop(1, YG, lambda d: loop(0, LH, lambda h: o_copy(d, h).wait()))
 
 
 def middle_kernel(
-    o_part, wo, wup, wdn, vecs, hid, cot,
+    o_all, wo, wup, wdn, vecs, hid, cot,
     result, gfs, d_all, ld_all, dup, ddn, dwo, vp,
-    o_rb, att, ld, st, own, first, n1, inv1, x_all, act, deriv, gd, gp, gb, gsec, rb, dbuf, ldrow, vg,
-    o_s, o_r, ag_s, ag_r, rs_s, rs_r, d_s, d_r, l_s, l_r, loc,
+    att, ld, st, own, first, n1, inv1, x_all, act, deriv, gd, gp, gb, gsec, rb, dbuf, ldrow, vg,
+    ag_s, ag_r, rs_s, rs_r, d_s, d_r, l_s, l_r, loc,
 ):
     s = lax.axis_index("sp")
     f = lax.axis_index("fsdp")
@@ -299,13 +359,6 @@
     def y_peer(d):
         return i * YG + lax.rem(j + d, YG)
 
-    def o_copy(d):
-        src = o_part.at[lax.rem(j + d, YG)]
-        return remote(src, o_rb.at[d - 1], o_s.at[d - 1], o_r.at[d - 1], fsdp=y_peer(d))
-
-    loop(1, YG, lambda d: o_copy(d).start())
-    loop(1, YG, lambda d: o_copy(d).wait())
-
     def span(b):
         return pl.ds(pl.multiple_of(b * rows, rows), rows)
 
@@ -315,8 +368,7 @@
         at = span(b)
         sums = jnp.zeros((rows, 128), F32)
         for h in range(LH):
-            parts = [o_part[j, h, at, :].astype(F32)]
-            parts += [o_rb[d, h, at, :].astype(F32) for d in range(YG - 1)]
+            parts = [o_all[d, h, at, :].astype(F32) for d in range(YG)]
             logs = [p[:, 0:1] + p[:, 32:33] for p in parts]
             top = functools.reduce(jnp.maximum, logs)
             weights = [jnp.exp(g - top) for g in logs]
@@ -459,18 +511,20 @@
             product = part.astype(F32) * att[at, 128 * h : 128 * h + 128].astype(F32)
             sums = jnp.where(lane == 2 * h + 1, jnp.sum(product, axis=1, keepdims=True), sums)
         ld[at, :] = sums
+        loop(1, YG, lambda n: d_copy(n, d).start())
+
+    def d_copy(n, d):
+        at = span(lax.rem(s + SP - d, SP))
+        sems = (d_s.at[n - 1, d], d_r.at[n - 1, d])
+        return remote(dbuf.at[:, at], d_all.at[j, :, at], *sems, fsdp=y_peer(n))
 
     loop(0, SP, branch)
     loop(1, SP, lambda d: gather(2, gb)(d).wait_send())
     ldrow[...] = jnp.transpose(ld[...], (1, 0))[0:8, :]
 
-    def d_copy(d):
-        return remote(dbuf, d_all.at[j], d_s.at[d - 1], d_r.at[d - 1], fsdp=y_peer(d))
-
     def l_copy(d):
         return remote(ldrow, ld_all.at[j], l_s.at[d - 1], l_r.at[d - 1], fsdp=y_peer(d))
 
-    loop(1, YG, lambda d: d_copy(d).start())
     loop(1, YG, lambda d: l_copy(d).start())
     d_own = pltpu.make_async_copy(dbuf, d_all.at[j], loc.at[0])
     l_own = pltpu.make_async_copy(ldrow, ld_all.at[j], loc.at[1])
@@ -492,71 +546,28 @@
         vp[8 * s + k, 8:16, :] = jnp.where(lane8 < 96, piece[:, 0:128], 0.0)
     d_own.wait()
     l_own.wait()
-    loop(1, YG, lambda d: d_copy(d).wait())
+    loop(1, YG, lambda n: loop(0, SP, lambda d: d_copy(n, d).wait()))
     loop(1, YG, lambda d: l_copy(d).wait())
 
 
-def attend_back_kernel(valid, q, dout, ld, kv, dkv, dq, acc):
-    h = pl.program_id(0)
-    step = pl.program_id(1)
-    keys = kv.shape[2]
-    f = lax.axis_index("fsdp")
-    first_key = (step * YG + lax.rem(f, YG)) * keys
-
-    @pl.when(step == 0)
-    def _():
-        acc[...] = jnp.zeros(acc.shape, F32)
-
-    def work(last):
-        block = kv[0, 0]
-        flipped = jnp.transpose(block.astype(F32), (1, 0))[0:HEAD_DIM].astype(BF)
-        total = None
-        for n in range(YG):
-            query = q[n, 0]
-            grad = dout[n, 0]
-            log_sum = ld[n, pl.ds(2 * h, 1), :]
-            delta = ld[n, pl.ds(2 * h + 1, 1), :]
-            scores = dot_nt(block, query)
-            if last:
-                place = first_key + lax.broadcasted_iota(jnp.int32, (keys, 1), 0)
-                scores = jnp.where(place < valid[0], scores, masked)
-            p = jnp.exp(scores - log_sum)
-            grad_p = dot_nt(block, grad)
-            grad_s = (p * (grad_p - delta)).astype(BF)
-            terms = dot_nn(grad_s, query) + dot_nn(p.astype(BF), grad)
-            total = terms if n == 0 else total + terms
-            acc[n] = acc[n] + dot_nn(flipped, grad_s)
-        dkv[0, 0] = total.astype(BF)
-
-    @pl.when(step < XG - 1)
-    def _():
-        work(False)
-
-    @pl.when(step == XG - 1)
-    def _():
-        work(True)
-        dq[:, 0] = acc[...].astype(BF)
-
-
-def finish_kernel(
-    dkv, dq, hid_all, wqkv, gfs, dup, ddn, dwo, vp,
+def backward_kernel(
+    valid, q_all, d_all, ld, kv_all, hid_all, wqkv, gfs, dup, ddn, dwo, vp,
     input_grad, qkvg, upg, dng, outg, vecg, qvg,
-    kv_rb, q_rb, g, wf, wp, bp, st, own, rb, wq_rb, up_rb, dn_rb, ou_rb, vp_rb, bp_rb,
+    acc, dq, dkv, kv_rb, q_rb, g, wf, wp, bp, st, own, rb, wq_rb, up_rb, dn_rb, ou_rb, vp_rb, bp_rb,
     up_fin, dn_fin, ou_fin, v_fin, qv_fin,
     kv_s, kv_r, q_s, q_r, wq_s, wq_r, up_s, up_r, dn_s, dn_r, ou_s, ou_r, vp_s, vp_r, bp_s, bp_r,
-    rs_s, rs_r, fin_s, fin_r, b_s, b_r,
+    rs_s, rs_r, fin_s, fin_r,
 ):
     s = lax.axis_index("sp")
     f = lax.axis_index("fsdp")
     i, j = f // YG, lax.rem(f, YG)
     rows = gfs.shape[0]
     tall = SP * rows
-    owner = s == f // 8
     greet_all(f, s)
 
     def kv_copy(d):
         to = lax.rem(i + d, XG)
-        return remote(dkv.at[to], kv_rb.at[d - 1], kv_s.at[d - 1], kv_r.at[d - 1], fsdp=to * YG + j)
+        return remote(dkv.at[d - 1], kv_rb.at[d - 1], kv_s.at[d - 1], kv_r.at[d - 1], fsdp=to * YG + j)
 
     def q_copy(d):
         to = lax.rem(j + d, YG)
@@ -575,14 +586,22 @@
     bp_copy = fs_copy(bp, bp_rb, bp_s, bp_r)
 
     def owner_copies(k):
-        to = 8 * s + k
+        to = {"fsdp": 8 * s + k, "sp": f // 8}
+        n = lax.rem(f, 8)
         return (
-            remote(ddn.at[k], dn_rb.at[f], dn_s.at[k], dn_r.at[f], fsdp=to),
-            remote(dwo.at[k], ou_rb.at[f], ou_s.at[k], ou_r.at[f], fsdp=to),
+            remote(ddn.at[k], dn_rb.at[n], dn_s.at[k], dn_r.at[n], **to),
+            remote(dwo.at[k], ou_rb.at[n], ou_s.at[k], ou_r.at[n], **to),
         )
 
-    loop(1, XG, lambda d: kv_copy(d).start())
-    loop(1, YG, lambda d: q_copy(d).start())
+    def owner_arrivals(n):
+        to = {"fsdp": 8 * s + n, "sp": f // 8}
+        return (
+            remote(ddn.at[n], dn_rb.at[n], dn_s.at[n], dn_r.at[n], **to),
+            remote(dwo.at[n], ou_rb.at[n], ou_s.at[n], ou_r.at[n], **to),
+        )
+
+    def is_self(t):
+        return (s == f // 8) & (8 * s + t == f)
 
     def early(d):
         up_copy(d).start()
@@ -591,12 +610,111 @@
     loop(1, FS, early)
 
     def to_owner(k):
-        @pl.when(8 * s + k != f)
+        @pl.when(jnp.logical_not(is_self(k)))
         def _():
             for copy in owner_copies(k):
                 copy.start()
 
+        @pl.when(is_self(k))
+        def _():
+            dn_rb[k] = ddn[k]
+            ou_rb[k] = dwo[k]
+
     loop(0, 8, to_owner)
+
+    acc[...] = jnp.zeros(acc.shape, F32)
+
+    def key_step(d):
+        at = lax.rem(i + d, XG)
+        first_key = (at * YG + j) * tall
+
+        def head(h):
+            def work(last):
+                block = kv_all[at, h]
+                flipped = jnp.transpose(block.astype(F32), (1, 0))[0:HEAD_DIM].astype(BF)
+                total = None
+                for n in range(YG):
+                    query = q_all[n, h]
+                    grad = d_all[n, h]
+                    log_sum = ld[n, pl.ds(2 * h, 1), :]
+                    delta = ld[n, pl.ds(2 * h + 1, 1), :]
+                    scores = dot_nt(block, query)
+                    if last:
+                        place = first_key + lax.broadcasted_iota(jnp.int32, (tall, 1), 0)
+                        scores = jnp.where(place < valid[0], scores, masked)
+                    p = jnp.exp(scores - log_sum)
+                    grad_p = dot_nt(block, grad)
+                    grad_s = (p * (grad_p - delta)).astype(BF)
+                    terms = dot_nn(grad_s, query) + dot_nn(p.astype(BF), grad)
+                    total = terms if n == 0 else total + terms
+                    acc[n, h] = acc[n, h] + dot_nn(flipped, grad_s)
+                dkv[d - 1, h] = total.astype(BF)
+
+            @pl.when(at < XG - 1)
+            def _():
+                work(False)
+
+            @pl.when(at == XG - 1)
+            def _():
+                work(True)
+
+        loop(0, LH, head)
+
+        @pl.when(d < XG)
+        def _():
+            kv_copy(d).start()
+
+    loop(1, XG + 1, key_step)
+    for n in range(YG):
+        for h in range(LH):
+            dq[n, 64 * h : 64 * h + 64, :] = acc[n, h].astype(BF)
+    loop(1, YG, lambda d: q_copy(d).start())
+
+    def late(d):
+        up_copy(d).wait()
+        vp_copy(d).wait()
+
+    loop(1, FS, late)
+
+    def add_up(buf, start):
+        def step(d, total):
+            return total + buf[d].astype(F32)
+
+        return lax.fori_loop(0, buf.shape[0], step, start)
+
+    up_fin[s] = add_up(up_rb, dup[f].astype(F32)).astype(BF)
+    v_fin[s] = add_up(vp_rb, vp[f])
+
+    def owner_wait(t):
+        @pl.when(jnp.logical_not(is_self(t)))
+        def _():
+            for copy in owner_copies(t):
+                copy.wait_send()
+            for copy in owner_arrivals(t):
+                copy.wait_recv()
+
+    loop(0, 8, owner_wait)
+
+    def down_rows(c):
+        at = pl.ds(pl.multiple_of(c * 32, 32), 32)
+        total = dn_rb[0, at, :].astype(F32)
+        for n in range(1, 8):
+            total = total + dn_rb[n, at, :].astype(F32)
+        dn_fin[s, at, :] = total.astype(BF)
+
+    loop(0, dn_fin.shape[1] // 32, down_rows)
+    ou_fin[s] = add_up(ou_rb, jnp.zeros(ou_fin.shape[1:], F32)).astype(BF)
+
+    def sp_copy(e, buf):
+        def copy(d):
+            at = buf.at[s]
+            return remote(at, at, fin_s.at[e, d - 1], fin_r.at[e, d - 1], sp=lax.rem(s + d, SP))
+
+        return copy
+
+    early_bufs = ((0, up_fin), (1, v_fin), (4, dn_fin), (5, ou_fin))
+    for e, buf in early_bufs:
+        loop(1, SP, lambda d: sp_copy(e, buf)(d).start())
 
     loop(1, XG, lambda d: kv_copy(d).wait())
     loop(1, YG, lambda d: q_copy(d).wait())
@@ -607,7 +725,7 @@
     def sum_keys(b):
         at = span(b)
         for h in range(LH):
-            total = dkv[i, h, at, :].astype(F32)
+            total = dkv[XG - 1, h, at, :].astype(F32)
             for d in range(XG - 1):
                 total = total + kv_rb[d, h, at, :].astype(F32)
             g[at, 128 * h : 128 * h + 128] = total.astype(BF)
@@ -670,79 +788,13 @@
         bp[8 * s + k] = jnp.where(lane < 24, piece[:, 0:128], 0.0)
     loop(1, FS, lambda d: bp_copy(d).start())
 
-    def late(d):
-        up_copy(d).wait()
-        vp_copy(d).wait()
-
-    loop(1, FS, late)
-
-    def add_up(src, buf, start):
-        def step(d, total):
-            return total + buf[d].astype(F32)
-
-        return lax.fori_loop(0, FS - 1, step, start)
-
-    up_fin[s] = add_up(dup, up_rb, dup[f].astype(F32)).astype(BF)
-    v_fin[s] = add_up(vp, vp_rb, vp[f])
-
-    def sp_copy(e, buf):
-        def copy(d):
-            at = buf.at[s]
-            return remote(at, at, fin_s.at[e, d - 1], fin_r.at[e, d - 1], sp=lax.rem(s + d, SP))
-
-        return copy
-
-    loop(1, SP, lambda d: sp_copy(0, up_fin)(d).start())
-    loop(1, SP, lambda d: sp_copy(1, v_fin)(d).start())
-
-    def own_copies(d):
-        to = lax.rem(s + d, SP)
-        return (
-            remote(dn_fin, dn_fin, b_s.at[0, d - 1], b_r.at[0], sp=to),
-            remote(ou_fin, ou_fin, b_s.at[1, d - 1], b_r.at[1], sp=to),
-        )
-
-    @pl.when(owner)
-    def _():
-        def arrived(d):
-            frm = lax.rem(f + d, FS)
-            remote(ddn.at[0], dn_rb.at[frm], dn_s.at[0], dn_r.at[frm], fsdp=frm).wait_recv()
-            remote(dwo.at[0], ou_rb.at[frm], ou_s.at[0], ou_r.at[frm], fsdp=frm).wait_recv()
-
-        loop(1, FS, arrived)
-        k = lax.rem(f, 8)
-        dn_rb[f] = ddn[k]
-        ou_rb[f] = dwo[k]
-
-        def down_rows(c):
-            at = pl.ds(pl.multiple_of(c * 32, 32), 32)
-
-            def step(n, total):
-                return total + dn_rb[n, at, :].astype(F32)
-
-            start = jnp.zeros((32, dn_fin.shape[1]), F32)
-            dn_fin[at, :] = lax.fori_loop(0, FS, step, start).astype(BF)
-
-        loop(0, dn_fin.shape[0] // 32, down_rows)
-
-        def step(n, total):
-            return total + ou_rb[n].astype(F32)
-
-        ou_fin[...] = lax.fori_loop(0, FS, step, jnp.zeros(ou_fin.shape, F32)).astype(BF)
-
-        def send(d):
-            for copy in own_copies(d):
-                copy.start()
-
-        loop(1, SP, send)
-
     def later(d):
         wq_copy(d).wait()
         bp_copy(d).wait()
 
     loop(1, FS, later)
-    qkvg[s] = add_up(wp, wq_rb, wp[f].astype(F32)).astype(BF)
-    qv_fin[s] = add_up(bp, bp_rb, bp[f])
+    qkvg[s] = add_up(wq_rb, wp[f].astype(F32)).astype(BF)
+    qv_fin[s] = add_up(bp_rb, bp[f])
     loop(1, SP, lambda d: sp_copy(2, qkvg)(d).start())
     loop(1, SP, lambda d: sp_copy(3, qv_fin)(d).start())
 
@@ -752,39 +804,22 @@
         total = total + rb[d].astype(F32)
     input_grad[...] = total
 
-    loop(1, SP, lambda d: sp_copy(0, up_fin)(d).wait())
-    loop(1, SP, lambda d: sp_copy(1, v_fin)(d).wait())
+    for e, buf in early_bufs:
+        loop(1, SP, lambda d: sp_copy(e, buf)(d).wait())
     for n in range(SP):
         upg[:, 768 * n : 768 * n + 768] = up_fin[n].astype(F32)
     vecg[...] = v_fin[0] + v_fin[1] + v_fin[2] + v_fin[3]
-
-    @pl.when(owner)
-    def _():
-        def sent(d):
-            for copy in own_copies(d):
-                copy.wait_send()
-
-        loop(1, SP, sent)
-
-    @pl.when(jnp.logical_not(owner))
-    def _():
-        for copy in own_copies(1):
-            copy.wait_recv()
-
-    dng[...] = dn_fin[...].astype(F32)
-    outg[...] = ou_fin[...].astype(F32)
+    down_sum = dn_fin[0].astype(F32)
+    out_sum = ou_fin[0].astype(F32)
+    for n in range(1, SP):
+        down_sum = down_sum + dn_fin[n].astype(F32)
+        out_sum = out_sum + ou_fin[n].astype(F32)
+    dng[...] = down_sum
+    outg[...] = out_sum
 
     loop(1, SP, lambda d: sp_copy(2, qkvg)(d).wait())
     loop(1, SP, lambda d: sp_copy(3, qv_fin)(d).wait())
     qvg[...] = qv_fin[0] + qv_fin[1] + qv_fin[2] + qv_fin[3]
-
-    def sent_all(k):
-        @pl.when(8 * s + k != f)
-        def _():
-            for copy in owner_copies(k):
-                copy.wait_send()
-
-    loop(0, 8, sent_all)
 
 
 def on_device(
@@ -831,20 +866,22 @@
     small = jnp.pad(small, ((0, 8), (0, 128 - slim)))
     small = lax.dynamic_update_slice(small, up_bias[None, :], (8, 0))
 
-    hid_all, wqkv, q_all, kv_all, up_g, down_g, out_g, vecs = pl.pallas_call(
-        project_kernel,
+    smem = pl.BlockSpec(memory_space=pltpu.SMEM)
+    hid_all, wqkv, q_all, kv_all, o_all, up_g, down_g, out_g, vecs = pl.pallas_call(
+        forward_kernel,
         out_shape=(
             shape((tall, width), BF),
             shape((width, cols), BF),
             shape((YG, LH, tall, 128), BF),
             shape((XG, LH, tall, 128), BF),
+            shape((YG, LH, tall, 128), BF),
             shape((FS, slim, share), BF),
             shape((8, deep, width), BF),
             shape((8, slim, width), BF),
             shape((16, width), F32),
         ),
-        in_specs=[vmem] * 6,
-        out_specs=(vmem, vmem, hbm, hbm, hbm, hbm, hbm, vmem),
+        in_specs=[smem] + [vmem] * 6,
+        out_specs=(vmem, vmem, vmem, vmem, vmem, hbm, hbm, hbm, vmem),
         scratch_shapes=[
             pltpu.VMEM((FS, slim, cols), BF),
             pltpu.VMEM((FS, 16, 128), BF),
@@ -852,28 +889,16 @@
             pltpu.VMEM((LH, tall, 128), BF),
             pltpu.VMEM((LH, tall, 128), BF),
             pltpu.VMEM((8, width), F32),
+            pltpu.VMEM((YG, LH, tall, 128), F32),
+            pltpu.VMEM((YG, LH, tall, 128), BF),
         ]
-        + [dma((n,)) for n in (3, 3, 31, 31, 31, 31, 31, 8, 31, 8, 31, 31, 3, 3, 7, 7, 5)],
+        + [dma((n,)) for n in (3, 3, 31, 31, 31, 31, 8, 8, 8, 8, 31, 31, 3, 3, 7, 7)]
+        + [dma((3, 3)), dma((3, 3)), dma((3,))],
         compiler_params=pltpu.CompilerParams(
             collective_id=0, has_side_effects=True, vmem_limit_bytes=VMEM_LIMIT
         ),
-        name="project",
-    )(hidden_in, wq, up, down_weight, output_weight, small)
-
-    flops = 4 * LH * YG * XG * tall * tall * HEAD_DIM
-    o_part = pl.pallas_call(
-        attend_kernel,
-        grid=(LH, YG),
-        out_shape=shape((YG, LH, tall, 128), BF),
-        in_specs=[
-            pl.BlockSpec(memory_space=pltpu.SMEM),
-            pl.BlockSpec((1, 1, tall, 128), lambda h, n: (n, h, 0, 0)),
-            pl.BlockSpec((XG, 1, tall, 128), lambda h, n: (0, h, 0, 0)),
-        ],
-        out_specs=pl.BlockSpec((1, 1, tall, 128), lambda h, n: (n, h, 0, 0)),
-        compiler_params=pltpu.CompilerParams(vmem_limit_bytes=VMEM_LIMIT),
-        name="attend",
-    )(valid_length, q_all, kv_all)
+        name="forward",
+    )(valid_length, hidden_in, wq, up, down_weight, output_weight, small)
 
     wo = jnp.pad(out_g.reshape(LH, HEAD_DIM, width), ((0, 0), (HEAD_DIM, 0), (0, 0)))
     wo = wo.reshape(LH * 128, width)
@@ -892,7 +917,6 @@
         in_specs=[vmem] * 7,
         out_specs=(vmem, vmem, hbm, hbm, vmem, vmem, vmem, vmem),
         scratch_shapes=[
-            pltpu.VMEM((YG - 1, LH, tall, 128), BF),
             pltpu.VMEM((tall, LH * 128), BF),
             pltpu.VMEM((tall, 128), F32),
             pltpu.VMEM((3, tall, width), BF),
@@ -912,40 +936,19 @@
             pltpu.VMEM((8, tall), F32),
             pltpu.VMEM((8, width), F32),
         ]
-        + [dma((3,)), dma((3,))]
         + [dma((3, 3)) for _ in range(4)]
-        + [dma((n,)) for n in (3, 3, 3, 3, 2)],
+        + [dma((3, 4)), dma((3, 4)), dma((3,)), dma((3,)), dma((2,))],
         compiler_params=pltpu.CompilerParams(
             collective_id=1, has_side_effects=True, vmem_limit_bytes=VMEM_LIMIT
         ),
         name="middle",
     )(
-        o_part, wo, up_g.reshape(width, share), down_g.reshape(share, width), vecs,
+        o_all, wo, up_g.reshape(width, share), down_g.reshape(share, width), vecs,
         hidden_in, out_cotangent,
     )
 
-    dkv, dq = pl.pallas_call(
-        attend_back_kernel,
-        grid=(LH, XG),
-        out_shape=(shape((XG, LH, tall, 128), BF), shape((YG, LH, HEAD_DIM, tall), BF)),
-        in_specs=[
-            pl.BlockSpec(memory_space=pltpu.SMEM),
-            pl.BlockSpec((YG, 1, tall, 128), lambda h, n: (0, h, 0, 0)),
-            pl.BlockSpec((YG, 1, tall, 128), lambda h, n: (0, h, 0, 0)),
-            pl.BlockSpec((YG, 8, tall), lambda h, n: (0, 0, 0)),
-            pl.BlockSpec((1, 1, tall, 128), lambda h, n: (n, h, 0, 0)),
-        ],
-        out_specs=(
-            pl.BlockSpec((1, 1, tall, 128), lambda h, n: (n, h, 0, 0)),
-            pl.BlockSpec((YG, 1, HEAD_DIM, tall), lambda h, n: (0, h, 0, 0)),
-        ),
-        scratch_shapes=[pltpu.VMEM((YG, HEAD_DIM, tall), F32)],
-        compiler_params=pltpu.CompilerParams(vmem_limit_bytes=VMEM_LIMIT),
-        name="attend_back",
-    )(valid_length, q_all, d_all, ld_all, kv_all)
-
     input_grad, qkvg, upg, dng, outg, vecg, qvg = pl.pallas_call(
-        finish_kernel,
+        backward_kernel,
         out_shape=(
             shape((rows, width), F32),
             shape((SP, slim, cols), BF),
@@ -955,9 +958,12 @@
             shape((16, 128), F32),
             shape((8, 128), F32),
         ),
-        in_specs=[vmem] * 9,
+        in_specs=[smem] + [vmem] * 11,
         out_specs=(vmem,) * 7,
         scratch_shapes=[
+            pltpu.VMEM((YG, LH, HEAD_DIM, tall), F32),
+            pltpu.VMEM((YG, LH * HEAD_DIM, tall), BF),
+            pltpu.VMEM((XG, LH, tall, 128), BF),
             pltpu.VMEM((XG - 1, LH, tall, 128), BF),
             pltpu.VMEM((YG - 1, LH * HEAD_DIM, tall), BF),
             pltpu.VMEM((tall, cols), BF),
@@ -969,24 +975,24 @@
             pltpu.VMEM((SP - 1, rows, width), BF),
             pltpu.VMEM((FS - 1, slim, cols), BF),
             pltpu.VMEM((FS - 1, slim, share), BF),
-            pltpu.VMEM((FS, deep, width), BF),
-            pltpu.VMEM((FS, slim, width), BF),
+            pltpu.VMEM((8, deep, width), BF),
+            pltpu.VMEM((8, slim, width), BF),
             pltpu.VMEM((FS - 1, 16, 128), F32),
             pltpu.VMEM((FS - 1, 8, 128), F32),
             pltpu.VMEM((SP, slim, share), BF),
-            pltpu.VMEM((deep, width), BF),
-            pltpu.VMEM((slim, width), BF),
+            pltpu.VMEM((SP, deep, width), BF),
+            pltpu.VMEM((SP, slim, width), BF),
             pltpu.VMEM((SP, 16, 128), F32),
             pltpu.VMEM((SP, 8, 128), F32),
         ]
-        + [dma((n,)) for n in (7, 7, 3, 3, 31, 31, 31, 31, 8, 32, 8, 32, 31, 31, 31, 31, 3, 3)]
-        + [dma((4, 3)), dma((4, 3)), dma((2, 3)), dma((2,))],
+        + [dma((n,)) for n in (7, 7, 3, 3, 31, 31, 31, 31, 8, 8, 8, 8, 31, 31, 31, 31, 3, 3)]
+        + [dma((6, 3)), dma((6, 3))],
         compiler_params=pltpu.CompilerParams(
             collective_id=2, has_side_effects=True, vmem_limit_bytes=VMEM_LIMIT
         ),
-        name="finish",
+        name="backward",
     )(
-        dkv, dq.reshape(YG, LH * HEAD_DIM, tall), hid_all, wqkv, gfs,
+        valid_length, q_all, d_all, ld_all, kv_all, hid_all, wqkv, gfs,
         dup.reshape(FS, slim, share), ddn.reshape(8, deep, width), dwo.reshape(8, slim, width), vp,
     )
 

time: 533 us -> 385 us (0.72)
  Pallas kernels: 511 us -> 366 us
    pallas_call x4 -> x2, Pallas kernels: 403 us -> 278 us  [the longest x1 147 us: on_device(): pl.pallas_call(backward_kernel, out_shape=(shape((rows, width), F32), sha...]
    pallas_call x1, Pallas kernels: 107 us -> 87.3 us  [on_device(): pl.pallas_call(middle_kernel, out_shape=(shape((rows, width), BF), shape(...]
where the time goes in v2:
time: 385 us; the launch traced here: 383 us
  Pallas kernels  366 us (95%)
  local copies, waits for them, and re-layouts  14.7 us (4%)
    pallas_call x1, Pallas kernels, on_device(): pl.pallas_call(backward_kernel, out_shape=(shape((rows, width), F32), sha...  147 us
    pallas_call x1, Pallas kernels, on_device(): pl.pallas_call(forward_kernel, out_shape=(shape((tall, width), BF), shape...  131 us
    pallas_call x1, Pallas kernels, on_device(): pl.pallas_call(middle_kernel, out_shape=(shape((rows, width), BF), shape(...  87.3 us

profile of v2, /device:TPU:1, one launch (start us, length us, event | category | flops | bytes accessed | tf_op | source)
XLA Modules:
  0.0 382.5 jit_solution(16387307389005243330)
XLA Ops:
  0.6 0.0 copy-start
  1.4 0.8 stack.39
  2.2 0.8 dynamic_update_slice.3.small
  3.0 0.0 copy-start.6
  3.0 0.6 constant_dynamic-slice_fusion.up
  3.6 1.1 reshape.66
  4.9 0.1 reshape.67
  5.0 0.1 reshape_squeeze.3
  5.1 0.6 pad_maximum_fusion.1.wq
  5.7 0.0 copy-done.6
  5.7 131.2 %forward.1 = (bf16[512,768]{1,0:T(8,128)(2,1)}, bf16[768,576]{1,0:T(8,128)(2,1)}, bf16[4,3,512,128]{3,2,1,0:T(8,128)(2,1)}, bf16[8,3,512,128]{3,2,1,0:T(8,128)(2...) custom-call(s32[1]{0:T(128)S(6)} %copy.53.valid, ...), custom_call_target="tpu_custom_call" | custom-call | tf_op jit(solution)/shard_map/forward/pallas_call | solution.py:870
  136.9 1.8 pad.9
  138.7 87.3 %middle.1 = (bf16[128,768]{1,0:T(8,128)(2,1)}, f32[128,768]{1,0:T(8,128)}, bf16[4,3,512,128]{3,2,1,0:T(8,128)(2,1)}, f32[4,8,512]{2,1,0:T(8,128)}, bf16[768,768]...) custom-call(bf16[4,3,512,128]{3,2,1,0:T(8,128)(2,1)} %get-tuple-element.39.o_all, ...), custom_call_target="tpu_custom_call" | custom-call | tf_op jit(solution)/shard_map/middle/pallas_call | solution.py:905
  226.0 147.1 %backward.1 = (f32[128,768]{1,0:T(8,128)}, bf16[4,24,576]{2,1,0:T(8,128)(2,1)}, f32[24,3072]{1,0:T(8,128)}, f32[96,768]{1,0:T(8,128)}, f32[24,768]{1,0:T(8,128)}, /*index=5*/f32[16,128]{1,0:T(8,128)}, f32[8,128]{1,0:T(8,128)}) custom-call(s32[1]{0:T(128)S(6)} %copy.53.valid, bf16[4,3,512,128]{3,2,1,0:T(8,128)(2,1)} %get-tuple-element.45.q_all, ...), custom_call_target="tpu_custom_call" | custom-call | tf_op jit(solution)/shard_map/backward/pallas_call | solution.py:950
  373.1 0.0 copy-start.4
  373.1 0.0 copy-start.1
  373.1 1.2 slice_bitcast_fusion.5
  374.4 1.4 slice_bitcast_fusion.2
  375.8 0.8 slice.45
  376.6 0.9 slice.46
  377.5 0.1 reshape.75
  377.6 0.1 reshape.76
  377.7 0.1 copy.42
  377.8 0.2 convert_bitcast_fusion
  378.0 0.0 copy-start.2
  378.0 1.1 reshape.77
  379.0 0.0 copy-done.4
  379.0 0.7 copy.54
  379.7 0.7 copy.55
  380.5 0.6 copy.56
  381.1 0.7 copy.57
  381.8 0.7 copy.58
  (14 shorter events, 0.1 us)
Async XLA Ops:
  0.6 2.3 copy-start
  3.0 2.7 copy-start.6
  373.1 6.0 %copy-start.4 = (bf16[128,768]{1,0:T(8,128)(2,1)S(1)}, bf16[128,768]{1,0:T(8,128)(2,1)}, u32[]{:S(2)}) copy-start(bf16[128,768]{1,0:T(8,128)(2,1)} %get-tuple-element.91) | copy-start | bytes 589828
  373.1 6.6 %copy-start.1 = (f32[128,768]{1,0:T(8,128)S(1)}, f32[128,768]{1,0:T(8,128)}, u32[]{:S(2)}) copy-start(f32[128,768]{1,0:T(8,128)} %get-tuple-element.92) | copy-start | bytes 1179652
  377.7 2.7 copy-start.5
  377.8 3.3 copy-start.3
  378.0 3.8 %copy-start.2 = (f32[96,768]{1,0:T(8,128)S(1)}, f32[96,768]{1,0:T(8,128)}, u32[]{:S(2)}) copy-start(f32[96,768]{1,0:T(8,128)} %get-tuple-element.102) | copy-start | bytes 884740

commit v3 on v2

--- a/solution.py
+++ b/solution.py
@@ -14,6 +14,9 @@
 YG = 4
 XG = 8
 LH = HEADS // SP
+
+KEY_STEPS = ((0, 1), (0, 3), (1, 0), (0, 2), (1, 1), (1, 3), (1, 2))
+PASSES = ((0, 1, 2), (3, 4, 5, 6))
 
 BF = jnp.bfloat16
 F32 = jnp.float32
@@ -93,10 +96,10 @@
 
 
 def forward_kernel(
-    valid, hid, wq, up, down, out, small,
-    hid_all, wqkv, q_all, kv_all, o_all, up_g, down_g, out_g, vecs,
-    wq_g, small_g, wf, q_st, kv_st, qvb, state, o_st,
-    hid_s, hid_r, wq_s, wq_r, up_s, up_r, dn_s, dn_r, ou_s, ou_r, sm_s, sm_r,
+    valid, hid, wq, out,
+    hid_all, wqkv, q_all, kv_all, o_all, out_g, vecs,
+    wq_g, wf, q_st, kv_st, qvb, state, o_st,
+    hid_s, hid_r, wq_s, wq_r, ou_s, ou_r,
     q_s, q_r, kv_s, kv_r, o_s, o_r, loc,
 ):
     s = lax.axis_index("sp")
@@ -115,65 +118,40 @@
         )
 
     wq_copy = fs_copy(wq, wq_g, wq_s, wq_r)
-    small_copy = fs_copy(small, small_g, sm_s, sm_r)
-    up_copy = fs_copy(up, up_g, up_s, up_r)
-
-    def owned_copies(t):
+
+    def out_copy(t):
         k = lax.rem(f, 8)
-        to = {"fsdp": 8 * s + t, "sp": f // 8}
-        return (
-            remote(down, down_g.at[k], dn_s.at[t], dn_r.at[k], **to),
-            remote(out, out_g.at[k], ou_s.at[t], ou_r.at[k], **to),
-        )
-
-    def owned_arrivals(k):
-        to = {"fsdp": 8 * s + k, "sp": f // 8}
-        return (
-            remote(down, down_g.at[k], dn_s.at[k], dn_r.at[k], **to),
-            remote(out, out_g.at[k], ou_s.at[k], ou_r.at[k], **to),
-        )
+        return remote(out, out_g.at[k], ou_s.at[t], ou_r.at[k], fsdp=8 * s + t, sp=f // 8)
+
+    def out_arrival(k):
+        return remote(out, out_g.at[k], ou_s.at[k], ou_r.at[k], fsdp=8 * s + k, sp=f // 8)
 
     def is_self(t):
         return (s == f // 8) & (8 * s + t == f)
 
     loop(1, SP, lambda d: hid_copy(d).start())
 
-    def first_sends(d):
-        wq_copy(d).start()
-        small_copy(d).start()
-
-    loop(1, FS, first_sends)
+    loop(1, FS, lambda d: wq_copy(d).start())
     hid_all[pl.ds(pl.multiple_of(s * rows, rows), rows), :] = hid[...]
     wq_g[f] = wq[...]
-    small_g[f] = small[...]
-    up_own = pltpu.make_async_copy(up, up_g.at[f], loc.at[0])
-    up_own.start()
-
     loop(1, SP, lambda d: hid_copy(d).wait())
 
-    def first_waits(d):
-        wq_copy(d).wait()
-        small_copy(d).wait()
-
-    loop(1, FS, first_waits)
+    loop(1, FS, lambda d: wq_copy(d).wait())
 
     width = vecs.shape[1]
-    total = jnp.zeros((8, width), F32)
-    pad = jnp.zeros((8, width - 128), F32)
-    for n in range(FS):
-        piece = small_g[n][0:8].astype(F32)
-        wide = jnp.concatenate((piece, pad), axis=1)
-        total = total + (wide if n == 0 else pltpu.roll(wide, 24 * n, 1))
-    vecs[0:8, :] = total
-    ub = jnp.zeros((8, width), F32)
+    pad = jnp.zeros((8, width - 64), F32)
+
+    def riders(n, low):
+        block = wq_g[n, low : low + 8, 512:640].astype(F32)
+        wide = jnp.concatenate((block[:, 64:128], pad), axis=1)
+        return wide
+
+    def shifted(wide, amount):
+        return wide if amount == 0 else pltpu.roll(wide, amount, 1)
+
     qv = jnp.zeros((8, width), F32)
-    for k in range(8):
-        block = small_g[8 * s + k].astype(F32)
-        ub_wide = jnp.concatenate((block[8:16], pad), axis=1)
-        qv_wide = jnp.concatenate((block[0:8], pad), axis=1)
-        ub = ub + (ub_wide if k == 0 else pltpu.roll(ub_wide, 96 * k, 1))
-        qv = qv + (qv_wide if k == 0 else pltpu.roll(qv_wide, 24 * k, 1))
-    vecs[8:16, :] = ub
+    for n in range(8):
+        qv = qv + shifted(riders(8 * s + n, 0), 24 * n)
     qvb[...] = qv
     lane = lax.broadcasted_iota(jnp.int32, (1, width), 1)
     qrow = qvb[0:1, :]
@@ -187,7 +165,7 @@
         bias = bias + jnp.where(here, pltpu.roll(wide_v, 64 * h + 64, 1)[0:1], 0.0)
 
     def assemble(n):
-        wf[pl.ds(pl.multiple_of(24 * n, 8), 24), :] = wq_g[n].astype(F32)
+        wf[pl.ds(pl.multiple_of(24 * n, 8), 24), :] = wq_g[n, :, 0:576].astype(F32)
 
     loop(0, FS, assemble)
     wqkv[...] = wf[...].astype(BF)
@@ -207,31 +185,60 @@
 
     loop(0, SP, project)
 
-    def kv_copy(d):
-        to = lax.rem(i + d, XG) * YG + j
-        return remote(kv_st, kv_all.at[i], kv_s.at[d - 1], kv_r.at[d - 1], fsdp=to)
+    def kv_copy(n):
+        dz, dx = KEY_STEPS[n]
+        to = lax.rem(i // YG + dz, 2) * YG + lax.rem(i + dx, YG)
+        return remote(kv_st, kv_all.at[i], kv_s.at[n], kv_r.at[n], fsdp=to * YG + j)
+
+    def kv_from(n):
+        dz, dx = KEY_STEPS[n]
+        return lax.rem(i // YG + dz, 2) * YG + lax.rem(i + YG - dx, YG)
 
     def q_copy(d):
         to = i * YG + lax.rem(j + d, YG)
         return remote(q_st, q_all.at[j], q_s.at[d - 1], q_r.at[d - 1], fsdp=to)
 
-    loop(1, XG, lambda d: kv_copy(d).start())
     loop(1, YG, lambda d: q_copy(d).start())
+    for n in range(XG - 1):
+        kv_copy(n).start()
     kv_all[i] = kv_st[...]
     q_all[j] = q_st[...]
 
+    total = jnp.zeros((8, width), F32)
+    for n in range(FS):
+        total = total + shifted(riders(n, 0), 24 * n)
+    vecs[0:8, :] = total
+    ub = jnp.zeros((8, width), F32)
+    for n in range(8):
+        rider = riders(8 * s + n, 8)
+        for c in range(4):
+            row = jnp.broadcast_to(rider[c : c + 1], (8, width))
+            ub = ub + shifted(row, 96 * n + 24 * c)
+    vecs[8:16, :] = ub
+
+    def send_out(t):
+        @pl.when(jnp.logical_not(is_self(t)))
+        def _():
+            out_copy(t).start()
+
+    loop(0, 8, send_out)
+
+    @pl.when(s == f // 8)
+    def _():
+        out_own = pltpu.make_async_copy(out, out_g.at[lax.rem(f, 8)], loc.at[0])
+        out_own.start()
+        out_own.wait()
+
     tall = SP * rows
-    half = tall // 2
     key_place = lax.broadcasted_iota(jnp.int32, (1, tall), 1)
-    lanes = lax.broadcasted_iota(jnp.int32, (half, 128), 1)
+    lanes = lax.broadcasted_iota(jnp.int32, (tall, 128), 1)
 
     def o_copy(d, h):
         to = lax.rem(j + YG - d, YG)
         src = o_st.at[to, h]
         return remote(src, o_all.at[j, h], o_s.at[d - 1, h], o_r.at[d - 1, h], fsdp=i * YG + to)
 
-    def attend(step, is_first, is_last):
-        places = [lax.rem(i + XG - 2 * step - c, XG) for c in range(2)]
+    def attend(places, is_first, is_last):
         limits = [
             jnp.where((at * YG + j) * tall + key_place < valid[0], 0.0, masked) for at in places
         ]
@@ -246,36 +253,33 @@
                 def _():
                     q_copy(d).wait_recv()
 
-            for r in range(2):
-                at = pl.ds(r * half, half)
-                query = q_all[n, h, at, :]
-                blocks = [kv_all[p, h] for p in places]
-                scores = [dot_nt(query, block) + limit for block, limit in zip(blocks, limits)]
-                tops = [jnp.max(score, axis=1, keepdims=True) for score in scores]
-                top = jnp.maximum(tops[0], tops[1])
-                if not is_first:
-                    old = state[n, h, at, :]
-                    before = old[:, 0:1]
-                    top = jnp.maximum(top, before)
-                probs = [jnp.exp(score - top) for score in scores]
-                total = functools.reduce(
-                    jnp.add, [jnp.sum(p, axis=1, keepdims=True) for p in probs]
-                )
-                weighted = functools.reduce(
-                    jnp.add, [dot_nn(p.astype(BF), block) for p, block in zip(probs, blocks)]
-                )
-                if not is_first:
-                    decay = jnp.exp(before - top)
-                    total = total + decay * old[:, 32:33]
-                    weighted = weighted + decay * old
-                if is_last:
-                    log_sum = top + jnp.log(total)
-                    high = log_sum.astype(BF).astype(F32)
-                    logs = jnp.where(lanes < 32, high, log_sum - high)
-                    o_st[n, h, at, :] = jnp.where(lanes >= 64, weighted / total, logs).astype(BF)
+            query = q_all[n, h]
+            m = l = acc = None
+            if not is_first:
+                acc = state[n, h]
+                m, l = acc[:, 0:1], acc[:, 32:33]
+            for at, limit in zip(places, limits):
+                block = kv_all[at, h]
+                scores = dot_nt(query, block) + limit
+                top = jnp.max(scores, axis=1, keepdims=True)
+                new = top if m is None else jnp.maximum(m, top)
+                p = jnp.exp(scores - new)
+                part = jnp.sum(p, axis=1, keepdims=True)
+                weighted = dot_nn(p.astype(BF), block)
+                if m is None:
+                    l, acc = part, weighted
                 else:
-                    logs = jnp.where(lanes < 32, top, total)
-                    state[n, h, at, :] = jnp.where(lanes >= 64, weighted, logs)
+                    decay = jnp.exp(m - new)
+                    l = l * decay + part
+                    acc = acc * decay + weighted
+                m = new
+            if is_last:
+                log_sum = m + jnp.log(l)
+                high = log_sum.astype(BF).astype(F32)
+                logs = jnp.where(lanes < 32, high, log_sum - high)
+                o_st[n, h] = jnp.where(lanes >= 64, acc / l, logs).astype(BF)
+            else:
+                state[n, h] = jnp.where(lanes >= 64, acc, jnp.where(lanes < 32, m, l))
             if is_last:
 
                 @pl.when(d > 0)
@@ -292,69 +296,87 @@
         else:
             loop(0, LH * YG, tile)
 
-    kv_copy(1).wait_recv()
-    attend(0, True, False)
-    loop(1, FS, lambda d: up_copy(d).start())
-
-    def send_owned(t):
-        @pl.when(jnp.logical_not(is_self(t)))
-        def _():
-            for copy in owned_copies(t):
-                copy.start()
-
-    loop(0, 8, send_owned)
-
-    @pl.when(s == f // 8)
-    def _():
-        dn_own = pltpu.make_async_copy(down, down_g.at[lax.rem(f, 8)], loc.at[1])
-        ou_own = pltpu.make_async_copy(out, out_g.at[lax.rem(f, 8)], loc.at[2])
-        dn_own.start()
-        ou_own.start()
-        dn_own.wait()
-        ou_own.wait()
-
-    def middle_pass(step):
-        kv_copy(2 * step).wait_recv()
-        kv_copy(2 * step + 1).wait_recv()
-        attend(step, False, False)
-
-    loop(1, XG // 2 - 1, middle_pass)
-    kv_copy(XG - 2).wait_recv()
-    kv_copy(XG - 1).wait_recv()
-    attend(XG // 2 - 1, False, True)
-
-    up_own.wait()
-    loop(1, XG, lambda d: kv_copy(d).wait_send())
+    for step, members in enumerate(PASSES):
+        for n in members:
+            kv_copy(n).wait_recv()
+        places = [kv_from(n) for n in members]
+        attend(places if step else [i] + places, step == 0, step == len(PASSES) - 1)
+
+    for n in range(XG - 1):
+        kv_copy(n).wait_send()
     loop(1, YG, lambda d: q_copy(d).wait_send())
-    loop(1, FS, lambda d: up_copy(d).wait())
 
     def owned_wait(t):
         @pl.when(jnp.logical_not(is_self(t)))
         def _():
-            for copy in owned_copies(t):
-                copy.wait_send()
-            for copy in owned_arrivals(t):
-                copy.wait_recv()
+            out_copy(t).wait_send()
+            out_arrival(t).wait_recv()
 
     loop(0, 8, owned_wait)
     loop(1, YG, lambda d: loop(0, LH, lambda h: o_copy(d, h).wait()))
 
 
 def middle_kernel(
-    o_all, wo, wup, wdn, vecs, hid, cot,
-    result, gfs, d_all, ld_all, dup, ddn, dwo, vp,
+    o_all, out_g, up, down, vecs, hid, cot,
+    result, gfs, d_all, ld_all, up_own, up_rb, dn_rb, dwo, vp,
+    up_g, wf, wo, wup, wdn, dup, ddn,
     att, ld, st, own, first, n1, inv1, x_all, act, deriv, gd, gp, gb, gsec, rb, dbuf, ldrow, vg,
     ag_s, ag_r, rs_s, rs_r, d_s, d_r, l_s, l_r, loc,
+    ua_s, ua_r, ub_s, ub_r, dn_s, dn_r, us_s, us_r, ds_s, ds_r,
 ):
     s = lax.axis_index("sp")
     f = lax.axis_index("fsdp")
     i, j = f // YG, lax.rem(f, YG)
     rows = hid.shape[0]
     tall = SP * rows
-    barrier = pltpu.get_barrier_semaphore()
-    loop(1, YG, lambda d: greet(barrier, fsdp=i * YG + lax.rem(j + d, YG)))
-    loop(1, SP, lambda d: greet(barrier, sp=lax.rem(s + d, SP)))
-    pl.semaphore_wait(barrier, YG - 1 + SP - 1)
+    z, x = f // 16, lax.rem(i, YG)
+    greet_all(f, s)
+
+    def zy_copy(n):
+        to = (lax.rem(z + (n + 1) // YG, 2) * YG + x) * YG + lax.rem(j + n + 1, YG)
+        return remote(up, up_g.at[f], ua_s.at[n], ua_r.at[n], fsdp=to)
+
+    def x_copy(d):
+        to = (z * YG + lax.rem(x + d, YG)) * YG + j
+        copies = []
+        for n in range(2):
+            at = up_g.at[pl.ds((n * YG + x) * YG, YG)]
+            copies.append(remote(at, at, ub_s.at[d - 1, n], ub_r.at[d - 1, n], fsdp=to))
+        return copies
+
+    def down_copy(t):
+        k = lax.rem(f, 8)
+        dst = wdn.at[pl.ds(k * 96, 96)]
+        return remote(down, dst, dn_s.at[t], dn_r.at[k], fsdp=8 * s + t, sp=f // 8)
+
+    def down_arrival(k):
+        dst = wdn.at[pl.ds(k * 96, 96)]
+        return remote(down, dst, dn_s.at[k], dn_r.at[k], fsdp=8 * s + k, sp=f // 8)
+
+    def is_self(t):
+        return (s == f // 8) & (8 * s + t == f)
+
+    def unless_self(work):
+        def step(t):
+            @pl.when(jnp.logical_not(is_self(t)))
+            def _():
+                work(t)
+
+        loop(0, 8, step)
+
+    for n in range(XG - 1):
+        zy_copy(n).start()
+    unless_self(lambda t: down_copy(t).start())
+    up_g[f] = up[...]
+
+    @pl.when(s == f // 8)
+    def _():
+        wdn[pl.ds(pl.multiple_of(lax.rem(f, 8) * 96, 32), 96), :] = down[...]
+
+    wf[0:192, :] = out_g[...].astype(F32).reshape(192, wf.shape[1])
+    for h in range(LH):
+        wo[128 * h : 128 * h + 64, :] = jnp.zeros((64, wo.shape[1]), BF)
+        wo[128 * h + 64 : 128 * h + 128, :] = wf[64 * h : 64 * h + 64, :].astype(BF)
 
     def y_peer(d):
         return i * YG + lax.rem(j + d, YG)
@@ -416,6 +438,11 @@
             own[...] = value
 
     loop(1, SP + 1, out_part)
+    for n in range(XG - 1):
+        zy_copy(n).wait()
+    for d in range(1, YG):
+        for copy in x_copy(d):
+            copy.start()
     summed = hid[...].astype(F32) + collect(0) + vecs[2:3, :]
     value, normed, inverse = norm_forward(summed, vecs[3:4, :], vecs[4:5, :])
     first[...] = value
@@ -423,6 +450,17 @@
     inv1[...] = jnp.broadcast_to(inverse, inv1.shape)
     x_all[span(s), :] = value.astype(BF)
     loop(1, SP, lambda d: gather(0, x_all)(d).start())
+
+    for d in range(1, YG):
+        for copy in x_copy(d):
+            copy.wait()
+
+    def assemble(n):
+        wf[pl.ds(pl.multiple_of(24 * n, 8), 24), :] = up_g[n].astype(F32)
+
+    loop(0, FS, assemble)
+    wup[...] = wf[...].astype(BF)
+    unless_self(lambda t: (down_copy(t).wait_send(), down_arrival(t).wait_recv()))
 
     def pipeline(e, buf, work):
         def step(d):
@@ -480,10 +518,46 @@
 
     def weight_terms(c):
         at = pl.ds(pl.multiple_of(128 * c, 128), 128)
+        wf[at, :] = dot_tn(x_all[:, at], gp[...])
         ddn[at, :] = dot_tn(act[:, at], gd[...]).astype(BF)
-        dup[at, :] = dot_tn(x_all[:, at], gp[...]).astype(BF)
 
     loop(0, act.shape[1] // 128, weight_terms)
+
+    def cut(n):
+        dup[n] = wf[pl.ds(pl.multiple_of(24 * n, 8), 24), :].astype(BF)
+
+    loop(0, FS, cut)
+
+    def up_sum(d):
+        to = lax.rem(x + d, YG)
+        copies = []
+        for n in range(2):
+            src = dup.at[pl.ds((n * YG + to) * YG, YG)]
+            sems = (us_s.at[d - 1, n], us_r.at[d - 1, n])
+            copies.append(remote(src, up_rb.at[d - 1, n], *sems, fsdp=(z * YG + to) * YG + j))
+        return copies
+
+    def down_sum(t):
+        k = lax.rem(f, 8)
+        src = ddn.at[pl.ds(t * 96, 96)]
+        return remote(src, dn_rb.at[k], ds_s.at[t], ds_r.at[k], fsdp=8 * s + t, sp=f // 8)
+
+    def down_sum_arrival(k):
+        src = ddn.at[pl.ds(k * 96, 96)]
+        return remote(src, dn_rb.at[k], ds_s.at[k], ds_r.at[k], fsdp=8 * s + k, sp=f // 8)
+
+    for d in range(1, YG):
+        for copy in up_sum(d):
+            copy.start()
+    unless_self(lambda t: down_sum(t).start())
+    for n in range(2):
+        up_own[n] = dup[pl.ds((n * YG + x) * YG, YG)]
+
+    @pl.when(s == f // 8)
+    def _():
+        k = lax.rem(f, 8)
+        dn_rb[k] = ddn[pl.ds(pl.multiple_of(k * 96, 32), 96), :]
+
     ub = jnp.sum(gp[...].astype(F32), axis=0, keepdims=True)
     grad_first = gsec[...] + collect(2)
     grad, ggain, gshift = norm_backward(grad_first, n1[...], inv1[:, 0:1], vecs[3:4, :])
@@ -548,14 +622,18 @@
     l_own.wait()
     loop(1, YG, lambda n: loop(0, SP, lambda d: d_copy(n, d).wait()))
     loop(1, YG, lambda d: l_copy(d).wait())
+    for d in range(1, YG):
+        for copy in up_sum(d):
+            copy.wait()
+    unless_self(lambda t: (down_sum(t).wait_send(), down_sum_arrival(t).wait_recv()))
 
 
 def backward_kernel(
-    valid, q_all, d_all, ld, kv_all, hid_all, wqkv, gfs, dup, ddn, dwo, vp,
-    input_grad, qkvg, upg, dng, outg, vecg, qvg,
-    acc, dq, dkv, kv_rb, q_rb, g, wf, wp, bp, st, own, rb, wq_rb, up_rb, dn_rb, ou_rb, vp_rb, bp_rb,
-    up_fin, dn_fin, ou_fin, v_fin, qv_fin,
-    kv_s, kv_r, q_s, q_r, wq_s, wq_r, up_s, up_r, dn_s, dn_r, ou_s, ou_r, vp_s, vp_r, bp_s, bp_r,
+    valid, q_all, d_all, ld, kv_all, hid_all, wqkv, gfs, up_own, up_rb, dn_rb, dwo, vp,
+    input_grad, wkg, wqg, upg, dng, outg, vecg,
+    acc, dq, dkv, kv_rb, q_rb, g, wf, wk, wp, st, own, rb, wk_rb, wq_rb, up_st, up_rc, ou_rb, vp_rb,
+    up_fin, dn_fin, ou_fin, v_fin, wk_fin, wq_fin,
+    kv_s, kv_r, q_s, q_r, wk_s, wk_r, wq_s, wq_r, up_s, up_r, ou_s, ou_r, vp_s, vp_r,
     rs_s, rs_r, fin_s, fin_r,
 ):
     s = lax.axis_index("sp")
@@ -580,47 +658,55 @@
 
         return copy
 
-    up_copy = fs_copy(dup, up_rb, up_s, up_r)
     vp_copy = fs_copy(vp, vp_rb, vp_s, vp_r)
     wq_copy = fs_copy(wp, wq_rb, wq_s, wq_r)
-    bp_copy = fs_copy(bp, bp_rb, bp_s, bp_r)
-
-    def owner_copies(k):
-        to = {"fsdp": 8 * s + k, "sp": f // 8}
+    wk_copy = fs_copy(wk, wk_rb, wk_s, wk_r)
+    z, x = f // 16, lax.rem(i, YG)
+
+    def up_copy(n):
+        zn, yn = lax.rem(z + (n + 1) // YG, 2), lax.rem(j + n + 1, YG)
+        to = (zn * YG + x) * YG + yn
+        return remote(up_st.at[zn * YG + yn], up_rc.at[n], up_s.at[n], up_r.at[n], fsdp=to)
+
+    def out_copy(k):
         n = lax.rem(f, 8)
-        return (
-            remote(ddn.at[k], dn_rb.at[n], dn_s.at[k], dn_r.at[n], **to),
-            remote(dwo.at[k], ou_rb.at[n], ou_s.at[k], ou_r.at[n], **to),
-        )
-
-    def owner_arrivals(n):
-        to = {"fsdp": 8 * s + n, "sp": f // 8}
-        return (
-            remote(ddn.at[n], dn_rb.at[n], dn_s.at[n], dn_r.at[n], **to),
-            remote(dwo.at[n], ou_rb.at[n], ou_s.at[n], ou_r.at[n], **to),
-        )
+        return remote(dwo.at[k], ou_rb.at[n], ou_s.at[k], ou_r.at[n], fsdp=8 * s + k, sp=f // 8)
+
+    def out_arrival(n):
+        return remote(dwo.at[n], ou_rb.at[n], ou_s.at[n], ou_r.at[n], fsdp=8 * s + n, sp=f // 8)
 
     def is_self(t):
         return (s == f // 8) & (8 * s + t == f)
 
-    def early(d):
-        up_copy(d).start()
-        vp_copy(d).start()
-
-    loop(1, FS, early)
+    for n in range(2):
+        for c in range(YG):
+            total = up_own[n, c].astype(F32)
+            for d in range(YG - 1):
+                total = total + up_rb[d, n, c].astype(F32)
+            up_st[n * YG + c] = total.astype(BF)
+    for n in range(XG - 1):
+        up_copy(n).start()
+    loop(1, FS, lambda d: vp_copy(d).start())
 
     def to_owner(k):
         @pl.when(jnp.logical_not(is_self(k)))
         def _():
-            for copy in owner_copies(k):
-                copy.start()
+            out_copy(k).start()
 
         @pl.when(is_self(k))
         def _():
-            dn_rb[k] = ddn[k]
             ou_rb[k] = dwo[k]
 
     loop(0, 8, to_owner)
+
+    def down_rows(c):
+        at = pl.ds(pl.multiple_of(c * 32, 32), 32)
+        total = dn_rb[0, at, :].astype(F32)
+        for n in range(1, 8):
+            total = total + dn_rb[n, at, :].astype(F32)
+        dn_fin[s, at, :] = total.astype(BF)
+
+    loop(0, dn_fin.shape[1] // 32, down_rows)
 
     acc[...] = jnp.zeros(acc.shape, F32)
 
@@ -670,55 +756,6 @@
             dq[n, 64 * h : 64 * h + 64, :] = acc[n, h].astype(BF)
     loop(1, YG, lambda d: q_copy(d).start())
 
-    def late(d):
-        up_copy(d).wait()
-        vp_copy(d).wait()
-
-    loop(1, FS, late)
-
-    def add_up(buf, start):
-        def step(d, total):
-            return total + buf[d].astype(F32)
-
-        return lax.fori_loop(0, buf.shape[0], step, start)
-
-    up_fin[s] = add_up(up_rb, dup[f].astype(F32)).astype(BF)
-    v_fin[s] = add_up(vp_rb, vp[f])
-
-    def owner_wait(t):
-        @pl.when(jnp.logical_not(is_self(t)))
-        def _():
-            for copy in owner_copies(t):
-                copy.wait_send()
-            for copy in owner_arrivals(t):
-                copy.wait_recv()
-
-    loop(0, 8, owner_wait)
-
-    def down_rows(c):
-        at = pl.ds(pl.multiple_of(c * 32, 32), 32)
-        total = dn_rb[0, at, :].astype(F32)
-        for n in range(1, 8):
-            total = total + dn_rb[n, at, :].astype(F32)
-        dn_fin[s, at, :] = total.astype(BF)
-
-    loop(0, dn_fin.shape[1] // 32, down_rows)
-    ou_fin[s] = add_up(ou_rb, jnp.zeros(ou_fin.shape[1:], F32)).astype(BF)
-
-    def sp_copy(e, buf):
-        def copy(d):
-            at = buf.at[s]
-            return remote(at, at, fin_s.at[e, d - 1], fin_r.at[e, d - 1], sp=lax.rem(s + d, SP))
-
-        return copy
-
-    early_bufs = ((0, up_fin), (1, v_fin), (4, dn_fin), (5, ou_fin))
-    for e, buf in early_bufs:
-        loop(1, SP, lambda d: sp_copy(e, buf)(d).start())
-
-    loop(1, XG, lambda d: kv_copy(d).wait())
-    loop(1, YG, lambda d: q_copy(d).wait())
-
     def span(b):
         return pl.ds(pl.multiple_of(b * rows, rows), rows)
 
@@ -730,73 +767,126 @@
                 total = total + kv_rb[d, h, at, :].astype(F32)
             g[at, 128 * h : 128 * h + 128] = total.astype(BF)
 
+    loop(1, XG, lambda d: kv_copy(d).wait())
     loop(0, SP, sum_keys)
+
+    def key_terms(c):
+        at = pl.ds(pl.multiple_of(128 * c, 128), 128)
+        wf[at, 0:384] = dot_tn(hid_all[:, at], g[:, 0:384])
+
+    loop(0, wf.shape[0] // 128, key_terms)
+
+    def cut_keys(n):
+        wk[n] = wf[pl.ds(pl.multiple_of(24 * n, 8), 24), 0:384].astype(BF)
+
+    loop(0, FS, cut_keys)
+    loop(1, FS, lambda d: wk_copy(d).start())
+
+    def add_up(buf, start):
+        def step(d, total):
+            return total + buf[d].astype(F32)
+
+        return lax.fori_loop(0, buf.shape[0], step, start)
+
+    for n in range(XG - 1):
+        up_copy(n).wait()
+    loop(1, FS, lambda d: vp_copy(d).wait())
+    up_fin[s] = add_up(up_rc, up_st[z * YG + j].astype(F32)).astype(BF)
+    v_fin[s] = add_up(vp_rb, vp[f])
+
+    def owner_wait(t):
+        @pl.when(jnp.logical_not(is_self(t)))
+        def _():
+            out_copy(t).wait_send()
+            out_arrival(t).wait_recv()
+
+    loop(0, 8, owner_wait)
+    ou_fin[s] = add_up(ou_rb, jnp.zeros(ou_fin.shape[1:], F32)).astype(BF)
+
+    def sp_copy(e, buf):
+        def copy(d):
+            at = buf.at[s]
+            return remote(at, at, fin_s.at[e, d - 1], fin_r.at[e, d - 1], sp=lax.rem(s + d, SP))
+
+        return copy
+
+    early_bufs = ((0, up_fin), (1, v_fin), (4, dn_fin), (5, ou_fin))
+    for e, buf in early_bufs:
+        loop(1, SP, lambda d: sp_copy(e, buf)(d).start())
+
+    loop(1, YG, lambda d: q_copy(d).wait())
     total = dq[j].astype(F32)
     for d in range(YG - 1):
         total = total + q_rb[d].astype(F32)
     g[:, 384:576] = (jnp.transpose(total, (1, 0)) * 0.125).astype(BF)
 
-    def weight_terms(c):
+    def query_terms(c):
         at = pl.ds(pl.multiple_of(128 * c, 128), 128)
-        wf[at, :] = dot_tn(hid_all[:, at], g[...])
-
-    loop(0, wf.shape[0] // 128, weight_terms)
-
-    def cut(n):
-        wp[n] = wf[pl.ds(pl.multiple_of(24 * n, 8), 24), :].astype(BF)
-
-    loop(0, FS, cut)
-    loop(1, FS, lambda d: wq_copy(d).start())
-
-    def input_part(d):
-        b = lax.rem(s + d, SP)
-        value = dot_nt(g[span(b), :], wqkv[...])
-
-        @pl.when(d < SP)
-        def _():
-            st[span(b), :] = value.astype(BF)
-            rs_copy(d).start()
-
-        @pl.when(d == SP)
-        def _():
-            own[...] = value
-
-    def rs_copy(d):
-        to = lax.rem(s + d, SP)
-        src = st.at[pl.ds(to * rows, rows)]
-        return remote(src, rb.at[d - 1], rs_s.at[d - 1], rs_r.at[d - 1], sp=to)
-
-    loop(1, SP + 1, input_part)
+        value = dot_tn(hid_all[:, at], g[:, 384:576])
+        wf[at, 384:640] = jnp.concatenate((value, jnp.zeros((128, 64), F32)), axis=1)
+
+    loop(0, wf.shape[0] // 128, query_terms)
 
     sums = jnp.sum(g[...].astype(F32), axis=0, keepdims=True)
-    lane = lax.broadcasted_iota(jnp.int32, (8, 128), 1)
     row = lax.broadcasted_iota(jnp.int32, (8, 256), 0)
     low = lax.broadcasted_iota(jnp.int32, (8, 128), 1) < 64
     wide = jnp.broadcast_to(jnp.concatenate((sums, jnp.zeros((1, 64), F32)), axis=1), (8, 640))
     heads = [pltpu.roll(wide[:, 128 * h : 128 * h + 128], 64, 1) for h in range(LH)]
     vrow = jnp.concatenate(
-        (
-            jnp.where(low, heads[0], wide[:, 128:256]),
-            jnp.where(low, heads[2], 0.0),
-        ),
-        axis=1,
+        (jnp.where(low, heads[0], wide[:, 128:256]), jnp.where(low, heads[2], 0.0)), axis=1
     )
     both = jnp.where(row == 0, wide[:, 384:640], jnp.where(row == 1, vrow, 0.0))
-    bp[...] = jnp.zeros(bp.shape, F32)
-    for k in range(8):
-        piece = both if k == 0 else pltpu.roll(both, 256 - 24 * k, 1)
-        bp[8 * s + k] = jnp.where(lane < 24, piece[:, 0:128], 0.0)
-    loop(1, FS, lambda d: bp_copy(d).start())
-
-    def later(d):
-        wq_copy(d).wait()
-        bp_copy(d).wait()
-
-    loop(1, FS, later)
-    qkvg[s] = add_up(wq_rb, wp[f].astype(F32)).astype(BF)
-    qv_fin[s] = add_up(bp_rb, bp[f])
-    loop(1, SP, lambda d: sp_copy(2, qkvg)(d).start())
-    loop(1, SP, lambda d: sp_copy(3, qv_fin)(d).start())
+
+    def cut_queries(n):
+        wp[n] = wf[pl.ds(pl.multiple_of(24 * n, 8), 24), 384:640].astype(BF)
+
+    loop(0, FS, cut_queries)
+    lane = lax.broadcasted_iota(jnp.int32, (8, 128), 1)
+    for n in range(8):
+        piece = both if n == 0 else pltpu.roll(both, 256 - 24 * n, 1)
+        piece = pltpu.roll(piece[:, 0:128], 64, 1)
+        piece = jnp.where((lane >= 64) & (lane < 88), piece, 0.0)
+        rest = jnp.concatenate((piece, jnp.zeros((16, 128), F32)), axis=0)
+        kept = wp[8 * s + n, :, 128:256].astype(F32)
+        lanes = lax.broadcasted_iota(jnp.int32, (24, 128), 1)
+        wp[8 * s + n, :, 128:256] = jnp.where(lanes < 64, kept, rest).astype(BF)
+    loop(1, FS, lambda d: wq_copy(d).start())
+
+    def input_part(d):
+        b = lax.rem(s + d, SP)
+        value = dot_nt(g[span(b), :], wqkv[...])
+
+        @pl.when(d < SP)
+        def _():
+            st[span(b), :] = value.astype(BF)
+            rs_copy(d).start()
+
+        @pl.when(d == SP)
+        def _():
+            own[...] = value
+
+    def rs_copy(d):
+        to = lax.rem(s + d, SP)
+        src = st.at[pl.ds(to * rows, rows)]
+        return remote(src, rb.at[d - 1], rs_s.at[d - 1], rs_r.at[d - 1], sp=to)
+
+    loop(1, SP + 1, input_part)
+
+    loop(1, FS, lambda d: wk_copy(d).wait())
+    wk_fin[s] = add_up(wk_rb, wk[f].astype(F32)).astype(BF)
+    loop(1, SP, lambda d: sp_copy(2, wk_fin)(d).start())
+    for e, buf in early_bufs:
+        loop(1, SP, lambda d: sp_copy(e, buf)(d).wait())
+    for n in range(SP):
+        upg[:, 768 * n : 768 * n + 768] = up_fin[n].astype(F32)
+    vecg[...] = v_fin[0] + v_fin[1] + v_fin[2] + v_fin[3]
+    down_total = dn_fin[0].astype(F32)
+    out_total = ou_fin[0].astype(F32)
+    for n in range(1, SP):
+        down_total = down_total + dn_fin[n].astype(F32)
+        out_total = out_total + ou_fin[n].astype(F32)
+    dng[...] = down_total
+    outg[...] = out_total
 
     loop(1, SP, lambda d: rs_copy(d).wait())
     total = gfs[...] + own[...]
@@ -804,22 +894,13 @@
         total = total + rb[d].astype(F32)
     input_grad[...] = total
 
-    for e, buf in early_bufs:
-        loop(1, SP, lambda d: sp_copy(e, buf)(d).wait())
-    for n in range(SP):
-        upg[:, 768 * n : 768 * n + 768] = up_fin[n].astype(F32)
-    vecg[...] = v_fin[0] + v_fin[1] + v_fin[2] + v_fin[3]
-    down_sum = dn_fin[0].astype(F32)
-    out_sum = ou_fin[0].astype(F32)
-    for n in range(1, SP):
-        down_sum = down_sum + dn_fin[n].astype(F32)
-        out_sum = out_sum + ou_fin[n].astype(F32)
-    dng[...] = down_sum
-    outg[...] = out_sum
-
-    loop(1, SP, lambda d: sp_copy(2, qkvg)(d).wait())
-    loop(1, SP, lambda d: sp_copy(3, qv_fin)(d).wait())
-    qvg[...] = qv_fin[0] + qv_fin[1] + qv_fin[2] + qv_fin[3]
+    loop(1, FS, lambda d: wq_copy(d).wait())
+    wq_fin[s] = add_up(wq_rb, wp[f].astype(F32)).astype(BF)
+    loop(1, SP, lambda d: sp_copy(3, wq_fin)(d).start())
+    loop(1, SP, lambda d: sp_copy(2, wk_fin)(d).wait())
+    wkg[...] = wk_fin[...].astype(F32)
+    loop(1, SP, lambda d: sp_copy(3, wq_fin)(d).wait())
+    wqg[...] = wq_fin[...].astype(F32)
 
 
 def on_device(
@@ -857,17 +938,17 @@
     kv_cols = jnp.stack((parts[:, 1], parts[:, 2]), axis=2).reshape(slim, -1)
     wq = jnp.concatenate((kv_cols, parts[:, 0].reshape(slim, -1)), axis=1)
     up = lax.dynamic_slice_in_dim(up_weight, s * share, share, 1)
-    small = jnp.stack(
+    riders = jnp.stack(
         (
             query_bias, value_bias, output_bias, first_gain, first_shift, down_bias,
             second_gain, second_shift,
         )
     )
-    small = jnp.pad(small, ((0, 8), (0, 128 - slim)))
-    small = lax.dynamic_update_slice(small, up_bias[None, :], (8, 0))
-
+    riders = jnp.pad(riders, ((0, slim - 8), (0, 64 - slim)))
+    riders = lax.dynamic_update_slice(riders, up_bias.reshape(4, slim), (8, 0))
+    wq = jnp.concatenate((wq, riders), axis=1)
     smem = pl.BlockSpec(memory_space=pltpu.SMEM)
-    hid_all, wqkv, q_all, kv_all, o_all, up_g, down_g, out_g, vecs = pl.pallas_call(
+    hid_all, wqkv, q_all, kv_all, o_all, out_g, vecs = pl.pallas_call(
         forward_kernel,
         out_shape=(
             shape((tall, width), BF),
@@ -875,16 +956,13 @@
             shape((YG, LH, tall, 128), BF),
             shape((XG, LH, tall, 128), BF),
             shape((YG, LH, tall, 128), BF),
-            shape((FS, slim, share), BF),
-            shape((8, deep, width), BF),
             shape((8, slim, width), BF),
             shape((16, width), F32),
         ),
-        in_specs=[smem] + [vmem] * 6,
-        out_specs=(vmem, vmem, vmem, vmem, vmem, hbm, hbm, hbm, vmem),
+        in_specs=[smem] + [vmem] * 3,
+        out_specs=(vmem, vmem, vmem, vmem, vmem, hbm, vmem),
         scratch_shapes=[
-            pltpu.VMEM((FS, slim, cols), BF),
-            pltpu.VMEM((FS, 16, 128), BF),
+            pltpu.VMEM((FS, slim, cols + 64), BF),
             pltpu.VMEM((width, cols), F32),
             pltpu.VMEM((LH, tall, 128), BF),
             pltpu.VMEM((LH, tall, 128), BF),
@@ -892,31 +970,37 @@
             pltpu.VMEM((YG, LH, tall, 128), F32),
             pltpu.VMEM((YG, LH, tall, 128), BF),
         ]
-        + [dma((n,)) for n in (3, 3, 31, 31, 31, 31, 8, 8, 8, 8, 31, 31, 3, 3, 7, 7)]
-        + [dma((3, 3)), dma((3, 3)), dma((3,))],
+        + [dma((n,)) for n in (3, 3, 31, 31, 8, 8, 3, 3, 7, 7)]
+        + [dma((3, 3)), dma((3, 3)), dma((1,))],
         compiler_params=pltpu.CompilerParams(
             collective_id=0, has_side_effects=True, vmem_limit_bytes=VMEM_LIMIT
         ),
         name="forward",
-    )(valid_length, hidden_in, wq, up, down_weight, output_weight, small)
-
-    wo = jnp.pad(out_g.reshape(LH, HEAD_DIM, width), ((0, 0), (HEAD_DIM, 0), (0, 0)))
-    wo = wo.reshape(LH * 128, width)
-    result, gfs, d_all, ld_all, dup, ddn, dwo, vp = pl.pallas_call(
+    )(valid_length, hidden_in, wq, output_weight)
+
+    result, gfs, d_all, ld_all, up_own, up_rb, dn_rb, dwo, vp = pl.pallas_call(
         middle_kernel,
         out_shape=(
             shape((rows, width), BF),
             shape((rows, width), F32),
             shape((YG, LH, tall, 128), BF),
             shape((YG, 8, tall), F32),
-            shape((width, share), BF),
-            shape((share, width), BF),
+            shape((2, YG, slim, share), BF),
+            shape((YG - 1, 2, YG, slim, share), BF),
+            shape((8, deep, width), BF),
             shape((LH * HEAD_DIM, width), BF),
             shape((FS, 16, 128), F32),
         ),
         in_specs=[vmem] * 7,
-        out_specs=(vmem, vmem, hbm, hbm, vmem, vmem, vmem, vmem),
+        out_specs=(vmem, vmem, hbm, hbm, vmem, vmem, vmem, vmem, vmem),
         scratch_shapes=[
+            pltpu.VMEM((FS, slim, share), BF),
+            pltpu.VMEM((width, share), F32),
+            pltpu.VMEM((LH * 128, width), BF),
+            pltpu.VMEM((width, share), BF),
+            pltpu.VMEM((share, width), BF),
+            pltpu.VMEM((FS, slim, share), BF),
+            pltpu.VMEM((share, width), BF),
             pltpu.VMEM((tall, LH * 128), BF),
             pltpu.VMEM((tall, 128), F32),
             pltpu.VMEM((3, tall, width), BF),
@@ -937,28 +1021,30 @@
             pltpu.VMEM((8, width), F32),
         ]
         + [dma((3, 3)) for _ in range(4)]
-        + [dma((3, 4)), dma((3, 4)), dma((3,)), dma((3,)), dma((2,))],
+        + [dma((3, 4)), dma((3, 4)), dma((3,)), dma((3,)), dma((2,))]
+        + [dma((7,)), dma((7,)), dma((3, 2)), dma((3, 2)), dma((8,)), dma((8,))]
+        + [dma((3, 2)), dma((3, 2)), dma((8,)), dma((8,))],
         compiler_params=pltpu.CompilerParams(
             collective_id=1, has_side_effects=True, vmem_limit_bytes=VMEM_LIMIT
         ),
         name="middle",
     )(
-        o_all, wo, up_g.reshape(width, share), down_g.reshape(share, width), vecs,
+        o_all, out_g, up, down_weight, vecs,
         hidden_in, out_cotangent,
     )
 
-    input_grad, qkvg, upg, dng, outg, vecg, qvg = pl.pallas_call(
+    input_grad, wkg, wqg, upg, dng, outg, vecg = pl.pallas_call(
         backward_kernel,
         out_shape=(
             shape((rows, width), F32),
-            shape((SP, slim, cols), BF),
+            shape((SP, slim, 2 * LH * HEAD_DIM), F32),
+            shape((SP, slim, 256), F32),
             shape((slim, SP * share), F32),
             shape((deep, width), F32),
             shape((slim, width), F32),
             shape((16, 128), F32),
-            shape((8, 128), F32),
         ),
-        in_specs=[smem] + [vmem] * 11,
+        in_specs=[smem] + [vmem] * 12,
         out_specs=(vmem,) * 7,
         scratch_shapes=[
             pltpu.VMEM((YG, LH, HEAD_DIM, tall), F32),
@@ -967,25 +1053,26 @@
             pltpu.VMEM((XG - 1, LH, tall, 128), BF),
             pltpu.VMEM((YG - 1, LH * HEAD_DIM, tall), BF),
             pltpu.VMEM((tall, cols), BF),
-            pltpu.VMEM((width, cols), F32),
-            pltpu.VMEM((FS, slim, cols), BF),
-            pltpu.VMEM((FS, 8, 128), F32),
+            pltpu.VMEM((width, 640), F32),
+            pltpu.VMEM((FS, slim, 384), BF),
+            pltpu.VMEM((FS, slim, 256), BF),
             pltpu.VMEM((tall, width), BF),
             pltpu.VMEM((rows, width), F32),
             pltpu.VMEM((SP - 1, rows, width), BF),
-            pltpu.VMEM((FS - 1, slim, cols), BF),
-            pltpu.VMEM((FS - 1, slim, share), BF),
-            pltpu.VMEM((8, deep, width), BF),
+            pltpu.VMEM((FS - 1, slim, 384), BF),
+            pltpu.VMEM((FS - 1, slim, 256), BF),
+            pltpu.VMEM((8, slim, share), BF),
+            pltpu.VMEM((XG - 1, slim, share), BF),
             pltpu.VMEM((8, slim, width), BF),
             pltpu.VMEM((FS - 1, 16, 128), F32),
-            pltpu.VMEM((FS - 1, 8, 128), F32),
             pltpu.VMEM((SP, slim, share), BF),
             pltpu.VMEM((SP, deep, width), BF),
             pltpu.VMEM((SP, slim, width), BF),
             pltpu.VMEM((SP, 16, 128), F32),
-            pltpu.VMEM((SP, 8, 128), F32),
+            pltpu.VMEM((SP, slim, 384), BF),
+            pltpu.VMEM((SP, slim, 256), BF),
         ]
-        + [dma((n,)) for n in (7, 7, 3, 3, 31, 31, 31, 31, 8, 8, 8, 8, 31, 31, 31, 31, 3, 3)]
+        + [dma((n,)) for n in (7, 7, 3, 3, 31, 31, 31, 31, 7, 7, 8, 8, 31, 31, 3, 3)]
         + [dma((6, 3)), dma((6, 3))],
         compiler_params=pltpu.CompilerParams(
             collective_id=2, has_side_effects=True, vmem_limit_bytes=VMEM_LIMIT
@@ -993,19 +1080,20 @@
         name="backward",
     )(
         valid_length, q_all, d_all, ld_all, kv_all, hid_all, wqkv, gfs,
-        dup.reshape(FS, slim, share), ddn.reshape(8, deep, width), dwo.reshape(8, slim, width), vp,
+        up_own, up_rb, dn_rb, dwo.reshape(8, slim, width), vp,
     )
 
-    kv_grad = qkvg[:, :, : LH * 128].reshape(SP, slim, LH, 2, HEAD_DIM)
-    q_grad = qkvg[:, :, LH * 128 :].reshape(SP, slim, LH, 1, HEAD_DIM)
+    kv_grad = wkg.reshape(SP, slim, LH, 2, HEAD_DIM)
+    q_grad = wqg[:, :, : LH * HEAD_DIM].reshape(SP, slim, LH, 1, HEAD_DIM)
     qkv_grad = jnp.concatenate((q_grad, kv_grad), axis=3)
-    qkv_grad = jnp.transpose(qkv_grad, (1, 3, 0, 2, 4)).reshape(slim, -1).astype(F32)
+    qkv_grad = jnp.transpose(qkv_grad, (1, 3, 0, 2, 4)).reshape(slim, -1)
+    qv_grad = jnp.sum(wqg[:, 0:2, LH * HEAD_DIM : LH * HEAD_DIM + slim], axis=0)
     return (
         result,
         input_grad,
         qkv_grad,
-        qvg[0, :slim],
-        qvg[1, :slim],
+        qv_grad[0],
+        qv_grad[1],
         outg,
         vecg[0, :slim],
         vecg[1, :slim],

time: 385 us -> 407 us (1.057)
  Pallas kernels: 366 us -> 390 us
    pallas_call x1, Pallas kernels: 87.3 us -> 113 us  [on_device(): pl.pallas_call(middle_kernel, out_shape=(shape((rows, width), BF), shape(...]
    pallas_call x1, Pallas kernels: 147 us -> 130 us  [on_device(): pl.pallas_call(backward_kernel, out_shape=(shape((rows, width), F32), sha...]
    pallas_call x1, Pallas kernels: 131 us -> 147 us  [on_device(): pl.pallas_call(forward_kernel, out_shape=(shape((tall, width), BF), shape...]
where the time goes in v3:
time: 407 us; the launch traced here: 406 us
  Pallas kernels  390 us (96%)
  local copies, waits for them, and re-layouts  13.3 us (3%)
    pallas_call x1, Pallas kernels, on_device(): pl.pallas_call(forward_kernel, out_shape=(shape((tall, width), BF), shape...  147 us
    pallas_call x1, Pallas kernels, on_device(): pl.pallas_call(backward_kernel, out_shape=(shape((rows, width), F32), sha...  130 us
    pallas_call x1, Pallas kernels, on_device(): pl.pallas_call(middle_kernel, out_shape=(shape((rows, width), BF), shape(...  113 us

profile of v3, /device:TPU:1, one launch (start us, length us, event | category | flops | bytes accessed | tf_op | source)
XLA Modules:
  0.0 406.4 jit_solution(830523584291749738)
XLA Ops:
  0.6 0.0 copy-start
  1.4 0.7 reshape.53
  2.1 0.8 stack.39
  2.9 0.3 dynamic_update_slice.3
  3.2 0.0 copy-done
  3.2 0.6 constant_dynamic-slice_fusion.up
  3.8 1.1 reshape.51
  5.1 0.1 reshape.52
  5.2 0.1 reshape_squeeze.3
  5.3 0.7 pad_maximum_fusion.1.wq
  6.0 147.0 %forward.1 = (bf16[512,768]{1,0:T(8,128)(2,1)}, bf16[768,576]{1,0:T(8,128)(2,1)}, bf16[4,3,512,128]{3,2,1,0:T(8,128)(2,1)}, bf16[8,3,512,128]{3,2,1,0:T(8,128)(2...) custom-call(s32[1]{0:T(128)S(6)} %copy.53.valid, bf16[128,768]{1,0:T(8,128)(2,1)} %hid.3, ...), custom_call_target="tpu_custom_call" | custom-call | tf_op jit(solution)/shard_map/forward/pallas_call | solution.py:951
  153.0 112.9 %middle.1 = (bf16[128,768]{1,0:T(8,128)(2,1)}, f32[128,768]{1,0:T(8,128)}, bf16[4,3,512,128]{3,2,1,0:T(8,128)(2,1)}, f32[4,8,512]{2,1,0:T(8,128)}, bf16[2,4,24,7...) custom-call(bf16[4,3,512,128]{3,2,1,0:T(8,128)(2,1)} %get-tuple-elem, ...), custom_call_target="tpu_custom_call" | custom-call | tf_op jit(solution)/shard_map/middle/pallas_call | solution.py:981
  265.9 130.0 %backward.1 = (f32[128,768]{1,0:T(8,128)}, f32[4,24,384]{2,1,0:T(8,128)}, f32[4,24,256]{2,1,0:T(8,128)}, f32[24,3072]{1,0:T(8,128)}, f32[96,768]{1,0:T(8,128)}, /*index=5*/f32[24,768]{1,0:T(8,128)}, f32[16,128]{1,0:T(8,128)}) custom-call(s32[1]{0:T(128)S(6)} %copy.53.valid, bf16[4,3,512,128]{3,2,1,0:T(8,128)(2,1)} %get-tuple-element.42.q_all, ...), custom_call_target="tpu_custom_call" | custom-call | tf_op jit(solution)/shard_map/backward/pallas_call | solution.py:1036
  395.9 1.2 slice_bitcast_fusion.5
  397.1 0.8 slice_reduce_fusion
  397.9 1.4 slice_bitcast_fusion.2
  399.4 1.0 reshape.55
  400.4 0.0 copy-start.4
  400.4 1.2 reshape.56
  401.5 0.0 copy-start.1
  401.6 0.1 copy.42
  401.7 0.0 copy-start.5
  401.7 0.0 copy-start.3
  401.7 0.2 maximum_bitcast_fusion
  401.8 0.0 copy-start.2
  401.9 1.1 reshape.57
  402.9 0.0 copy-done.4
  402.9 0.7 copy.54
  403.6 0.7 copy.55
  404.3 0.6 copy.56
  405.0 0.7 copy.57
  405.7 0.7 copy.58
  (11 shorter events, 0.1 us)
Async XLA Ops:
  0.6 2.6 copy-start
  400.4 2.5 copy-start.4
  401.5 2.0 copy-start.1
  401.7 2.7 copy-start.5
  401.7 3.3 copy-start.3
  401.8 3.8 copy-start.2

commit v4 on v3

--- a/solution.py
+++ b/solution.py
@@ -17,6 +17,7 @@
 
 KEY_STEPS = ((0, 1), (0, 3), (1, 0), (0, 2), (1, 1), (1, 3), (1, 2))
 PASSES = ((0, 1, 2), (3, 4, 5, 6))
+UP_STEP = 1
 
 BF = jnp.bfloat16
 F32 = jnp.float32
@@ -96,11 +97,12 @@
 
 
 def forward_kernel(
-    valid, hid, wq, out,
-    hid_all, wqkv, q_all, kv_all, o_all, out_g, vecs,
+    valid, hid, wq, out, up, down,
+    hid_all, wqkv, q_all, kv_all, o_all, out_g, up_g, wdn, vecs,
     wq_g, wf, q_st, kv_st, qvb, state, o_st,
     hid_s, hid_r, wq_s, wq_r, ou_s, ou_r,
     q_s, q_r, kv_s, kv_r, o_s, o_r, loc,
+    ua_s, ua_r, ub_s, ub_r, dn_s, dn_r,
 ):
     s = lax.axis_index("sp")
     f = lax.axis_index("fsdp")
@@ -126,8 +128,39 @@
     def out_arrival(k):
         return remote(out, out_g.at[k], ou_s.at[k], ou_r.at[k], fsdp=8 * s + k, sp=f // 8)
 
+    z, x = f // 16, lax.rem(i, YG)
+
+    def zy_copy(n):
+        to = (lax.rem(z + (n + 1) // YG, 2) * YG + x) * YG + lax.rem(j + n + 1, YG)
+        return remote(up, up_g.at[f], ua_s.at[n], ua_r.at[n], fsdp=to)
+
+    def x_copy(d):
+        to = (z * YG + lax.rem(x + d, YG)) * YG + j
+        copies = []
+        for n in range(2):
+            at = up_g.at[pl.ds((n * YG + x) * YG, YG)]
+            copies.append(remote(at, at, ub_s.at[d - 1, n], ub_r.at[d - 1, n], fsdp=to))
+        return copies
+
+    def down_copy(t):
+        k = lax.rem(f, 8)
+        dst = wdn.at[pl.ds(k * 96, 96)]
+        return remote(down, dst, dn_s.at[t], dn_r.at[k], fsdp=8 * s + t, sp=f // 8)
+
+    def down_arrival(k):
+        dst = wdn.at[pl.ds(k * 96, 96)]
+        return remote(down, dst, dn_s.at[k], dn_r.at[k], fsdp=8 * s + k, sp=f // 8)
+
     def is_self(t):
         return (s == f // 8) & (8 * s + t == f)
+
+    def unless_self(work):
+        def step(t):
+            @pl.when(jnp.logical_not(is_self(t)))
+            def _():
+                work(t)
+
+        loop(0, 8, step)
 
     loop(1, SP, lambda d: hid_copy(d).start())
 
@@ -229,9 +262,19 @@
         out_own.start()
         out_own.wait()
 
+    for n in range(XG - 1):
+        zy_copy(n).start()
+    unless_self(lambda t: down_copy(t).start())
+    up_g[f] = up[...]
+
+    @pl.when(s == f // 8)
+    def _():
+        wdn[pl.ds(pl.multiple_of(lax.rem(f, 8) * 96, 32), 96), :] = down[...]
+
     tall = SP * rows
     key_place = lax.broadcasted_iota(jnp.int32, (1, tall), 1)
-    lanes = lax.broadcasted_iota(jnp.int32, (tall, 128), 1)
+    half = tall // 2
+    lanes = lax.broadcasted_iota(jnp.int32, (half, 128), 1)
 
     def o_copy(d, h):
         to = lax.rem(j + YG - d, YG)
@@ -253,33 +296,37 @@
                 def _():
                     q_copy(d).wait_recv()
 
-            query = q_all[n, h]
-            m = l = acc = None
-            if not is_first:
-                acc = state[n, h]
-                m, l = acc[:, 0:1], acc[:, 32:33]
-            for at, limit in zip(places, limits):
-                block = kv_all[at, h]
-                scores = dot_nt(query, block) + limit
-                top = jnp.max(scores, axis=1, keepdims=True)
-                new = top if m is None else jnp.maximum(m, top)
-                p = jnp.exp(scores - new)
-                part = jnp.sum(p, axis=1, keepdims=True)
-                weighted = dot_nn(p.astype(BF), block)
-                if m is None:
-                    l, acc = part, weighted
+            for r in range(2):
+                part_at = pl.ds(r * half, half)
+                query = q_all[n, h, part_at, :]
+                blocks = [kv_all[at, h] for at in places]
+                scores = [dot_nt(query, block) + limit for block, limit in zip(blocks, limits)]
+                tops = [jnp.max(score, axis=1, keepdims=True) for score in scores]
+                top = functools.reduce(jnp.maximum, tops)
+                if not is_first:
+                    old = state[n, h, part_at, :]
+                    before = old[:, 0:1]
+                    top = jnp.maximum(top, before)
+                probs = [jnp.exp(score - top) for score in scores]
+                total = functools.reduce(
+                    jnp.add, [jnp.sum(p, axis=1, keepdims=True) for p in probs]
+                )
+                weighted = functools.reduce(
+                    jnp.add, [dot_nn(p.astype(BF), block) for p, block in zip(probs, blocks)]
+                )
+                if not is_first:
+                    decay = jnp.exp(before - top)
+                    total = total + decay * old[:, 32:33]
+                    weighted = weighted + decay * old
+                if is_last:
+                    log_sum = top + jnp.log(total)
+                    high = log_sum.astype(BF).astype(F32)
+                    logs = jnp.where(lanes < 32, high, log_sum - high)
+                    merged = jnp.where(lanes >= 64, weighted / total, logs)
+                    o_st[n, h, part_at, :] = merged.astype(BF)
                 else:
-                    decay = jnp.exp(m - new)
-                    l = l * decay + part
-                    acc = acc * decay + weighted
-                m = new
-            if is_last:
-                log_sum = m + jnp.log(l)
-                high = log_sum.astype(BF).astype(F32)
-                logs = jnp.where(lanes < 32, high, log_sum - high)
-                o_st[n, h] = jnp.where(lanes >= 64, acc / l, logs).astype(BF)
-            else:
-                state[n, h] = jnp.where(lanes >= 64, acc, jnp.where(lanes < 32, m, l))
+                    logs = jnp.where(lanes < 32, top, total)
+                    state[n, h, part_at, :] = jnp.where(lanes >= 64, weighted, logs)
             if is_last:
 
                 @pl.when(d > 0)
@@ -296,12 +343,23 @@
         else:
             loop(0, LH * YG, tile)
 
+    attend([i], True, False)
     for step, members in enumerate(PASSES):
         for n in members:
             kv_copy(n).wait_recv()
+        if step == UP_STEP:
+            for n in range(XG - 1):
+                zy_copy(n).wait()
+            for d in range(1, YG):
+                for copy in x_copy(d):
+                    copy.start()
         places = [kv_from(n) for n in members]
-        attend(places if step else [i] + places, step == 0, step == len(PASSES) - 1)
-
+        attend(places, False, step == len(PASSES) - 1)
+
+    for d in range(1, YG):
+        for copy in x_copy(d):
+            copy.wait()
+    unless_self(lambda t: (down_copy(t).wait_send(), down_arrival(t).wait_recv()))
     for n in range(XG - 1):
         kv_copy(n).wait_send()
     loop(1, YG, lambda d: q_copy(d).wait_send())
@@ -317,61 +375,21 @@
 
 
 def middle_kernel(
-    o_all, out_g, up, down, vecs, hid, cot,
-    result, gfs, d_all, ld_all, up_own, up_rb, dn_rb, dwo, vp,
-    up_g, wf, wo, wup, wdn, dup, ddn,
+    o_all, out_g, up_g, wdn, vecs, hid, cot,
+    result, gfs, d_all, ld_all, dup, ddn, dwo, vp,
+    wf, wo, wup,
     att, ld, st, own, first, n1, inv1, x_all, act, deriv, gd, gp, gb, gsec, rb, dbuf, ldrow, vg,
     ag_s, ag_r, rs_s, rs_r, d_s, d_r, l_s, l_r, loc,
-    ua_s, ua_r, ub_s, ub_r, dn_s, dn_r, us_s, us_r, ds_s, ds_r,
 ):
     s = lax.axis_index("sp")
     f = lax.axis_index("fsdp")
     i, j = f // YG, lax.rem(f, YG)
     rows = hid.shape[0]
     tall = SP * rows
-    z, x = f // 16, lax.rem(i, YG)
-    greet_all(f, s)
-
-    def zy_copy(n):
-        to = (lax.rem(z + (n + 1) // YG, 2) * YG + x) * YG + lax.rem(j + n + 1, YG)
-        return remote(up, up_g.at[f], ua_s.at[n], ua_r.at[n], fsdp=to)
-
-    def x_copy(d):
-        to = (z * YG + lax.rem(x + d, YG)) * YG + j
-        copies = []
-        for n in range(2):
-            at = up_g.at[pl.ds((n * YG + x) * YG, YG)]
-            copies.append(remote(at, at, ub_s.at[d - 1, n], ub_r.at[d - 1, n], fsdp=to))
-        return copies
-
-    def down_copy(t):
-        k = lax.rem(f, 8)
-        dst = wdn.at[pl.ds(k * 96, 96)]
-        return remote(down, dst, dn_s.at[t], dn_r.at[k], fsdp=8 * s + t, sp=f // 8)
-
-    def down_arrival(k):
-        dst = wdn.at[pl.ds(k * 96, 96)]
-        return remote(down, dst, dn_s.at[k], dn_r.at[k], fsdp=8 * s + k, sp=f // 8)
-
-    def is_self(t):
-        return (s == f // 8) & (8 * s + t == f)
-
-    def unless_self(work):
-        def step(t):
-            @pl.when(jnp.logical_not(is_self(t)))
-            def _():
-                work(t)
-
-        loop(0, 8, step)
-
-    for n in range(XG - 1):
-        zy_copy(n).start()
-    unless_self(lambda t: down_copy(t).start())
-    up_g[f] = up[...]
-
-    @pl.when(s == f // 8)
-    def _():
-        wdn[pl.ds(pl.multiple_of(lax.rem(f, 8) * 96, 32), 96), :] = down[...]
+    barrier = pltpu.get_barrier_semaphore()
+    loop(1, YG, lambda d: greet(barrier, fsdp=i * YG + lax.rem(j + d, YG)))
+    loop(1, SP, lambda d: greet(barrier, sp=lax.rem(s + d, SP)))
+    pl.semaphore_wait(barrier, YG - 1 + SP - 1)
 
     wf[0:192, :] = out_g[...].astype(F32).reshape(192, wf.shape[1])
     for h in range(LH):
@@ -438,11 +456,6 @@
             own[...] = value
 
     loop(1, SP + 1, out_part)
-    for n in range(XG - 1):
-        zy_copy(n).wait()
-    for d in range(1, YG):
-        for copy in x_copy(d):
-            copy.start()
     summed = hid[...].astype(F32) + collect(0) + vecs[2:3, :]
     value, normed, inverse = norm_forward(summed, vecs[3:4, :], vecs[4:5, :])
     first[...] = value
@@ -451,16 +464,11 @@
     x_all[span(s), :] = value.astype(BF)
     loop(1, SP, lambda d: gather(0, x_all)(d).start())
 
-    for d in range(1, YG):
-        for copy in x_copy(d):
-            copy.wait()
-
     def assemble(n):
         wf[pl.ds(pl.multiple_of(24 * n, 8), 24), :] = up_g[n].astype(F32)
 
     loop(0, FS, assemble)
     wup[...] = wf[...].astype(BF)
-    unless_self(lambda t: (down_copy(t).wait_send(), down_arrival(t).wait_recv()))
 
     def pipeline(e, buf, work):
         def step(d):
@@ -527,36 +535,6 @@
         dup[n] = wf[pl.ds(pl.multiple_of(24 * n, 8), 24), :].astype(BF)
 
     loop(0, FS, cut)
-
-    def up_sum(d):
-        to = lax.rem(x + d, YG)
-        copies = []
-        for n in range(2):
-            src = dup.at[pl.ds((n * YG + to) * YG, YG)]
-            sems = (us_s.at[d - 1, n], us_r.at[d - 1, n])
-            copies.append(remote(src, up_rb.at[d - 1, n], *sems, fsdp=(z * YG + to) * YG + j))
-        return copies
-
-    def down_sum(t):
-        k = lax.rem(f, 8)
-        src = ddn.at[pl.ds(t * 96, 96)]
-        return remote(src, dn_rb.at[k], ds_s.at[t], ds_r.at[k], fsdp=8 * s + t, sp=f // 8)
-
-    def down_sum_arrival(k):
-        src = ddn.at[pl.ds(k * 96, 96)]
-        return remote(src, dn_rb.at[k], ds_s.at[k], ds_r.at[k], fsdp=8 * s + k, sp=f // 8)
-
-    for d in range(1, YG):
-        for copy in up_sum(d):
-            copy.start()
-    unless_self(lambda t: down_sum(t).start())
-    for n in range(2):
-        up_own[n] = dup[pl.ds((n * YG + x) * YG, YG)]
-
-    @pl.when(s == f // 8)
-    def _():
-        k = lax.rem(f, 8)
-        dn_rb[k] = ddn[pl.ds(pl.multiple_of(k * 96, 32), 96), :]
 
     ub = jnp.sum(gp[...].astype(F32), axis=0, keepdims=True)
     grad_first = gsec[...] + collect(2)
@@ -622,19 +600,15 @@
     l_own.wait()
     loop(1, YG, lambda n: loop(0, SP, lambda d: d_copy(n, d).wait()))
     loop(1, YG, lambda d: l_copy(d).wait())
-    for d in range(1, YG):
-        for copy in up_sum(d):
-            copy.wait()
-    unless_self(lambda t: (down_sum(t).wait_send(), down_sum_arrival(t).wait_recv()))
 
 
 def backward_kernel(
-    valid, q_all, d_all, ld, kv_all, hid_all, wqkv, gfs, up_own, up_rb, dn_rb, dwo, vp,
+    valid, q_all, d_all, ld, kv_all, hid_all, wqkv, gfs, dup, ddn, dwo, vp,
     input_grad, wkg, wqg, upg, dng, outg, vecg,
-    acc, dq, dkv, kv_rb, q_rb, g, wf, wk, wp, st, own, rb, wk_rb, wq_rb, up_st, up_rc, ou_rb, vp_rb,
+    acc, dq, dkv, kv_rb, q_rb, g, wf, wk, wp, st, own, rb, wk_rb, wq_rb, up_rb, dn_rb, up_st, up_rc, ou_rb, vp_rb,
     up_fin, dn_fin, ou_fin, v_fin, wk_fin, wq_fin,
     kv_s, kv_r, q_s, q_r, wk_s, wk_r, wq_s, wq_r, up_s, up_r, ou_s, ou_r, vp_s, vp_r,
-    rs_s, rs_r, fin_s, fin_r,
+    rs_s, rs_r, fin_s, fin_r, us_s, us_r, ds_s, ds_r,
 ):
     s = lax.axis_index("sp")
     f = lax.axis_index("fsdp")
@@ -678,14 +652,41 @@
     def is_self(t):
         return (s == f // 8) & (8 * s + t == f)
 
-    for n in range(2):
-        for c in range(YG):
-            total = up_own[n, c].astype(F32)
-            for d in range(YG - 1):
-                total = total + up_rb[d, n, c].astype(F32)
-            up_st[n * YG + c] = total.astype(BF)
-    for n in range(XG - 1):
-        up_copy(n).start()
+    def unless_self(work):
+        def step(t):
+            @pl.when(jnp.logical_not(is_self(t)))
+            def _():
+                work(t)
+
+        loop(0, 8, step)
+
+    def up_sum(d):
+        to = lax.rem(x + d, YG)
+        copies = []
+        for n in range(2):
+            src = dup.at[pl.ds((n * YG + to) * YG, YG)]
+            sems = (us_s.at[d - 1, n], us_r.at[d - 1, n])
+            copies.append(remote(src, up_rb.at[d - 1, n], *sems, fsdp=(z * YG + to) * YG + j))
+        return copies
+
+    def down_sum(t):
+        k = lax.rem(f, 8)
+        src = ddn.at[pl.ds(t * 96, 96)]
+        return remote(src, dn_rb.at[k], ds_s.at[t], ds_r.at[k], fsdp=8 * s + t, sp=f // 8)
+
+    def down_sum_arrival(k):
+        src = ddn.at[pl.ds(k * 96, 96)]
+        return remote(src, dn_rb.at[k], ds_s.at[k], ds_r.at[k], fsdp=8 * s + k, sp=f // 8)
+
+    for d in range(1, YG):
+        for copy in up_sum(d):
+            copy.start()
+    unless_self(lambda t: down_sum(t).start())
+    @pl.when(s == f // 8)
+    def _():
+        k = lax.rem(f, 8)
+        dn_rb[k] = ddn[pl.ds(pl.multiple_of(k * 96, 32), 96), :]
+
     loop(1, FS, lambda d: vp_copy(d).start())
 
     def to_owner(k):
@@ -698,15 +699,6 @@
             ou_rb[k] = dwo[k]
 
     loop(0, 8, to_owner)
-
-    def down_rows(c):
-        at = pl.ds(pl.multiple_of(c * 32, 32), 32)
-        total = dn_rb[0, at, :].astype(F32)
-        for n in range(1, 8):
-            total = total + dn_rb[n, at, :].astype(F32)
-        dn_fin[s, at, :] = total.astype(BF)
-
-    loop(0, dn_fin.shape[1] // 32, down_rows)
 
     acc[...] = jnp.zeros(acc.shape, F32)
 
@@ -750,7 +742,19 @@
         def _():
             kv_copy(d).start()
 
-    loop(1, XG + 1, key_step)
+    loop(1, 4, key_step)
+    for d in range(1, YG):
+        for copy in up_sum(d):
+            copy.wait()
+    for n in range(2):
+        for c in range(YG):
+            total = dup[(n * YG + x) * YG + c].astype(F32)
+            for d in range(YG - 1):
+                total = total + up_rb[d, n, c].astype(F32)
+            up_st[n * YG + c] = total.astype(BF)
+    for n in range(XG - 1):
+        up_copy(n).start()
+    loop(4, XG + 1, key_step)
     for n in range(YG):
         for h in range(LH):
             dq[n, 64 * h : 64 * h + 64, :] = acc[n, h].astype(BF)
@@ -801,6 +805,17 @@
             out_arrival(t).wait_recv()
 
     loop(0, 8, owner_wait)
+    unless_self(lambda t: (down_sum(t).wait_send(), down_sum_arrival(t).wait_recv()))
+
+    def down_rows(c):
+        at = pl.ds(pl.multiple_of(c * 32, 32), 32)
+        total = dn_rb[0, at, :].astype(F32)
+        for n in range(1, 8):
+            total = total + dn_rb[n, at, :].astype(F32)
+        dn_fin[s, at, :] = total.astype(BF)
+
+    loop(0, dn_fin.shape[1] // 32, down_rows)
+
     ou_fin[s] = add_up(ou_rb, jnp.zeros(ou_fin.shape[1:], F32)).astype(BF)
 
     def sp_copy(e, buf):
@@ -948,7 +963,7 @@
     riders = lax.dynamic_update_slice(riders, up_bias.reshape(4, slim), (8, 0))
     wq = jnp.concatenate((wq, riders), axis=1)
     smem = pl.BlockSpec(memory_space=pltpu.SMEM)
-    hid_all, wqkv, q_all, kv_all, o_all, out_g, vecs = pl.pallas_call(
+    hid_all, wqkv, q_all, kv_all, o_all, out_g, up_g, wdn, vecs = pl.pallas_call(
         forward_kernel,
         out_shape=(
             shape((tall, width), BF),
@@ -957,10 +972,12 @@
             shape((XG, LH, tall, 128), BF),
             shape((YG, LH, tall, 128), BF),
             shape((8, slim, width), BF),
+            shape((FS, slim, share), BF),
+            shape((share, width), BF),
             shape((16, width), F32),
         ),
-        in_specs=[smem] + [vmem] * 3,
-        out_specs=(vmem, vmem, vmem, vmem, vmem, hbm, vmem),
+        in_specs=[smem] + [vmem] * 5,
+        out_specs=(vmem, vmem, vmem, vmem, vmem, hbm, vmem, vmem, vmem),
         scratch_shapes=[
             pltpu.VMEM((FS, slim, cols + 64), BF),
             pltpu.VMEM((width, cols), F32),
@@ -971,36 +988,32 @@
             pltpu.VMEM((YG, LH, tall, 128), BF),
         ]
         + [dma((n,)) for n in (3, 3, 31, 31, 8, 8, 3, 3, 7, 7)]
-        + [dma((3, 3)), dma((3, 3)), dma((1,))],
+        + [dma((3, 3)), dma((3, 3)), dma((1,))]
+        + [dma((7,)), dma((7,)), dma((3, 2)), dma((3, 2)), dma((8,)), dma((8,))],
         compiler_params=pltpu.CompilerParams(
             collective_id=0, has_side_effects=True, vmem_limit_bytes=VMEM_LIMIT
         ),
         name="forward",
-    )(valid_length, hidden_in, wq, output_weight)
-
-    result, gfs, d_all, ld_all, up_own, up_rb, dn_rb, dwo, vp = pl.pallas_call(
+    )(valid_length, hidden_in, wq, output_weight, up, down_weight)
+
+    result, gfs, d_all, ld_all, dup, ddn, dwo, vp = pl.pallas_call(
         middle_kernel,
         out_shape=(
             shape((rows, width), BF),
             shape((rows, width), F32),
             shape((YG, LH, tall, 128), BF),
             shape((YG, 8, tall), F32),
-            shape((2, YG, slim, share), BF),
-            shape((YG - 1, 2, YG, slim, share), BF),
-            shape((8, deep, width), BF),
+            shape((FS, slim, share), BF),
+            shape((share, width), BF),
             shape((LH * HEAD_DIM, width), BF),
             shape((FS, 16, 128), F32),
         ),
         in_specs=[vmem] * 7,
-        out_specs=(vmem, vmem, hbm, hbm, vmem, vmem, vmem, vmem, vmem),
+        out_specs=(vmem, vmem, hbm, hbm, vmem, vmem, vmem, vmem),
         scratch_shapes=[
-            pltpu.VMEM((FS, slim, share), BF),
             pltpu.VMEM((width, share), F32),
             pltpu.VMEM((LH * 128, width), BF),
             pltpu.VMEM((width, share), BF),
-            pltpu.VMEM((share, width), BF),
-            pltpu.VMEM((FS, slim, share), BF),
-            pltpu.VMEM((share, width), BF),
             pltpu.VMEM((tall, LH * 128), BF),
             pltpu.VMEM((tall, 128), F32),
             pltpu.VMEM((3, tall, width), BF),
@@ -1021,15 +1034,13 @@
             pltpu.VMEM((8, width), F32),
         ]
         + [dma((3, 3)) for _ in range(4)]
-        + [dma((3, 4)), dma((3, 4)), dma((3,)), dma((3,)), dma((2,))]
-        + [dma((7,)), dma((7,)), dma((3, 2)), dma((3, 2)), dma((8,)), dma((8,))]
-        + [dma((3, 2)), dma((3, 2)), dma((8,)), dma((8,))],
+        + [dma((3, 4)), dma((3, 4)), dma((3,)), dma((3,)), dma((2,))],
         compiler_params=pltpu.CompilerParams(
             collective_id=1, has_side_effects=True, vmem_limit_bytes=VMEM_LIMIT
         ),
         name="middle",
     )(
-        o_all, out_g, up, down_weight, vecs,
+        o_all, out_g, up_g, wdn, vecs,
         hidden_in, out_cotangent,
     )
 
@@ -1044,7 +1055,7 @@
             shape((slim, width), F32),
             shape((16, 128), F32),
         ),
-        in_specs=[smem] + [vmem] * 12,
+        in_specs=[smem] + [vmem] * 11,
         out_specs=(vmem,) * 7,
         scratch_shapes=[
             pltpu.VMEM((YG, LH, HEAD_DIM, tall), F32),
@@ -1061,6 +1072,8 @@
             pltpu.VMEM((SP - 1, rows, width), BF),
             pltpu.VMEM((FS - 1, slim, 384), BF),
             pltpu.VMEM((FS - 1, slim, 256), BF),
+            pltpu.VMEM((YG - 1, 2, YG, slim, share), BF),
+            pltpu.VMEM((8, deep, width), BF),
             pltpu.VMEM((8, slim, share), BF),
             pltpu.VMEM((XG - 1, slim, share), BF),
             pltpu.VMEM((8, slim, width), BF),
@@ -1073,14 +1086,14 @@
             pltpu.VMEM((SP, slim, 256), BF),
         ]
         + [dma((n,)) for n in (7, 7, 3, 3, 31, 31, 31, 31, 7, 7, 8, 8, 31, 31, 3, 3)]
-        + [dma((6, 3)), dma((6, 3))],
+        + [dma((6, 3)), dma((6, 3)), dma((3, 2)), dma((3, 2)), dma((8,)), dma((8,))],
         compiler_params=pltpu.CompilerParams(
             collective_id=2, has_side_effects=True, vmem_limit_bytes=VMEM_LIMIT
         ),
         name="backward",
     )(
         valid_length, q_all, d_all, ld_all, kv_all, hid_all, wqkv, gfs,
-        up_own, up_rb, dn_rb, dwo.reshape(8, slim, width), vp,
+        dup, ddn, dwo.reshape(8, slim, width), vp,
     )
 
     kv_grad = wkg.reshape(SP, slim, LH, 2, HEAD_DIM)

time: 407 us -> 368 us (0.904)
  Pallas kernels: 390 us -> 350 us
    pallas_call x1, Pallas kernels: 113 us -> 75.4 us  [on_device(): pl.pallas_call(middle_kernel, out_shape=(shape((rows, width), BF), shape(...]
    pallas_call x1, Pallas kernels: 147 us -> 142 us  [on_device(): pl.pallas_call(forward_kernel, out_shape=(shape((tall, width), BF), shape...]
where the time goes in v4:
time: 368 us; the launch traced here: 366 us
  Pallas kernels  350 us (95%)
  local copies, waits for them, and re-layouts  13.3 us (4%)
    pallas_call x1, Pallas kernels, on_device(): pl.pallas_call(forward_kernel, out_shape=(shape((tall, width), BF), shape...  142 us
    pallas_call x1, Pallas kernels, on_device(): pl.pallas_call(backward_kernel, out_shape=(shape((rows, width), F32), sha...  132 us
    pallas_call x1, Pallas kernels, on_device(): pl.pallas_call(middle_kernel, out_shape=(shape((rows, width), BF), shape(...  75.4 us

profile of v4, /device:TPU:1, one launch (start us, length us, event | category | flops | bytes accessed | tf_op | source)
XLA Modules:
  0.0 366.2 jit_solution(2181438701400896212)
XLA Ops:
  0.6 0.0 copy-start
  1.4 0.7 reshape.53
  2.1 0.8 stack.39
  2.9 0.3 dynamic_update_slice.3
  3.2 0.0 copy-done
  3.2 0.6 constant_dynamic-slice_fusion.up
  3.8 1.1 reshape.51
  5.1 0.1 reshape.52
  5.2 0.1 reshape_squeeze.3
  5.3 0.7 pad_maximum_fusion.1.wq
  6.0 142.3 %forward.1 = (bf16[512,768]{1,0:T(8,128)(2,1)}, bf16[768,576]{1,0:T(8,128)(2,1)}, bf16[4,3,512,128]{3,2,1,0:T(8,128)(2,1)}, bf16[8,3,512,128]{3,2,1,0:T(8,128)(2...) custom-call(s32[1]{0:T(128)S(6)} %copy.53.valid, ...), custom_call_target="tpu_custom_call" | custom-call | tf_op jit(solution)/shard_map/forward/pallas_call | solution.py:966
  148.3 75.4 %middle.1 = (bf16[128,768]{1,0:T(8,128)(2,1)}, f32[128,768]{1,0:T(8,128)}, bf16[4,3,512,128]{3,2,1,0:T(8,128)(2,1)}, f32[4,8,512]{2,1,0:T(8,128)}, bf16[32,24,76...) custom-call(bf16[4,3,512,128]{3,2,1,0:T(8,128)(2,1)} %get-tuple-element.39.o_all,, ...), custom_call_target="tpu_custom_call" | custom-call | tf_op jit(solution)/shard_map/middle/pallas_call | solution.py:999
  223.7 132.0 %backward.1 = (f32[128,768]{1,0:T(8,128)}, f32[4,24,384]{2,1,0:T(8,128)}, f32[4,24,256]{2,1,0:T(8,128)}, f32[24,3072]{1,0:T(8,128)}, f32[96,768]{1,0:T(8,128)}, /*index=5*/f32[24,768]{1,0:T(8,128)}, f32[16,128]{1,0:T(8,128)}) custom-call(s32[1]{0:T(128)S(6)} %copy.53.valid, bf16[4,3,512,128]{3,2,1,0:T(8,128)(2,1)} %get-tuple-element.45.q_all, ...), custom_call_target="tpu_custom_call" | custom-call | tf_op jit(solution)/shard_map/backward/pallas_call | solution.py:1047
  355.7 1.2 slice_bitcast_fusion.5
  356.9 0.8 slice_reduce_fusion
  357.7 1.4 slice_bitcast_fusion.2
  359.1 1.0 reshape.55
  360.2 0.0 copy-start.4
  360.2 1.2 reshape.56
  361.3 0.0 copy-start.1
  361.3 0.1 copy.42
  361.4 0.0 copy-start.5
  361.5 0.0 copy-start.3
  361.5 0.2 maximum_bitcast_fusion
  361.6 0.0 copy-start.2
  361.6 1.1 reshape.57
  362.7 0.0 copy-done.4
  362.7 0.7 copy.54
  363.4 0.7 copy.55
  364.1 0.6 copy.56
  364.8 0.7 copy.57
  365.5 0.7 copy.58
  (11 shorter events, 0.1 us)
Async XLA Ops:
  0.6 2.6 copy-start
  360.2 2.5 copy-start.4
  361.3 2.0 copy-start.1
  361.4 2.7 copy-start.5
  361.5 3.3 copy-start.3
  361.6 3.8 %copy-start.2 = (f32[96,768]{1,0:T(8,128)S(1)}, f32[96,768]{1,0:T(8,128)}, u32[]{:S(2)}) copy-start(f32[96,768]{1,0:T(8,128)} %get-tuple-element.102) | copy-start | bytes 884740

commit v5 on v4

--- a/solution.py
+++ b/solution.py
@@ -617,13 +617,16 @@
     tall = SP * rows
     greet_all(f, s)
 
-    def kv_copy(d):
+    def kv_copy(d, h):
         to = lax.rem(i + d, XG)
-        return remote(dkv.at[d - 1], kv_rb.at[d - 1], kv_s.at[d - 1], kv_r.at[d - 1], fsdp=to * YG + j)
-
-    def q_copy(d):
+        sems = (kv_s.at[d - 1, h], kv_r.at[d - 1, h])
+        return remote(dkv.at[d - 1, h], kv_rb.at[d - 1, h], *sems, fsdp=to * YG + j)
+
+    def q_copy(d, h):
         to = lax.rem(j + d, YG)
-        return remote(dq.at[to], q_rb.at[d - 1], q_s.at[d - 1], q_r.at[d - 1], fsdp=i * YG + to)
+        at = pl.ds(pl.multiple_of(64 * h, 64), 64)
+        sems = (q_s.at[d - 1, h], q_r.at[d - 1, h])
+        return remote(dq.at[to, at], q_rb.at[d - 1, at], *sems, fsdp=i * YG + to)
 
     def fs_copy(src, buf, send, recv):
         def copy(d):
@@ -702,63 +705,67 @@
 
     acc[...] = jnp.zeros(acc.shape, F32)
 
-    def key_step(d):
+    def key_step(d, h):
         at = lax.rem(i + d, XG)
         first_key = (at * YG + j) * tall
 
-        def head(h):
-            def work(last):
-                block = kv_all[at, h]
-                flipped = jnp.transpose(block.astype(F32), (1, 0))[0:HEAD_DIM].astype(BF)
-                total = None
-                for n in range(YG):
-                    query = q_all[n, h]
-                    grad = d_all[n, h]
-                    log_sum = ld[n, pl.ds(2 * h, 1), :]
-                    delta = ld[n, pl.ds(2 * h + 1, 1), :]
-                    scores = dot_nt(block, query)
-                    if last:
-                        place = first_key + lax.broadcasted_iota(jnp.int32, (tall, 1), 0)
-                        scores = jnp.where(place < valid[0], scores, masked)
-                    p = jnp.exp(scores - log_sum)
-                    grad_p = dot_nt(block, grad)
-                    grad_s = (p * (grad_p - delta)).astype(BF)
-                    terms = dot_nn(grad_s, query) + dot_nn(p.astype(BF), grad)
-                    total = terms if n == 0 else total + terms
-                    acc[n, h] = acc[n, h] + dot_nn(flipped, grad_s)
-                dkv[d - 1, h] = total.astype(BF)
-
-            @pl.when(at < XG - 1)
-            def _():
-                work(False)
-
-            @pl.when(at == XG - 1)
-            def _():
-                work(True)
-
-        loop(0, LH, head)
+        def work(last):
+            block = kv_all[at, h]
+            flipped = jnp.transpose(block.astype(F32), (1, 0))[0:HEAD_DIM].astype(BF)
+            total = None
+            for n in range(YG):
+                query = q_all[n, h]
+                grad = d_all[n, h]
+                log_sum = ld[n, pl.ds(2 * h, 1), :]
+                delta = ld[n, pl.ds(2 * h + 1, 1), :]
+                scores = dot_nt(block, query)
+                if last:
+                    place = first_key + lax.broadcasted_iota(jnp.int32, (tall, 1), 0)
+                    scores = jnp.where(place < valid[0], scores, masked)
+                p = jnp.exp(scores - log_sum)
+                grad_p = dot_nt(block, grad)
+                grad_s = (p * (grad_p - delta)).astype(BF)
+                terms = dot_nn(grad_s, query) + dot_nn(p.astype(BF), grad)
+                total = terms if n == 0 else total + terms
+                acc[n, h] = acc[n, h] + dot_nn(flipped, grad_s)
+            dkv[d - 1, h] = total.astype(BF)
+
+        @pl.when(at < XG - 1)
+        def _():
+            work(False)
+
+        @pl.when(at == XG - 1)
+        def _():
+            work(True)
 
         @pl.when(d < XG)
         def _():
-            kv_copy(d).start()
-
-    loop(1, 4, key_step)
-    for d in range(1, YG):
-        for copy in up_sum(d):
-            copy.wait()
-    for n in range(2):
-        for c in range(YG):
-            total = dup[(n * YG + x) * YG + c].astype(F32)
-            for d in range(YG - 1):
-                total = total + up_rb[d, n, c].astype(F32)
-            up_st[n * YG + c] = total.astype(BF)
-    for n in range(XG - 1):
-        up_copy(n).start()
-    loop(4, XG + 1, key_step)
-    for n in range(YG):
-        for h in range(LH):
-            dq[n, 64 * h : 64 * h + 64, :] = acc[n, h].astype(BF)
-    loop(1, YG, lambda d: q_copy(d).start())
+            kv_copy(d, h).start()
+
+    def second_stage():
+        for d in range(1, YG):
+            for copy in up_sum(d):
+                copy.wait()
+        for n in range(2):
+            for c in range(YG):
+                total = dup[(n * YG + x) * YG + c].astype(F32)
+                for d in range(YG - 1):
+                    total = total + up_rb[d, n, c].astype(F32)
+                up_st[n * YG + c] = total.astype(BF)
+        for n in range(XG - 1):
+            up_copy(n).start()
+
+    def head(h):
+        loop(1, XG + 1, lambda d: key_step(d, h))
+        for n in range(YG):
+            dq[n, pl.ds(pl.multiple_of(64 * h, 64), 64), :] = acc[n, h].astype(BF)
+        loop(1, YG, lambda d: q_copy(d, h).start())
+
+        @pl.when(h == 0)
+        def _():
+            second_stage()
+
+    loop(0, LH, head)
 
     def span(b):
         return pl.ds(pl.multiple_of(b * rows, rows), rows)
@@ -771,7 +778,7 @@
                 total = total + kv_rb[d, h, at, :].astype(F32)
             g[at, 128 * h : 128 * h + 128] = total.astype(BF)
 
-    loop(1, XG, lambda d: kv_copy(d).wait())
+    loop(1, XG, lambda d: loop(0, LH, lambda h: kv_copy(d, h).wait()))
     loop(0, SP, sum_keys)
 
     def key_terms(c):
@@ -829,7 +836,9 @@
     for e, buf in early_bufs:
         loop(1, SP, lambda d: sp_copy(e, buf)(d).start())
 
-    loop(1, YG, lambda d: q_copy(d).wait())
+    for h in range(LH):
+        for d in range(1, YG):
+            q_copy(d, h).wait()
     total = dq[j].astype(F32)
     for d in range(YG - 1):
         total = total + q_rb[d].astype(F32)
@@ -1085,7 +1094,8 @@
             pltpu.VMEM((SP, slim, 384), BF),
             pltpu.VMEM((SP, slim, 256), BF),
         ]
-        + [dma((n,)) for n in (7, 7, 3, 3, 31, 31, 31, 31, 7, 7, 8, 8, 31, 31, 3, 3)]
+        + [dma((7, LH)), dma((7, LH)), dma((YG - 1, LH)), dma((YG - 1, LH))]
+        + [dma((n,)) for n in (31, 31, 31, 31, 7, 7, 8, 8, 31, 31, 3, 3)]
         + [dma((6, 3)), dma((6, 3)), dma((3, 2)), dma((3, 2)), dma((8,)), dma((8,))],
         compiler_params=pltpu.CompilerParams(
             collective_id=2, has_side_effects=True, vmem_limit_bytes=VMEM_LIMIT

time: 368 us -> 365 us (level)
  Pallas kernels: 350 us -> 345 us
    pallas_call x1, Pallas kernels: 132 us -> 127 us  [on_device(): pl.pallas_call(backward_kernel, out_shape=(shape((rows, width), F32), sha...]
where the time goes in v5:
time: 365 us; the launch traced here: 361 us
  Pallas kernels  345 us (95%)
  local copies, waits for them, and re-layouts  13.3 us (4%)
    pallas_call x1, Pallas kernels, on_device(): pl.pallas_call(forward_kernel, out_shape=(shape((tall, width), BF), shape...  142 us
    pallas_call x1, Pallas kernels, on_device(): pl.pallas_call(backward_kernel, out_shape=(shape((rows, width), F32), sha...  127 us
    pallas_call x1, Pallas kernels, on_device(): pl.pallas_call(middle_kernel, out_shape=(shape((rows, width), BF), shape(...  75.4 us

profile of v5, /device:TPU:1, one launch (start us, length us, event | category | flops | bytes accessed | tf_op | source)
XLA Modules:
  0.0 361.5 jit_solution(16145807848115510600)
XLA Ops:
  0.6 0.0 copy-start
  1.4 0.7 reshape.53
  2.1 0.8 stack.39
  2.9 0.3 dynamic_update_slice.3
  3.2 0.0 copy-done
  3.2 0.6 constant_dynamic-slice_fusion.up
  3.8 1.1 reshape.51
  5.1 0.1 reshape.52
  5.2 0.1 reshape_squeeze.3
  5.3 0.7 pad_maximum_fusion.1.wq
  6.0 142.3 %forward.1 = (bf16[512,768]{1,0:T(8,128)(2,1)}, bf16[768,576]{1,0:T(8,128)(2,1)}, bf16[4,3,512,128]{3,2,1,0:T(8,128)(2,1)}, bf16[8,3,512,128]{3,2,1,0:T(8,128)(2...) custom-call(s32[1]{0:T(128)S(6)} %copy.53.valid, ...), custom_call_target="tpu_custom_call" | custom-call | tf_op jit(solution)/shard_map/forward/pallas_call | solution.py:975
  148.3 75.4 %middle.1 = (bf16[128,768]{1,0:T(8,128)(2,1)}, f32[128,768]{1,0:T(8,128)}, bf16[4,3,512,128]{3,2,1,0:T(8,128)(2,1)}, f32[4,8,512]{2,1,0:T(8,128)}, bf16[32,24,76...) custom-call(bf16[4,3,512,128]{3,2,1,0:T(8,128)(2,1)} %get-tuple-element.39.o_all,, ...), custom_call_target="tpu_custom_call" | custom-call | tf_op jit(solution)/shard_map/middle/pallas_call | solution.py:1008
  223.7 127.3 %backward.1 = (f32[128,768]{1,0:T(8,128)}, f32[4,24,384]{2,1,0:T(8,128)}, f32[4,24,256]{2,1,0:T(8,128)}, f32[24,3072]{1,0:T(8,128)}, f32[96,768]{1,0:T(8,128)}, /*index=5*/f32[24,768]{1,0:T(8,128)}, f32[16,128]{1,0:T(8,128)}) custom-call(s32[1]{0:T(128)S(6)} %copy.53.valid, bf16[4,3,512,128]{3,2,1,0:T(8,128)(2,1)} %get-tuple-element.45.q_all, ...), custom_call_target="tpu_custom_call" | custom-call | tf_op jit(solution)/shard_map/backward/pallas_call | solution.py:1056
  351.0 1.2 slice_bitcast_fusion.5
  352.2 0.8 slice_reduce_fusion
  353.0 1.4 slice_bitcast_fusion.2
  354.4 1.0 reshape.55
  355.5 0.0 copy-start.4
  355.5 1.2 reshape.56
  356.6 0.0 copy-start.1
  356.6 0.1 copy.42
  356.8 0.2 maximum_bitcast_fusion
  356.9 1.1 reshape.57
  358.0 0.0 copy-done.4
  358.0 0.7 copy.54
  358.7 0.0 copy-done.1
  358.7 0.7 copy.55
  359.4 0.6 copy.56
  360.1 0.0 copy-done.3
  360.1 0.7 copy.57
  360.8 0.0 copy-done.2
  360.8 0.7 copy.58
  (11 shorter events, 0.1 us)
Async XLA Ops:
  0.6 2.6 copy-start
  355.5 2.5 copy-start.4
  356.6 2.0 copy-start.1
  356.8 2.7 copy-start.5
  356.8 3.3 copy-start.3
  356.9 3.8 %copy-start.2 = (f32[96,768]{1,0:T(8,128)S(1)}, f32[96,768]{1,0:T(8,128)}, u32[]{:S(2)}) copy-start(f32[96,768]{1,0:T(8,128)} %get-tuple-element.102) | copy-start | bytes 884740
